TPU v7x, 512 devices: a whole 4x4x16 slice. The times are simulated.
512 devices in a mesh: expert: 64 (over z, y), tensor: 8 (over x, core).
Axes of the slice: x: 4, y: 4, z: 16, core: 2. Of those that a mesh axis runs over, the one named last changes fastest.
Arguments:
- tokens: bfloat16 [24576, 2048], P(('expert', 'tensor')), may hold values from -400 to 400
- modulation: float32 [64, 3, 2048], P('expert'), may hold values from -4 to 4
- w_router: bfloat16 [2048, 64], replicated, may hold values from -0.125 to 0.125
- gate_weight: bfloat16 [64, 2048, 2048], P('expert', None, 'tensor'), may hold values from -0.125 to 0.125
- up_weight: bfloat16 [64, 2048, 2048], P('expert', None, 'tensor'), may hold values from -0.125 to 0.125
- down_weight: bfloat16 [64, 2048, 2048], P('expert', 'tensor'), may hold values from -0.125 to 0.125
- expert_ids: int32 [24576, 2], P(('expert', 'tensor')), may hold values from 0 to 63, all different within a row; in each aligned block of 384 rows (0 to 383, 384 to 767, ...) at most 16 rows name the same one
Outputs:
- branch_out: bfloat16 [24576, 2048], P(('expert', 'tensor'))
Inputs may be any that keep to these rules, and one draw needn't show every extreme that they name: `expert_ids`: among the 384 rows of one image, no expert is named by more than 16 rows.
All inputs are finite; a program needn't handle non-finite values.
Results may differ from a plain program's by a relative error of at most 0.02.
Values may be sent and summed in bfloat16 or wider, within the bound.
No kernel may reach another device: no remote copies, remote signals or barrier semaphores. Data moves between devices by JAX's collectives and lax.ppermute only.
A program may use at most 64 MiB of HBM per device.

v0:
```python
import jax
import jax.numpy as jnp
from jax import lax
from jax.sharding import PartitionSpec as P

TOP = 2


EPS = 1e-06


def body(tokens, modulation, w_router, gate_weight, up_weight, down_weight, expert_ids):
    members = lax.axis_size("tensor")
    wide_count = lax.axis_size("expert")
    own_rows = tokens.shape[0]
    slot_rows = 2 * members * own_rows // wide_count * 4 // 3
    values = tokens.astype(jnp.float32)
    average = jnp.mean(values, axis=-1, keepdims=True)
    centred = values - average
    spread = jnp.mean(centred * centred, axis=-1, keepdims=True)
    normed = centred * lax.rsqrt(spread + EPS)
    modulated = (normed * (1.0 + modulation[0, 1][None, :]) + modulation[0, 0][None, :]).astype(
        jnp.bfloat16
    )
    gathered, choices_all = (
        lax.all_gather(modulated, "tensor", axis=0, tiled=True),
        lax.all_gather(expert_ids, "tensor", axis=0, tiled=True),
    )
    group_rows = gathered.shape[0]
    features = gathered.shape[1]
    experts = w_router.shape[1]
    logits = jnp.dot(gathered, w_router, preferred_element_type=jnp.float32)
    chance = jnp.take_along_axis(jax.nn.sigmoid(logits), choices_all, axis=1)
    combine = chance / jnp.sum(chance, axis=1, keepdims=True)
    counts = jnp.sum(
        (choices_all[:, :, None] == jnp.arange(experts, dtype=jnp.int32)[None, None, :]).astype(
            jnp.int32
        ),
        axis=1,
    )
    before = jnp.cumsum(counts, axis=0) - counts
    position = jnp.take_along_axis(before, choices_all, axis=1)
    flat_index = choices_all * slot_rows + position
    token_index = jnp.repeat(jnp.arange(group_rows, dtype=jnp.int32), TOP)
    slot_table = (
        jnp.full((experts * slot_rows,), group_rows, jnp.int32)
        .at[flat_index.reshape(-1)]
        .set(token_index)
    )
    outgoing = jnp.take(gathered, slot_table, axis=0, mode="fill", fill_value=0).reshape(
        experts, slot_rows, features
    )
    arrived = lax.all_to_all(outgoing, "expert", split_axis=0, concat_axis=0, tiled=True)
    arrived_slots = arrived.shape[1]
    flat_rows = arrived.reshape(-1, features)
    gate_part = jnp.dot(flat_rows, gate_weight[0], preferred_element_type=jnp.float32)
    up_part = jnp.dot(flat_rows, up_weight[0], preferred_element_type=jnp.float32)
    hidden = (jax.nn.silu(gate_part) * up_part).astype(jnp.bfloat16)
    partial_value = jnp.dot(hidden, down_weight[0], preferred_element_type=jnp.float32).astype(
        jnp.bfloat16
    )
    send_partial_value = partial_value.reshape(arrived.shape[0], arrived_slots, features)
    produced = lax.all_to_all(send_partial_value, "expert", split_axis=0, concat_axis=0, tiled=True)
    picked = jnp.take(produced.reshape(-1, features), flat_index.reshape(-1), axis=0).reshape(
        group_rows, TOP, features
    )
    combined = jnp.sum(combine[:, :, None] * picked.astype(jnp.float32), axis=1)
    mixture = lax.psum_scatter(
        combined.astype(jnp.bfloat16), "tensor", scatter_dimension=0, tiled=True
    ).astype(jnp.float32)
    return (modulation[0, 2][None, :] * mixture).astype(jnp.bfloat16)


def solution(mesh):
    placed = (
        P(("expert", "tensor"), None),
        P("expert", None, None),
        P(),
        P("expert", None, "tensor"),
        P("expert", None, "tensor"),
        P("expert", "tensor", None),
        P(("expert", "tensor"), None),
    )
    return jax.shard_map(
        body, mesh=mesh, in_specs=placed, out_specs=P(("expert", "tensor"), None), check_vma=False
    )
```

profile of v0, /device:TPU:1, one launch (start us, length us, event | category | flops | bytes accessed | tf_op | source)
XLA Modules:
  0.0 546.7 jit_solution(1794156661442516900)
XLA Ops:
  6.5 0.0 copy-start
  6.5 0.0 all-gather.3.cloned.1.call-start
  6.5 1.1 convert_reduce_fusion
  7.7 1.2 fusion.17
  8.9 1.3 fusion.27
  10.2 1.7 fusion.20
  11.9 0.0 all-gather.3.cloned.1.call-update
  12.0 14.8 %all-gather = s32[8,48,2]{1,2,0:T(2,128)S(1)} all-gather(s32[1,48,2]{1,2,0:T(2,128)} %bitcast.48), channel_id=1, replica_groups=mesh['expert'=64,'tensor'=8] {'tensor'}, dimensions={0}, use_global_device_ids=true | all-gather | bytes 3456 | tf_op jit(solution)/shard_map/all_gather | solution.py:27
  26.8 0.1 reshape.175
  26.9 0.1 copy.39
  27.1 0.9 reduce-window.6
  28.0 0.2 slice_reduce_fusion
  28.2 0.1 broadcast_add_fusion
  28.3 0.1 copy.43
  28.5 0.1 copy.33
  28.6 0.1 reshape.148
  28.8 5.1 gather_fusion.3
  34.0 0.2 reshape.157
  34.1 0.1 copy.40
  34.3 0.1 copy.42
  34.4 0.2 reshape.127
  34.6 0.1 reshape.164
  34.8 3.4 scatter_custom_fusion
  38.2 0.1 broadcast_in_dim.50
  38.3 11.5 %all-gather.3.cloned.1.call-done = bf16[384,2048]{1,0:T(8,128)(2,1)} async-done(((bf16[48,2048]{1,0:T(8,128)(2,1)}), bf16[384,2048]{1,0:T(8,128)(2,1)}) %all-gather.3.cloned.1.call-update) | async-done | bytes 1572880 | tf_op jit(solution)/shard_map/all_gather | solution.py:26
  49.8 10.4 %gather_fusion = bf16[1024,2048]{1,0:T(8,128)(2,1)} fusion(bf16[384,2048]{1,0:T(8,128)(2,1)} %all-gather.3.cloned.1.call-done, s32[1024]{0:T(1024)S(1)} %fusion.21), kind=kCustom, calls=%fused_computation | custom fusion | bytes 8392704 | tf_op jit(solution)/shard_map/jit(_take)/gather | solution.py:50
  60.3 2.5 broadcast_select_fusion.1
  62.8 0.0 copy-start.4
  62.8 202.4 %all_to_all.10 = bf16[64,16,2048]{2,1,0:T(8,128)(2,1)S(1)} all-to-all(bf16[64,16,2048]{2,1,0:T(8,128)(2,1)S(1)} %broadcast_select_fusion.1), channel_id=1, replica_groups=mesh['expert'=64,'tensor'=8] {'expert'}, dimensions={0} | all-to-all | bytes 8388608 | tf_op jit(solution)/shard_map/all_to_all | solution.py:53
  265.3 0.0 copy-start.2
  265.3 2.0 copy-done.2
  267.2 0.0 copy-done.4
  267.2 2.3 fusion.7
  269.5 0.0 copy-done
  269.5 9.1 %convolution_convert_fusion = bf16[1024,2048]{1,0:T(8,128)(2,1)} fusion(bf16[1024,2048]{1,0:T(8,128)(2,1)} %bitcast.43, bf16[1,256,2048]{2,1,0:T(8,128)(2,1)S(1)} %copy-done, bf16[1,2048,256]{2,1,0:T(8,128)(2,1)} %param.11, f32[1024,256]{1,0:T(8,128)} %fusion.7), kind=kOutput, calls=%fused_computation.8 | convolution fusion | flops 2151153664 | bytes 11534336 | tf_op jit(solution)/shard_map/dot_general | solution.py:59
  278.6 0.0 copy-start.1
  278.6 0.0 copy-start.5
  278.6 8.8 %all-to-all-start.1 = ((bf16[64,16,2048]{2,1,0:T(8,128)(2,1)}), bf16[64,16,2048]{2,1,0:T(8,128)(2,1)}, u32[]{:S(2)}, u32[]{:S(2)}) async-start(bf16[64,16,2048]{2,1,0:T(8,128)(2,1)} %bitcast.41), calls=%async_computation.1 | async-start | bytes 8388608 | tf_op jit(solution)/shard_map/all_to_all | solution.py:63
  287.4 0.2 reduce-scatter.2.cloned.1.call-start
  287.7 0.2 copy.41
  287.9 0.0 copy-done.1
  287.9 0.0 copy-done.5
  287.9 0.6 fusion.3
  288.5 6.3 %gather_fusion.2 = f32[768]{0:T(1024)S(1)} fusion(f32[384,64]{0,1:T(8,128)S(1)} %fusion.3, s32[768]{0:T(1024)S(1)} %reshape.148), kind=kCustom, calls=%fused_computation.2 | custom fusion | bytes 12288 | tf_op jit(solution)/shard_map/jit(take_along_axis)/gather | solution.py:33
  294.8 0.2 reshape.151
  295.0 0.1 copy.34
  295.2 0.1 copy.35
  295.3 175.8 %all-to-all-done.1 = bf16[64,16,2048]{2,1,0:T(8,128)(2,1)} async-done(((bf16[64,16,2048]{2,1,0:T(8,128)(2,1)}), bf16[64,16,2048]{2,1,0:T(8,128)(2,1)}, u32[]{:S(2)}, u32[]{:S(2)}) %all-to-all-start.1) | async-done | bytes 4194336 | tf_op jit(solution)/shard_map/all_to_all | solution.py:63
  471.1 9.8 %gather_fusion.1 = bf16[768,2048]{1,0:T(8,128)(2,1)} fusion(bf16[1024,2048]{1,0:T(8,128)(2,1)} %bitcast.14, s32[1024]{0:T(1024)S(1)} %pad_clamp_fusion), kind=kCustom, calls=%fused_computation.1 | custom fusion | bytes 6294528 | tf_op jit(solution)/shard_map/jit(_take)/gather | solution.py:64
  480.9 6.0 %gather.25 = bf16[384,2,2048]{2,1,0:T(2,128)(2,1)} reshape(bf16[768,2048]{1,0:T(8,128)(2,1)} %gather_fusion.1) | data formatting | bytes 6291456 | tf_op jit(solution)/shard_map/jit(_take)/gather | solution.py:64
  486.9 0.0 copy-start.3
  486.9 15.4 %multiply_reduce_fusion = bf16[384,2048]{1,0:T(8,128)(2,1)} fusion(bf16[384,2,2048]{2,1,0:T(2,128)(2,1)} %gather.25, pred[384,2]{1,0:T(8,128)(4,1)S(1)} %copy.41, f32[384,2]{1,0:T(8,128)S(1)} %copy.35), kind=kLoop, calls=%fused_computation.5 | loop fusion | flops 5505024 | bytes 4722432 | tf_op jit(solution)/shard_map/reduce_sum | solution.py:67
  502.4 0.0 reduce-scatter.2.cloned.1.call-update
  502.4 35.8 %reduce-scatter.2.cloned.1.call-done = bf16[48,2048]{1,0:T(8,128)(2,1)} async-done(((bf16[384,2048]{1,0:T(8,128)(2,1)}), bf16[48,2048]{1,0:T(8,128)(2,1)}) %reduce-scatter.2.cloned.1.call-update) | async-done | bytes 196624 | tf_op jit(solution)/shard_map/reduce_scatter | solution.py:68
  538.2 0.0 copy-done.3
  538.2 1.6 multiply_convert_fusion
  (16 shorter events, 0.3 us)
Async XLA Ops:
  6.5 263.0 %copy-start = (bf16[1,256,2048]{2,1,0:T(8,128)(2,1)S(1)}, bf16[1,256,2048]{2,1,0:T(8,128)(2,1)}, u32[]{:S(2)}) copy-start(bf16[1,256,2048]{2,1,0:T(8,128)(2,1)} %param.12) | copy-start | bytes 3145732
  6.5 43.3 %all-gather.3.cloned.1.call-start = ((), (), s32[]{:S(2)}) async-start(), calls=%async_computation.3 | async-start | bytes 1769472 | tf_op jit(solution)/shard_map/all_gather | solution.py:26
  62.8 204.4 %copy-start.4 = (bf16[1,2048,256]{2,1,0:T(8,128)(2,1)S(1)}, bf16[1,2048,256]{2,1,0:T(8,128)(2,1)}, u32[]{:S(2)}) copy-start(bf16[1,2048,256]{2,1,0:T(8,128)(2,1)} %param.10) | copy-start | bytes 3145732
  265.3 2.0 copy-start.2
  278.6 9.3 %copy-start.1 = (bf16[384,2048]{1,0:T(8,128)(2,1)S(1)}, bf16[384,2048]{1,0:T(8,128)(2,1)}, u32[]{:S(2)}) copy-start(bf16[384,2048]{1,0:T(8,128)(2,1)} %all-gather.3.cloned.1.call-done) | copy-start | bytes 4718596
  278.6 9.3 %copy-start.5 = (bf16[2048,64]{0,1:T(8,128)(2,1)S(1)}, bf16[2048,64]{0,1:T(8,128)(2,1)}, u32[]{:S(2)}) copy-start(bf16[2048,64]{0,1:T(8,128)(2,1)} %param.9) | copy-start | bytes 786436
  278.6 192.5 %all-to-all-start.1 = ((bf16[64,16,2048]{2,1,0:T(8,128)(2,1)}), bf16[64,16,2048]{2,1,0:T(8,128)(2,1)}, u32[]{:S(2)}, u32[]{:S(2)}) async-start(bf16[64,16,2048]{2,1,0:T(8,128)(2,1)} %bitcast.41), calls=%async_computation.1 | async-start | bytes 8388608 | tf_op jit(solution)/shard_map/all_to_all | solution.py:63
  287.4 250.8 %reduce-scatter.2.cloned.1.call-start = ((), (), s32[]{:S(2)}) async-start(), calls=%async_computation.4 | async-start | bytes 1769472 | tf_op jit(solution)/shard_map/reduce_scatter | solution.py:68
  486.9 51.2 %copy-start.3 = (f32[1,1,2048]{2,0,1:T(1,128)S(1)}, f32[1,1,2048]{2,0,1:T(1,128)}, u32[]{:S(2)}) copy-start(f32[1,1,2048]{2,0,1:T(1,128)} %get-tuple-element.7) | copy-start | bytes 24580
Sparse Core Ops, SparseCore 0:
  12.1 37.6 all-gather.2
  502.5 35.6 reduce-scatter.1
where the time goes:
time: 548 us; the launch traced here: 547 us
  waiting for transfers between devices  223 us (41%)
  blocking collectives  217 us (40%)
  local copies, waits for them, and re-layouts  45.4 us (8%)
  other arithmetic  26.3 us (5%)
  between operations  13.7 us (2%)
  matrix products  11.9 us (2%)
  starting transfers between devices  9.06 us (2%)
    all_to_all x1, blocking collectives, body(): lax.all_to_all(outgoing, 'expert', split_axis=0, concat_axis=0, tiled=True)  202 us
    all_to_all x1, waiting for transfers between devices, body(): lax.all_to_all(send_partial_value, 'expert', split_axis=0, concat_axis=0,...  176 us
    reduce_scatter x1, waiting for transfers between devices, body(): lax.psum_scatter(combined.astype(jnp.bfloat16), 'tensor', scatter_dimensi...  35.8 us
    gather x2, local copies, waits for them, and re-layouts, body(): jnp.take(produced.reshape(-1, features), flat_index.reshape(-1), axis=0)  15.8 us
    reduce_sum x1, other arithmetic, body(): combined = jnp.sum(combine[:, :, None] * picked.astype(jnp.float32), axis=1)  15.4 us
    all_gather x1, blocking collectives, body(): lax.all_gather(expert_ids, 'tensor', axis=0, tiled=True)  14.8 us
    all_gather x1, waiting for transfers between devices, body(): lax.all_gather(modulated, 'tensor', axis=0, tiled=True)  11.5 us
  transfers between devices with their start and end apart: 3, of which 3 were waited for; matrix products, arithmetic and copies ran while one was open for 3% of the time, Pallas kernels for 0%

commit v1 on v0

v1 whole, which is shorter than its diff:
```python
import functools

import jax
import jax.numpy as jnp
from jax import lax
from jax.experimental import pallas as pl
from jax.experimental.pallas import tpu as pltpu
from jax.sharding import Mesh, PartitionSpec as P

EPS = 1e-06
F32 = jnp.float32
BF16 = jnp.bfloat16
CORES = 2
SLOT = 16
PAD = 64
ROUTE = 16
VMEM_LIMIT = 48 * 1024 * 1024


def call(kernel, out_shape, flops, nbytes):
    return pl.pallas_call(
        kernel,
        out_shape=out_shape,
        compiler_params=pltpu.CompilerParams(vmem_limit_bytes=VMEM_LIMIT),
        cost_estimate=pl.CostEstimate(flops=flops, bytes_accessed=nbytes, transcendentals=0),
    )


def high_low(value):
    high = value.astype(BF16).astype(F32)
    return high, value - high


def modulate_kernel(member_ref, tokens_ref, modulation_ref, router_ref, ids_ref, packet_ref):
    rows, width = tokens_ref.shape
    lanes = packet_ref.shape[2]
    values = tokens_ref[...].astype(F32)
    average = jnp.mean(values, axis=-1, keepdims=True)
    centred = values - average
    spread = jnp.mean(centred * centred, axis=-1, keepdims=True)
    normed = centred * lax.rsqrt(spread + EPS)
    modulated = (normed * (1.0 + modulation_ref[1]) + modulation_ref[0]).astype(BF16)
    logits = lax.dot_general(
        router_ref[...], modulated, (((1,), (1,)), ((), ())), preferred_element_type=F32
    )
    chance_all = jax.nn.sigmoid(logits)
    expert = lax.broadcasted_iota(jnp.int32, logits.shape, 0)
    ids = ids_ref[...]
    chance = [
        jnp.sum(jnp.where(expert == ids[c : c + 1], chance_all, 0.0), axis=0, keepdims=True)
        for c in range(2)
    ]
    total = chance[0] + chance[1]
    first_high, first_low = high_low(chance[0] / total)
    second_high, second_low = high_low(chance[1] / total)
    named = ids.astype(F32)
    route = jnp.concatenate(
        [
            named[0:1] + 1.0,
            named[1:2] + 1.0,
            first_high,
            first_low,
            second_high,
            second_low,
            jnp.zeros((ROUTE - 6, rows), F32),
        ],
        axis=0,
    ).astype(BF16)
    token = lax.broadcasted_iota(jnp.int32, (rows, lanes), 0)
    lane = lax.broadcasted_iota(jnp.int32, (rows, lanes), 1)
    place = jnp.where(lane == token + member_ref[0] * PAD, 1.0, 0.0).astype(BF16)
    placed = jnp.dot(route, place, preferred_element_type=F32).astype(BF16)
    for member in range(packet_ref.shape[0]):
        quarter = member // CORES
        packet_ref[member, 0:rows, :] = modulated[:, quarter * lanes : (quarter + 1) * lanes]
        packet_ref[member, rows:PAD, :] = placed


def fill_kernel(core_ref, packet_ref, slots_ref, route_ref):
    members, _, lanes = packet_ref.shape
    count = slots_ref.shape[0]
    half = SLOT // CORES
    experts = count // half
    tokens = PAD - ROUTE
    route = packet_ref[0, tokens:PAD, :].astype(F32)
    for member in range(1, members):
        route = route + packet_ref[member, tokens:PAD, :].astype(F32)
    everything = packet_ref.shape[0] * PAD
    named = [route[c : c + 1].astype(jnp.int32) - 1 for c in range(2)]
    expert = lax.broadcasted_iota(jnp.int32, (experts, everything), 0)
    names = [expert == named[c] for c in range(2)]
    either = jnp.where(names[0] | names[1], 1.0, 0.0).astype(BF16)
    earlier = lax.broadcasted_iota(jnp.int32, (everything, everything), 0) < (
        lax.broadcasted_iota(jnp.int32, (everything, everything), 1)
    )
    before = jnp.dot(
        either, jnp.where(earlier, 1.0, 0.0).astype(BF16), preferred_element_type=F32
    )
    place = []
    for c in range(2):
        position = jnp.sum(jnp.where(names[c], before, 0.0), axis=0, keepdims=True)
        position = position.astype(jnp.int32) - core_ref[0] * half
        here = (position >= 0) & (position < half) & (named[c] >= 0)
        place.append(jnp.where(here, named[c] * half + position, -1))
    slot = lax.broadcasted_iota(jnp.int32, (count, everything), 0)
    pick = jnp.where((slot == place[0]) | (slot == place[1]), 1.0, 0.0).astype(BF16)
    rows = packet_ref[...].reshape(everything, lanes)
    slots_ref[...] = jnp.dot(pick, rows, preferred_element_type=F32).astype(BF16)
    route_ref[...] = jnp.concatenate(
        [place[0].astype(F32), place[1].astype(F32), route[2:6], jnp.zeros((2, everything), F32)],
        axis=0,
    )


def expert_kernel(
    quarter_ref, a_ref, b_ref, c_ref, d_ref, g0, u0, w0, g1, u1, w1, out_ref
):
    width = a_ref.shape[1]
    blocks = out_ref.shape[0]
    hidden = []
    for gate_ref, up_ref in ((g0, u0), (g1, u1)):
        gate = up = None
        for step, ref in enumerate((a_ref, b_ref, c_ref, d_ref)):
            start = pl.multiple_of(lax.rem(quarter_ref[0] + step, blocks) * width, width)
            gate_term = jnp.dot(ref[...], gate_ref[pl.ds(start, width), :], preferred_element_type=F32)
            up_term = jnp.dot(ref[...], up_ref[pl.ds(start, width), :], preferred_element_type=F32)
            gate = gate_term if gate is None else gate + gate_term
            up = up_term if up is None else up + up_term
        hidden.append((gate * jax.nn.sigmoid(gate) * up).astype(BF16))
    for block in range(blocks):
        cols = slice(block * width, (block + 1) * width)
        out_ref[block] = (
            jnp.dot(hidden[0], w0[:, cols], preferred_element_type=F32)
            + jnp.dot(hidden[1], w1[:, cols], preferred_element_type=F32)
        ).astype(BF16)


def sum_kernel(parts_ref, out_ref):
    total = parts_ref[0].astype(F32)
    for part in range(1, parts_ref.shape[0]):
        total = total + parts_ref[part].astype(F32)
    out_ref[...] = total.astype(BF16)


def combine_kernel(slots_ref, route_ref, out_ref):
    count = slots_ref.shape[0]
    everything = route_ref.shape[1]
    slot = lax.broadcasted_iota(jnp.int32, (count, everything), 0)
    first = slot == route_ref[0:1].astype(jnp.int32)
    second = slot == route_ref[1:2].astype(jnp.int32)
    high = jnp.where(first, route_ref[2:3], 0.0) + jnp.where(second, route_ref[4:5], 0.0)
    low = jnp.where(first, route_ref[3:4], 0.0) + jnp.where(second, route_ref[5:6], 0.0)
    rows = slots_ref[...]
    dims = (((0,), (0,)), ((), ()))
    mixed = lax.dot_general(high.astype(BF16), rows, dims, preferred_element_type=F32)
    mixed = mixed + lax.dot_general(low.astype(BF16), rows, dims, preferred_element_type=F32)
    mixed = mixed.astype(BF16)
    tokens = out_ref.shape[1]
    for member in range(out_ref.shape[0]):
        out_ref[member] = mixed[member * PAD : member * PAD + tokens, :]


def gate_kernel(parts_ref, modulation_ref, out_ref):
    lanes = parts_ref.shape[2]
    for quarter in range(parts_ref.shape[0] // CORES):
        total = parts_ref[CORES * quarter].astype(F32)
        for core in range(1, CORES):
            total = total + parts_ref[CORES * quarter + core].astype(F32)
        cols = slice(quarter * lanes, (quarter + 1) * lanes)
        out_ref[:, cols] = (modulation_ref[2][:, cols] * total).astype(BF16)


def body(tokens, modulation, w_router, gate_weight, up_weight, down_weight, expert_ids):
    chips = lax.axis_size("x")
    members = chips * CORES
    own, width = tokens.shape
    lanes = width // chips
    experts = w_router.shape[1]
    images = lax.axis_size("expert")
    half = SLOT // CORES
    count = experts * half
    x = lax.axis_index("x")
    core = lax.axis_index("c")
    tensor = ("x", "c")
    modulation = jnp.transpose(modulation, (1, 0, 2))
    swap = [(0, 1), (1, 0)]
    weights = [gate_weight[0], up_weight[0], down_weight[0]]
    others = [lax.ppermute(w, "c", swap) for w in weights]

    packet = call(
        modulate_kernel,
        jax.ShapeDtypeStruct((members, PAD, lanes), BF16),
        2 * own * width * experts,
        4 * own * width,
    )(
        (x * CORES + core).astype(jnp.int32).reshape(1),
        tokens,
        modulation,
        w_router.T,
        expert_ids.T,
    )
    packet = lax.all_to_all(packet, tensor, 0, 0, tiled=True)
    slots, route = call(
        fill_kernel,
        (
            jax.ShapeDtypeStruct((count, lanes), BF16),
            jax.ShapeDtypeStruct((8, members * PAD), F32),
        ),
        2 * count * members * PAD * lanes,
        4 * count * lanes,
    )(core.astype(jnp.int32).reshape(1), packet)
    arrived = lax.all_to_all(
        slots.reshape(experts, half, lanes), "expert", 0, 0, tiled=True
    ).reshape(count, lanes)

    blocks = [arrived] + [
        lax.ppermute(arrived, "x", [(i, (i - step) % chips) for i in range(chips)])
        for step in range(1, chips)
    ]
    partial = call(
        expert_kernel,
        jax.ShapeDtypeStruct((chips, count, lanes), BF16),
        6 * count * width * gate_weight.shape[2] * CORES,
        12 * width * gate_weight.shape[2],
    )(x.astype(jnp.int32).reshape(1), *blocks, *weights, *others)
    partial = lax.all_to_all(partial, "x", 0, 0, tiled=True)
    summed = call(
        sum_kernel, jax.ShapeDtypeStruct((count, lanes), BF16), count * width, 2 * count * width
    )(partial)
    produced = lax.all_to_all(
        summed.reshape(images, half, lanes), "expert", 0, 0, tiled=True
    ).reshape(count, lanes)
    mixed = call(
        combine_kernel,
        jax.ShapeDtypeStruct((members, own, lanes), BF16),
        4 * count * members * PAD * lanes,
        4 * count * lanes,
    )(produced, route)
    mixed = lax.all_to_all(mixed, tensor, 0, 0, tiled=True)
    return call(
        gate_kernel, jax.ShapeDtypeStruct((own, width), BF16), own * width, 4 * own * width
    )(mixed, modulation)


def solution(mesh):
    images, members = mesh.devices.shape
    fine = Mesh(mesh.devices.reshape(images, members // CORES, CORES), ("expert", "x", "c"))
    tensor = ("x", "c")
    rows = P(("expert", "x", "c"), None)
    placed = (
        rows,
        P("expert", None, None),
        P(),
        P("expert", None, tensor),
        P("expert", None, tensor),
        P("expert", tensor, None),
        rows,
    )
    return jax.shard_map(body, mesh=fine, in_specs=placed, out_specs=rows, check_vma=False)
```

time: 548 us -> 191 us (0.35)
  waiting for transfers between devices: 223 us -> 41.3 us
  blocking collectives: 217 us -> 102 us
  local copies, waits for them, and re-layouts: 45.4 us -> 4.53 us
  other arithmetic: 26.3 us -> 0 us
  starting transfers between devices: 9.06 us -> 31.6 us
  between operations: 13.7 us -> 0.13 us
  matrix products: 11.9 us -> 0 us
  Pallas kernels: 0 us -> 10.6 us
    all_to_all x1, waiting for transfers between devices: 176 us -> 21.6 us  [body(): lax.all_to_all(slots.reshape(experts, half, lanes), 'expert', 0, 0, tiled...]
    all_to_all x1 -> x4, blocking collectives: 202 us -> 102 us  [the longest x1 38.9 us: body(): lax.all_to_all(summed.reshape(images, half, lanes), 'expert', 0, 0, tiled...]
    gather x11 -> x0, local copies, waits for them, and re-layouts: 38.6 us -> none  [the longest x2 15.8 us: body(): jnp.take(produced.reshape(-1, features), flat_index.reshape(-1), axis=0)]
    reduce_scatter x1 -> x0, waiting for transfers between devices: 35.8 us -> none  [body(): lax.psum_scatter(combined.astype(jnp.bfloat16), 'tensor', scatter_dimensi...]
    ppermute x0 -> x6, waiting for transfers between devices: none -> 19.7 us  [the longest x3 19.7 us: body(): lax.ppermute(arrived, 'x', [(i, (i - step) % chips) for i in range(chips)])]
    reduce_sum x5 -> x0, other arithmetic: 17.8 us -> none  [the longest x1 15.4 us: body(): combined = jnp.sum(combine[:, :, None] * picked.astype(jnp.float32), axis=1)]
    ppermute x0 -> x6, starting transfers between devices: none -> 16.8 us  [the longest x3 9.23 us: body(): lax.ppermute(arrived, 'x', [(i, (i - step) % chips) for i in range(chips)])]
    all_gather x1 -> x0, blocking collectives: 14.8 us -> none  [body(): lax.all_gather(expert_ids, 'tensor', axis=0, tiled=True)]
  transfers between devices with their start and end apart: 3 -> 7, of which waited for: 3 -> 4; matrix products, arithmetic and copies ran while one was open for 3% -> 0% of each run, Pallas kernels for 0% -> 0%
where the time goes in v1:
time: 191 us; the launch traced here: 190 us
  blocking collectives  102 us (53%)
  waiting for transfers between devices  41.3 us (22%)
  starting transfers between devices  31.6 us (17%)
  Pallas kernels  10.6 us (6%)
  local copies, waits for them, and re-layouts  4.53 us (2%)
    all_to_all x1, blocking collectives, body(): lax.all_to_all(summed.reshape(images, half, lanes), 'expert', 0, 0, tiled...  38.9 us
    all_to_all x1, blocking collectives, body(): partial = lax.all_to_all(partial, 'x', 0, 0, tiled=True)  29.3 us
    all_to_all x1, waiting for transfers between devices, body(): lax.all_to_all(slots.reshape(experts, half, lanes), 'expert', 0, 0, tiled...  21.6 us
    ppermute x3, waiting for transfers between devices, body(): lax.ppermute(arrived, 'x', [(i, (i - step) % chips) for i in range(chips)])  19.7 us
    all_to_all x1, blocking collectives, body(): packet = lax.all_to_all(packet, tensor, 0, 0, tiled=True)  18.6 us
    all_to_all x1, blocking collectives, body(): mixed = lax.all_to_all(mixed, tensor, 0, 0, tiled=True)  15.3 us
    all_to_all x1, starting transfers between devices, body(): lax.all_to_all(slots.reshape(experts, half, lanes), 'expert', 0, 0, tiled...  14.8 us
    ppermute x3, starting transfers between devices, body(): lax.ppermute(arrived, 'x', [(i, (i - step) % chips) for i in range(chips)])  9.23 us
  transfers between devices with their start and end apart: 7, of which 4 were waited for; matrix products, arithmetic and copies ran while one was open for 0% of the time, Pallas kernels for 0%

profile of v1, /device:TPU:1, one launch (start us, length us, event | category | flops | bytes accessed | tf_op | source)
XLA Modules:
  0.0 190.4 jit_solution(1313233094580516867)
XLA Ops:
  0.0 0.0 copy-start
  0.0 0.9 copy-done
  1.0 0.0 copy-start.1
  1.0 0.9 copy-done.1
  1.9 0.0 copy-start.2
  1.9 0.7 copy-done.2
  2.6 0.0 copy-start.4
  2.6 0.7 copy-done.4
  3.3 0.0 copy-start.5
  3.3 0.0 copy-start.6
  3.3 0.6 shard_map.73
  3.9 18.6 %all_to_all.25.packet_ref = bf16[8,64,512]{2,1,0:T(8,128)(2,1)S(1)} all-to-all(bf16[8,64,512]{2,1,0:T(8,128)(2,1)S(1)} %shard_map.73), channel_id=1, replica_groups=mesh['expert'=64,'x'=4,'c'=2] {'x','c'}, dimensions={0} | all-to-all | bytes 1048576 | tf_op jit(solution)/shard_map/all_to_all | solution.py:202
  22.6 1.4 shard_map.74
  24.0 14.8 %all-to-all-start.1 = ((bf16[64,8,512]{2,1,0:T(8,128)(2,1)}), bf16[64,8,512]{2,1,0:T(8,128)(2,1)S(1)}, u32[]{:S(2)}, u32[]{:S(2)}) async-start(bf16[64,8,512]{2,1,0:T(8,128)(2,1)} %bitcast.6), calls=%async_computation.1 | async-start | bytes 1048576 | tf_op jit(solution)/shard_map/all_to_all | solution.py:212
  38.8 0.0 copy-done.5
  38.8 3.2 %collective-permute-start.3 = (bf16[2048,256]{1,0:T(8,128)(2,1)S(1)}, bf16[2048,256]{1,0:T(8,128)(2,1)}, u32[]{:S(2)}, u32[]{:S(2)}) collective-permute-start(bf16[2048,256]{1,0:T(8,128)(2,1)S(1)} %bitcast.23), channel_id=1, source_target_pairs={{0,1},{1,0},{2,3},{3,2},{4,5},{5,4},{6,7},{7,6},{8,9},{9,8},{10,11... | collective-permute-start | bytes 3145736 | tf_op jit(solution)/shard_map/ppermute | solution.py:188
  42.0 0.0 copy-done.6
  42.0 1.9 %collective-permute-start.4 = (bf16[2048,256]{1,0:T(8,128)(2,1)S(1)}, bf16[2048,256]{1,0:T(8,128)(2,1)}, u32[]{:S(2)}, u32[]{:S(2)}) collective-permute-start(bf16[2048,256]{1,0:T(8,128)(2,1)S(1)} %bitcast.25), channel_id=1, source_target_pairs={{0,1},{1,0},{2,3},{3,2},{4,5},{5,4},{6,7},{7,6},{8,9},{9,8},{10,11... | collective-permute-start | bytes 3145736 | tf_op jit(solution)/shard_map/ppermute | solution.py:188
  44.0 2.4 %collective-permute-start.5 = (bf16[256,2048]{1,0:T(8,128)(2,1)}, bf16[256,2048]{1,0:T(8,128)(2,1)}, u32[]{:S(2)}, u32[]{:S(2)}) collective-permute-start(bf16[256,2048]{1,0:T(8,128)(2,1)} %bitcast.27), channel_id=1, source_target_pairs={{0,1},{1,0},{2,3},{3,2},{4,5},{5,4},{6,7},{7,6},{8,9},{9,8},{10,11... | collective-permute-start | bytes 3145736 | tf_op jit(solution)/shard_map/ppermute | solution.py:188
  46.4 21.6 %all-to-all-done.1 = bf16[64,8,512]{2,1,0:T(8,128)(2,1)S(1)} async-done(((bf16[64,8,512]{2,1,0:T(8,128)(2,1)}), bf16[64,8,512]{2,1,0:T(8,128)(2,1)S(1)}, u32[]{:S(2)}, u32[]{:S(2)}) %all-to-all-start.1) | async-done | bytes 524320 | tf_op jit(solution)/shard_map/all_to_all | solution.py:212
  67.9 2.2 %collective-permute-start.2 = (bf16[512,512]{1,0:T(8,128)(2,1)S(1)}, bf16[512,512]{1,0:T(8,128)(2,1)S(1)}, u32[]{:S(2)}, u32[]{:S(2)}) collective-permute-start(bf16[512,512]{1,0:T(8,128)(2,1)S(1)} %bitcast.14), channel_id=1, source_target_pairs={{0,2},{2,4},{4,6},{6,0},{1,3},{3,5},{5,7},{7,1},{8,10},{10,12},{12... | collective-permute-start | bytes 1572872 | tf_op jit(solution)/shard_map/ppermute | solution.py:217
  70.1 3.7 %collective-permute-start.1 = (bf16[512,512]{1,0:T(8,128)(2,1)S(1)}, bf16[512,512]{1,0:T(8,128)(2,1)S(1)}, u32[]{:S(2)}, u32[]{:S(2)}) collective-permute-start(bf16[512,512]{1,0:T(8,128)(2,1)S(1)} %bitcast.15), channel_id=1, source_target_pairs={{0,4},{2,6},{4,0},{6,2},{1,5},{3,7},{5,1},{7,3},{8,12},{10,14},{12... | collective-permute-start | bytes 1572872 | tf_op jit(solution)/shard_map/ppermute | solution.py:217
  73.8 0.0 collective-permute-done.3.g1
  73.8 3.4 %collective-permute-start = (bf16[512,512]{1,0:T(8,128)(2,1)S(1)}, bf16[512,512]{1,0:T(8,128)(2,1)S(1)}, u32[]{:S(2)}, u32[]{:S(2)}) collective-permute-start(bf16[512,512]{1,0:T(8,128)(2,1)S(1)} %bitcast.16), channel_id=1, source_target_pairs={{0,6},{2,0},{4,2},{6,4},{1,7},{3,1},{5,3},{7,5},{8,14},{10,8},{12,... | collective-permute-start | bytes 1572872 | tf_op jit(solution)/shard_map/ppermute | solution.py:217
  77.2 0.0 collective-permute-done.4.u1
  77.2 0.0 collective-permute-done.5.w1
  77.2 3.2 %collective-permute-done.2.d_ref = bf16[512,512]{1,0:T(8,128)(2,1)S(1)} collective-permute-done((bf16[512,512]{1,0:T(8,128)(2,1)S(1)}, bf16[512,512]{1,0:T(8,128)(2,1)S(1)}, u32[]{:S(2)}, u32[]{:S(2)}) %collective-permute-start.2) | collective-permute-done | bytes 524320 | tf_op jit(solution)/shard_map/ppermute | solution.py:217
  80.4 10.0 %collective-permute-done.1.c_ref = bf16[512,512]{1,0:T(8,128)(2,1)S(1)} collective-permute-done((bf16[512,512]{1,0:T(8,128)(2,1)S(1)}, bf16[512,512]{1,0:T(8,128)(2,1)S(1)}, u32[]{:S(2)}, u32[]{:S(2)}) %collective-permute-start.1) | collective-permute-done | bytes 524320 | tf_op jit(solution)/shard_map/ppermute | solution.py:217
  90.4 6.5 %collective-permute-done.b_ref = bf16[512,512]{1,0:T(8,128)(2,1)S(1)} collective-permute-done((bf16[512,512]{1,0:T(8,128)(2,1)S(1)}, bf16[512,512]{1,0:T(8,128)(2,1)S(1)}, u32[]{:S(2)}, u32[]{:S(2)}) %collective-permute-start) | collective-permute-done | bytes 524320 | tf_op jit(solution)/shard_map/ppermute | solution.py:217
  96.9 0.0 copy-start.7
  96.9 1.2 copy-done.7
  98.1 6.7 %shard_map.75 = bf16[4,512,512]{2,1,0:T(8,128)(2,1)} custom-call(s32[1]{0:T(128)} %bitcast.quarter_ref, bf16[512,512]{1,0:T(8,128)(2,1)S(1)} %bitcast.17, bf16[512,512]{1,0:T(8,128)(2,1)S(1)} %collective-permute-done.b_ref, bf16[512,512]{1,0:T(8,128)(2,1)S(1)} %collective-permute-done.1.c_ref, bf16[512,512]{1,0:T(8,128)(2,1)S(1)} %collective-permute-done.2.d_ref, ...), custom_call_target="tpu_custom_call" | custom-call | flops 3221225472 | bytes 6291456 | tf_op jit(solution)/shard_map/pallas_call | solution.py:220
  104.8 29.3 %all_to_all.26.parts_ref = bf16[4,512,512]{2,1,0:T(8,128)(2,1)S(1)} all-to-all(bf16[4,512,512]{2,1,0:T(8,128)(2,1)} %shard_map.75), channel_id=1, replica_groups=mesh['expert'=64,'x'=4,'c'=2] {'x'}, dimensions={0} | all-to-all | bytes 4194304 | tf_op jit(solution)/shard_map/all_to_all | solution.py:226
  134.1 0.3 shard_map.76
  134.4 0.0 copy-start.3
  134.4 38.9 %all_to_all.27 = bf16[64,8,512]{2,1,0:T(8,128)(2,1)S(1)} all-to-all(bf16[64,8,512]{2,1,0:T(8,128)(2,1)S(1)} %bitcast.13), channel_id=1, replica_groups=mesh['expert'=64,'x'=4,'c'=2] {'expert'}, dimensions={0} | all-to-all | bytes 1048576 | tf_op jit(solution)/shard_map/all_to_all | solution.py:230
  173.4 0.9 shard_map.77
  174.3 15.3 %all_to_all.28.parts_ref = bf16[8,48,512]{2,1,0:T(8,128)(2,1)S(1)} all-to-all(bf16[8,48,512]{2,1,0:T(8,128)(2,1)S(1)} %shard_map.77), channel_id=1, replica_groups=mesh['expert'=64,'x'=4,'c'=2] {'x','c'}, dimensions={0} | all-to-all | bytes 786432 | tf_op jit(solution)/shard_map/all_to_all | solution.py:239
  189.6 0.0 copy-done.3
  189.6 0.7 shard_map.78
Async XLA Ops:
  0.0 0.9 copy-start
  1.0 0.9 copy-start.1
  1.9 0.7 copy-start.2
  2.6 0.7 copy-start.4
  3.3 35.5 %copy-start.5 = (bf16[1,2048,256]{2,1,0:T(8,128)(2,1)S(1)}, bf16[1,2048,256]{2,1,0:T(8,128)(2,1)}, u32[]{:S(2)}) copy-start(bf16[1,2048,256]{2,1,0:T(8,128)(2,1)} %param.10) | copy-start | bytes 3145732
  3.3 38.7 %copy-start.6 = (bf16[1,2048,256]{2,1,0:T(8,128)(2,1)S(1)}, bf16[1,2048,256]{2,1,0:T(8,128)(2,1)}, u32[]{:S(2)}) copy-start(bf16[1,2048,256]{2,1,0:T(8,128)(2,1)} %param.11) | copy-start | bytes 3145732
  24.0 43.9 %all-to-all-start.1 = ((bf16[64,8,512]{2,1,0:T(8,128)(2,1)}), bf16[64,8,512]{2,1,0:T(8,128)(2,1)S(1)}, u32[]{:S(2)}, u32[]{:S(2)}) async-start(bf16[64,8,512]{2,1,0:T(8,128)(2,1)} %bitcast.6), calls=%async_computation.1 | async-start | bytes 1048576 | tf_op jit(solution)/shard_map/all_to_all | solution.py:212
  38.8 35.0 %collective-permute-start.3 = (bf16[2048,256]{1,0:T(8,128)(2,1)S(1)}, bf16[2048,256]{1,0:T(8,128)(2,1)}, u32[]{:S(2)}, u32[]{:S(2)}) collective-permute-start(bf16[2048,256]{1,0:T(8,128)(2,1)S(1)} %bitcast.23), channel_id=1, source_target_pairs={{0,1},{1,0},{2,3},{3,2},{4,5},{5,4},{6,7},{7,6},{8,9},{9,8},{10,11... | collective-permute-start | bytes 3145736 | tf_op jit(solution)/shard_map/ppermute | solution.py:188
  42.0 35.2 %collective-permute-start.4 = (bf16[2048,256]{1,0:T(8,128)(2,1)S(1)}, bf16[2048,256]{1,0:T(8,128)(2,1)}, u32[]{:S(2)}, u32[]{:S(2)}) collective-permute-start(bf16[2048,256]{1,0:T(8,128)(2,1)S(1)} %bitcast.25), channel_id=1, source_target_pairs={{0,1},{1,0},{2,3},{3,2},{4,5},{5,4},{6,7},{7,6},{8,9},{9,8},{10,11... | collective-permute-start | bytes 3145736 | tf_op jit(solution)/shard_map/ppermute | solution.py:188
  44.0 33.2 %collective-permute-start.5 = (bf16[256,2048]{1,0:T(8,128)(2,1)}, bf16[256,2048]{1,0:T(8,128)(2,1)}, u32[]{:S(2)}, u32[]{:S(2)}) collective-permute-start(bf16[256,2048]{1,0:T(8,128)(2,1)} %bitcast.27), channel_id=1, source_target_pairs={{0,1},{1,0},{2,3},{3,2},{4,5},{5,4},{6,7},{7,6},{8,9},{9,8},{10,11... | collective-permute-start | bytes 3145736 | tf_op jit(solution)/shard_map/ppermute | solution.py:188
  67.9 12.5 %collective-permute-start.2 = (bf16[512,512]{1,0:T(8,128)(2,1)S(1)}, bf16[512,512]{1,0:T(8,128)(2,1)S(1)}, u32[]{:S(2)}, u32[]{:S(2)}) collective-permute-start(bf16[512,512]{1,0:T(8,128)(2,1)S(1)} %bitcast.14), channel_id=1, source_target_pairs={{0,2},{2,4},{4,6},{6,0},{1,3},{3,5},{5,7},{7,1},{8,10},{10,12},{12... | collective-permute-start | bytes 1572872 | tf_op jit(solution)/shard_map/ppermute | solution.py:217
  70.1 20.3 %collective-permute-start.1 = (bf16[512,512]{1,0:T(8,128)(2,1)S(1)}, bf16[512,512]{1,0:T(8,128)(2,1)S(1)}, u32[]{:S(2)}, u32[]{:S(2)}) collective-permute-start(bf16[512,512]{1,0:T(8,128)(2,1)S(1)} %bitcast.15), channel_id=1, source_target_pairs={{0,4},{2,6},{4,0},{6,2},{1,5},{3,7},{5,1},{7,3},{8,12},{10,14},{12... | collective-permute-start | bytes 1572872 | tf_op jit(solution)/shard_map/ppermute | solution.py:217
  73.8 23.1 %collective-permute-start = (bf16[512,512]{1,0:T(8,128)(2,1)S(1)}, bf16[512,512]{1,0:T(8,128)(2,1)S(1)}, u32[]{:S(2)}, u32[]{:S(2)}) collective-permute-start(bf16[512,512]{1,0:T(8,128)(2,1)S(1)} %bitcast.16), channel_id=1, source_target_pairs={{0,6},{2,0},{4,2},{6,4},{1,7},{3,1},{5,3},{7,5},{8,14},{10,8},{12,... | collective-permute-start | bytes 1572872 | tf_op jit(solution)/shard_map/ppermute | solution.py:217
  96.9 1.2 copy-start.7
  134.4 55.2 %copy-start.3 = (f32[1,3,2048]{2,0,1:T(1,128)S(1)}, f32[1,3,2048]{2,0,1:T(1,128)}, u32[]{:S(2)}) copy-start(f32[1,3,2048]{2,0,1:T(1,128)} %param.8) | copy-start | bytes 73732

commit v2 on v1

--- a/solution.py
+++ b/solution.py
@@ -14,7 +14,7 @@
 SLOT = 16
 PAD = 64
 ROUTE = 16
-VMEM_LIMIT = 48 * 1024 * 1024
+VMEM_LIMIT = 12 * 1024 * 1024
 
 
 def call(kernel, out_shape, flops, nbytes):
@@ -112,34 +112,71 @@
     )
 
 
-def expert_kernel(
-    quarter_ref, a_ref, b_ref, c_ref, d_ref, g0, u0, w0, g1, u1, w1, out_ref
+def cut(quarter_ref, step, blocks, width):
+    return pl.ds(pl.multiple_of(lax.rem(quarter_ref[0] + step, blocks) * width, width), width)
+
+
+def near_kernel(quarter_ref, a_ref, l_ref, r_ref, g0, u0, g1, u1, out_ref):
+    width = a_ref.shape[1]
+    blocks = g0.shape[0] // width
+    for index, weight_ref in enumerate((g0, u0, g1, u1)):
+        total = None
+        for step, ref in ((0, a_ref), (1, r_ref), (blocks - 1, l_ref)):
+            rows = weight_ref[cut(quarter_ref, step, blocks, width), :]
+            term = jnp.dot(ref[...], rows, preferred_element_type=F32)
+            total = term if total is None else total + term
+        out_ref[index] = total
+
+
+def far_kernel(
+    quarter_ref, near_ref, top_ref, bottom_ref, g0, u0, g1, u1, w0, w1, hidden_ref, out_ref
 ):
-    width = a_ref.shape[1]
-    blocks = out_ref.shape[0]
-    hidden = []
-    for gate_ref, up_ref in ((g0, u0), (g1, u1)):
-        gate = up = None
-        for step, ref in enumerate((a_ref, b_ref, c_ref, d_ref)):
-            start = pl.multiple_of(lax.rem(quarter_ref[0] + step, blocks) * width, width)
-            gate_term = jnp.dot(ref[...], gate_ref[pl.ds(start, width), :], preferred_element_type=F32)
-            up_term = jnp.dot(ref[...], up_ref[pl.ds(start, width), :], preferred_element_type=F32)
-            gate = gate_term if gate is None else gate + gate_term
-            up = up_term if up is None else up + up_term
-        hidden.append((gate * jax.nn.sigmoid(gate) * up).astype(BF16))
-    for block in range(blocks):
-        cols = slice(block * width, (block + 1) * width)
-        out_ref[block] = (
-            jnp.dot(hidden[0], w0[:, cols], preferred_element_type=F32)
-            + jnp.dot(hidden[1], w1[:, cols], preferred_element_type=F32)
-        ).astype(BF16)
-
-
-def sum_kernel(parts_ref, out_ref):
-    total = parts_ref[0].astype(F32)
-    for part in range(1, parts_ref.shape[0]):
-        total = total + parts_ref[part].astype(F32)
-    out_ref[...] = total.astype(BF16)
+    rows, width = top_ref.shape
+    blocks = g0.shape[0] // width
+    where = cut(quarter_ref, blocks // 2, blocks, width)
+    for part, ref in enumerate((top_ref, bottom_ref)):
+        span = slice(part * rows, (part + 1) * rows)
+        total = [
+            near_ref[index, span, :]
+            + jnp.dot(ref[...], weight_ref[where, :], preferred_element_type=F32)
+            for index, weight_ref in enumerate((g0, u0, g1, u1))
+        ]
+        far = None
+        for core, down_ref in enumerate((w0, w1)):
+            gate, up = total[2 * core], total[2 * core + 1]
+            hidden = (gate * jax.nn.sigmoid(gate) * up).astype(BF16)
+            hidden_ref[core, span, :] = hidden
+            term = jnp.dot(hidden, down_ref[:, where], preferred_element_type=F32)
+            far = term if far is None else far + term
+        out_ref[part] = far.astype(BF16)
+
+
+def down(hidden_ref, w0, w1, where):
+    return jnp.dot(hidden_ref[0], w0[:, where], preferred_element_type=F32) + jnp.dot(
+        hidden_ref[1], w1[:, where], preferred_element_type=F32
+    )
+
+
+def next_kernel(quarter_ref, hidden_ref, w0, w1, top_ref, bottom_ref, right_ref, left_ref):
+    half, width = top_ref.shape
+    blocks = w0.shape[1] // width
+    right = down(hidden_ref, w0, w1, cut(quarter_ref, 1, blocks, width))
+    right_ref[0:half, :] = (right[0:half] + top_ref[...].astype(F32)).astype(BF16)
+    right_ref[half:, :] = right[half:].astype(BF16)
+    left = down(hidden_ref, w0, w1, cut(quarter_ref, blocks - 1, blocks, width))
+    left_ref[0:half, :] = left[0:half].astype(BF16)
+    left_ref[half:, :] = (left[half:] + bottom_ref[...].astype(F32)).astype(BF16)
+
+
+def own_kernel(quarter_ref, hidden_ref, w0, w1, out_ref):
+    width = out_ref.shape[1]
+    out_ref[...] = down(hidden_ref, w0, w1, cut(quarter_ref, 0, w0.shape[1] // width, width))
+
+
+def sum_kernel(own_ref, left_ref, right_ref, out_ref):
+    out_ref[...] = (
+        own_ref[...] + left_ref[...].astype(F32) + right_ref[...].astype(F32)
+    ).astype(BF16)
 
 
 def combine_kernel(slots_ref, route_ref, out_ref):
@@ -213,20 +250,49 @@
         slots.reshape(experts, half, lanes), "expert", 0, 0, tiled=True
     ).reshape(count, lanes)
 
-    blocks = [arrived] + [
-        lax.ppermute(arrived, "x", [(i, (i - step) % chips) for i in range(chips)])
-        for step in range(1, chips)
-    ]
-    partial = call(
-        expert_kernel,
-        jax.ShapeDtypeStruct((chips, count, lanes), BF16),
-        6 * count * width * gate_weight.shape[2] * CORES,
-        12 * width * gate_weight.shape[2],
-    )(x.astype(jnp.int32).reshape(1), *blocks, *weights, *others)
-    partial = lax.all_to_all(partial, "x", 0, 0, tiled=True)
-    summed = call(
-        sum_kernel, jax.ShapeDtypeStruct((count, lanes), BF16), count * width, 2 * count * width
-    )(partial)
+    quarter = x.astype(jnp.int32).reshape(1)
+    onward = [(i, (i + 1) % chips) for i in range(chips)]
+    backward = [(i, (i - 1) % chips) for i in range(chips)]
+    g0, u0, w0 = weights
+    g1, u1, w1 = others
+    cols = gate_weight.shape[2]
+    cut_rows = count // 2
+    left = lax.ppermute(arrived, "x", onward)
+    right = lax.ppermute(arrived, "x", backward)
+    top = lax.ppermute(left[:cut_rows], "x", onward)
+    bottom = lax.ppermute(right[cut_rows:], "x", backward)
+    near = call(
+        near_kernel,
+        jax.ShapeDtypeStruct((4, count, cols), F32),
+        24 * count * lanes * cols,
+        16 * lanes * cols + 16 * count * cols,
+    )(quarter, arrived, left, right, g0, u0, g1, u1)
+    hidden, far = call(
+        far_kernel,
+        (
+            jax.ShapeDtypeStruct((2, count, cols), BF16),
+            jax.ShapeDtypeStruct((2, cut_rows, lanes), BF16),
+        ),
+        12 * count * lanes * cols,
+        16 * count * cols,
+    )(quarter, near, top, bottom, g0, u0, g1, u1, w0, w1)
+    top = lax.ppermute(far[0], "x", onward)
+    bottom = lax.ppermute(far[1], "x", backward)
+    piece = jax.ShapeDtypeStruct((count, lanes), BF16)
+    to_right, to_left = call(
+        next_kernel, (piece, piece), 8 * count * lanes * cols, 8 * count * lanes
+    )(quarter, hidden, w0, w1, top, bottom)
+    left = lax.ppermute(to_right, "x", onward)
+    right = lax.ppermute(to_left, "x", backward)
+    own_sum = call(
+        own_kernel,
+        jax.ShapeDtypeStruct((count, lanes), F32),
+        4 * count * lanes * cols,
+        4 * count * lanes,
+    )(quarter, hidden, w0, w1)
+    summed = call(sum_kernel, piece, 2 * count * lanes, 10 * count * lanes)(
+        own_sum, left, right
+    )
     produced = lax.all_to_all(
         summed.reshape(images, half, lanes), "expert", 0, 0, tiled=True
     ).reshape(count, lanes)

time: 191 us -> 182 us (0.953)
  blocking collectives: 102 us -> 79.4 us
  starting transfers between devices: 31.6 us -> 45.6 us
    all_to_all x1 -> x0, blocking collectives: 29.3 us -> none  [body(): partial = lax.all_to_all(partial, 'x', 0, 0, tiled=True)]
    ppermute x3 -> x8, starting transfers between devices: 9.23 us -> 23 us  [the longest x1 4.24 us: body(): right = lax.ppermute(to_left, 'x', backward)]
    all_to_all x1, blocking collectives: 15.3 us -> 18.8 us  [body(): mixed = lax.all_to_all(mixed, tensor, 0, 0, tiled=True)]
    all_to_all x1, blocking collectives: 38.9 us -> 41.9 us  [body(): lax.all_to_all(summed.reshape(images, half, lanes), 'expert', 0, 0, tiled...]
    pallas_call x2 -> x5, Pallas kernels: 6.92 us -> 8.38 us  [the longest x1 3.88 us: body(): call(near_kernel, jax.ShapeDtypeStruct((4, count, cols), F32), 24 * count...]
    unnamed x16 -> x14, local copies, waits for them, and re-layouts: 4.53 us -> 3.45 us
    ppermute x3 -> x8, waiting for transfers between devices: 19.7 us -> 18.9 us  [the longest x1 5.61 us: body(): right = lax.ppermute(arrived, 'x', backward)]
  transfers between devices with their start and end apart: 7 -> 12, of which waited for: 4 -> 7; matrix products, arithmetic and copies ran while one was open for 0% -> 0% of each run, Pallas kernels for 0% -> 2%
where the time goes in v2:
time: 182 us; the launch traced here: 181 us
  blocking collectives  79.4 us (44%)
  starting transfers between devices  45.6 us (25%)
  waiting for transfers between devices  40.3 us (22%)
  Pallas kernels  12.1 us (7%)
  local copies, waits for them, and re-layouts  3.52 us (2%)
    all_to_all x1, blocking collectives, body(): lax.all_to_all(summed.reshape(images, half, lanes), 'expert', 0, 0, tiled...  41.9 us
    all_to_all x1, waiting for transfers between devices, body(): lax.all_to_all(slots.reshape(experts, half, lanes), 'expert', 0, 0, tiled...  21.4 us
    all_to_all x1, blocking collectives, body(): mixed = lax.all_to_all(mixed, tensor, 0, 0, tiled=True)  18.8 us
    all_to_all x1, blocking collectives, body(): packet = lax.all_to_all(packet, tensor, 0, 0, tiled=True)  18.6 us
    all_to_all x1, starting transfers between devices, body(): lax.all_to_all(slots.reshape(experts, half, lanes), 'expert', 0, 0, tiled...  15 us
    ppermute x3, starting transfers between devices, body(): others = [lax.ppermute(w, 'c', swap) for w in weights]  7.56 us
    ppermute x1, waiting for transfers between devices, body(): right = lax.ppermute(arrived, 'x', backward)  5.61 us
    ppermute x1, waiting for transfers between devices, body(): left = lax.ppermute(to_right, 'x', onward)  5.09 us
  transfers between devices with their start and end apart: 12, of which 7 were waited for; matrix products, arithmetic and copies ran while one was open for 0% of the time, Pallas kernels for 2%

profile of v2, /device:TPU:1, one launch (start us, length us, event | category | flops | bytes accessed | tf_op | source)
XLA Modules:
  0.0 181.1 jit_solution(17885510350112883795)
XLA Ops:
  0.0 0.0 copy-start.1
  0.0 0.0 copy-start
  0.0 0.0 copy-start.2
  0.0 1.1 copy-done.2
  1.1 0.0 copy-start.3
  1.1 0.9 copy-done.3
  2.0 0.0 copy-start.4
  2.0 0.7 copy-done.4
  2.8 0.0 copy-start.6
  2.8 0.7 copy-done.6
  3.4 0.6 shard_map.73
  4.1 18.6 %all_to_all.20.packet_ref = bf16[8,64,512]{2,1,0:T(8,128)(2,1)S(1)} all-to-all(bf16[8,64,512]{2,1,0:T(8,128)(2,1)S(1)} %shard_map.73), channel_id=1, replica_groups=mesh['expert'=64,'x'=4,'c'=2] {'x','c'}, dimensions={0} | all-to-all | bytes 1048576 | tf_op jit(solution)/shard_map/all_to_all | solution.py:239
  22.7 1.4 shard_map.74
  24.1 15.0 %all-to-all-start.1 = ((bf16[64,8,512]{2,1,0:T(8,128)(2,1)}), bf16[64,8,512]{2,1,0:T(8,128)(2,1)}, u32[]{:S(2)}, u32[]{:S(2)}) async-start(bf16[64,8,512]{2,1,0:T(8,128)(2,1)} %bitcast.6), calls=%async_computation.1 | async-start | bytes 1048576 | tf_op jit(solution)/shard_map/all_to_all | solution.py:249
  39.2 0.0 copy-done.1
  39.2 3.2 %collective-permute-start.2 = (bf16[2048,256]{1,0:T(8,128)(2,1)S(1)}, bf16[2048,256]{1,0:T(8,128)(2,1)}, u32[]{:S(2)}, u32[]{:S(2)}) collective-permute-start(bf16[2048,256]{1,0:T(8,128)(2,1)S(1)} %bitcast.21), channel_id=1, source_target_pairs={{0,1},{1,0},{2,3},{3,2},{4,5},{5,4},{6,7},{7,6},{8,9},{9,8},{10,11... | collective-permute-start | bytes 3145736 | tf_op jit(solution)/shard_map/ppermute | solution.py:225
  42.4 1.9 %collective-permute-start.3 = (bf16[2048,256]{1,0:T(8,128)(2,1)}, bf16[2048,256]{1,0:T(8,128)(2,1)}, u32[]{:S(2)}, u32[]{:S(2)}) collective-permute-start(bf16[2048,256]{1,0:T(8,128)(2,1)} %bitcast.9.u0), channel_id=1, source_target_pairs={{0,1},{1,0},{2,3},{3,2},{4,5},{5,4},{6,7},{7,6},{8,9},{9,8},{10,11... | collective-permute-start | bytes 3145736 | tf_op jit(solution)/shard_map/ppermute | solution.py:225
  44.4 0.0 copy-done
  44.4 2.4 %collective-permute-start.6 = (bf16[256,2048]{1,0:T(8,128)(2,1)S(1)}, bf16[256,2048]{1,0:T(8,128)(2,1)S(1)}, u32[]{:S(2)}, u32[]{:S(2)}) collective-permute-start(bf16[256,2048]{1,0:T(8,128)(2,1)S(1)} %bitcast.17), channel_id=1, source_target_pairs={{0,1},{1,0},{2,3},{3,2},{4,5},{5,4},{6,7},{7,6},{8,9},{9,8},{10,11... | collective-permute-start | bytes 3145736 | tf_op jit(solution)/shard_map/ppermute | solution.py:225
  46.8 21.4 %all-to-all-done.1 = bf16[64,8,512]{2,1,0:T(8,128)(2,1)} async-done(((bf16[64,8,512]{2,1,0:T(8,128)(2,1)}), bf16[64,8,512]{2,1,0:T(8,128)(2,1)}, u32[]{:S(2)}, u32[]{:S(2)}) %all-to-all-start.1) | async-done | bytes 524320 | tf_op jit(solution)/shard_map/all_to_all | solution.py:249
  68.2 2.8 %collective-permute-start.1 = (bf16[512,512]{1,0:T(8,128)(2,1)}, bf16[512,512]{1,0:T(8,128)(2,1)S(1)}, u32[]{:S(2)}, u32[]{:S(2)}) collective-permute-start(bf16[512,512]{1,0:T(8,128)(2,1)} %bitcast.7.a_ref), channel_id=1, source_target_pairs={{0,6},{2,0},{4,2},{6,4},{1,7},{3,1},{5,3},{7,5},{8,14},{10,8},{12,... | collective-permute-start | bytes 1572872 | tf_op jit(solution)/shard_map/ppermute | solution.py:261
  71.0 2.5 %collective-permute-start = (bf16[512,512]{1,0:T(8,128)(2,1)}, bf16[512,512]{1,0:T(8,128)(2,1)S(1)}, u32[]{:S(2)}, u32[]{:S(2)}) collective-permute-start(bf16[512,512]{1,0:T(8,128)(2,1)} %bitcast.7.a_ref), channel_id=1, source_target_pairs={{0,2},{2,4},{4,6},{6,0},{1,3},{3,5},{5,7},{7,1},{8,10},{10,12},{12... | collective-permute-start | bytes 1572872 | tf_op jit(solution)/shard_map/ppermute | solution.py:260
  73.5 5.6 %collective-permute-done.1.r_ref = bf16[512,512]{1,0:T(8,128)(2,1)S(1)} collective-permute-done((bf16[512,512]{1,0:T(8,128)(2,1)}, bf16[512,512]{1,0:T(8,128)(2,1)S(1)}, u32[]{:S(2)}, u32[]{:S(2)}) %collective-permute-start.1) | collective-permute-done | bytes 524320 | tf_op jit(solution)/shard_map/ppermute | solution.py:261
  79.1 4.0 %collective-permute-start.5 = (bf16[256,512]{1,0:T(8,128)(2,1)S(1)}, bf16[256,512]{1,0:T(8,128)(2,1)S(1)}, u32[]{:S(2)}, u32[]{:S(2)}) collective-permute-start(bf16[256,512]{1,0:T(8,128)(2,1)S(1)} %slice.17), channel_id=1, source_target_pairs={{0,6},{2,0},{4,2},{6,4},{1,7},{3,1},{5,3},{7,5},{8,14},{10,8},{12,... | collective-permute-start | bytes 786440 | tf_op jit(solution)/shard_map/ppermute | solution.py:263
  83.1 0.0 collective-permute-done.l_ref
  83.1 1.9 %collective-permute-start.4 = (bf16[256,512]{1,0:T(8,128)(2,1)S(1)}, bf16[256,512]{1,0:T(8,128)(2,1)S(1)}, u32[]{:S(2)}, u32[]{:S(2)}) collective-permute-start(bf16[256,512]{1,0:T(8,128)(2,1)S(1)} %slice.16), channel_id=1, source_target_pairs={{0,2},{2,4},{4,6},{6,0},{1,3},{3,5},{5,7},{7,1},{8,10},{10,12},{12... | collective-permute-start | bytes 786440 | tf_op jit(solution)/shard_map/ppermute | solution.py:262
  85.1 0.0 collective-permute-done.2.g1
  85.1 0.0 collective-permute-done.3.u1
  85.1 3.9 %shard_map.75.near_ref = f32[4,512,256]{2,1,0:T(8,128)S(1)} custom-call(s32[1]{0:T(128)} %bitcast.quarter_ref, bf16[512,512]{1,0:T(8,128)(2,1)} %bitcast.7.a_ref, bf16[512,512]{1,0:T(8,128)(2,1)S(1)} %collective-permute-done.l_ref, bf16[512,512]{1,0:T(8,128)(2,1)S(1)} %collective-permute-done.1.r_ref, bf16[2048,256]{1,0:T(8,128)(2,1)S(1)} %bitcast.22, ...), custom_call_target="tpu_custom_call" | custom-call | flops 1610612736 | bytes 4194304 | tf_op jit(solution)/shard_map/pallas_call | solution.py:264
  89.0 0.0 collective-permute-done.6.w1
  89.0 0.0 collective-permute-done.5.bottom_ref
  89.0 2.5 %collective-permute-done.4.top_ref = bf16[256,512]{1,0:T(8,128)(2,1)S(1)} collective-permute-done((bf16[256,512]{1,0:T(8,128)(2,1)S(1)}, bf16[256,512]{1,0:T(8,128)(2,1)S(1)}, u32[]{:S(2)}, u32[]{:S(2)}) %collective-permute-start.4) | collective-permute-done | bytes 262176 | tf_op jit(solution)/shard_map/ppermute | solution.py:262
  91.5 3.1 %shard_map.76 = (bf16[2,512,256]{2,1,0:T(8,128)(2,1)S(1)}, bf16[2,256,512]{2,1,0:T(8,128)(2,1)S(1)}) custom-call(s32[1]{0:T(128)} %bitcast.quarter_ref, f32[4,512,256]{2,1,0:T(8,128)S(1)} %shard_map.75.near_ref, bf16[256,512]{1,0:T(8,128)(2,1)S(1)} %collective-permute-done.4.top_ref, bf16[256,512]{1,0:T(8,128)(2,1)S(1)} %collective-permute-done.5.bottom_ref, ...), custom_call_target="tpu_custom_call" | custom-call | flops 805306368 | bytes 2097152 | tf_op jit(solution)/shard_map/pallas_call | solution.py:270
  94.6 2.1 %collective-permute-start.8 = (bf16[256,512]{1,0:T(8,128)(2,1)S(1)}, bf16[256,512]{1,0:T(8,128)(2,1)S(1)}, u32[]{:S(2)}, u32[]{:S(2)}) collective-permute-start(bf16[256,512]{1,0:T(8,128)(2,1)S(1)} %get-tuple-element.17), channel_id=1, source_target_pairs={{0,6},{2,0},{4,2},{6,4},{1,7},{3,1},{5,3},{7,5},{8,14},{10,8},{12,... | collective-permute-start | bytes 786440 | tf_op jit(solution)/shard_map/ppermute | solution.py:280
  96.8 3.2 %collective-permute-start.7 = (bf16[256,512]{1,0:T(8,128)(2,1)S(1)}, bf16[256,512]{1,0:T(8,128)(2,1)S(1)}, u32[]{:S(2)}, u32[]{:S(2)}) collective-permute-start(bf16[256,512]{1,0:T(8,128)(2,1)S(1)} %get-tuple-element.18), channel_id=1, source_target_pairs={{0,2},{2,4},{4,6},{6,0},{1,3},{3,5},{5,7},{7,1},{8,10},{10,12},{12... | collective-permute-start | bytes 786440 | tf_op jit(solution)/shard_map/ppermute | solution.py:279
  99.9 1.8 %collective-permute-done.8.bottom_ref = bf16[256,512]{1,0:T(8,128)(2,1)S(1)} collective-permute-done((bf16[256,512]{1,0:T(8,128)(2,1)S(1)}, bf16[256,512]{1,0:T(8,128)(2,1)S(1)}, u32[]{:S(2)}, u32[]{:S(2)}) %collective-permute-start.8) | collective-permute-done | bytes 262176 | tf_op jit(solution)/shard_map/ppermute | solution.py:280
  101.7 3.3 %collective-permute-done.7.top_ref = bf16[256,512]{1,0:T(8,128)(2,1)S(1)} collective-permute-done((bf16[256,512]{1,0:T(8,128)(2,1)S(1)}, bf16[256,512]{1,0:T(8,128)(2,1)S(1)}, u32[]{:S(2)}, u32[]{:S(2)}) %collective-permute-start.7) | collective-permute-done | bytes 262176 | tf_op jit(solution)/shard_map/ppermute | solution.py:279
  105.1 0.8 shard_map.78
  105.9 2.2 %collective-permute-start.9 = (bf16[512,512]{1,0:T(8,128)(2,1)S(1)}, bf16[512,512]{1,0:T(8,128)(2,1)S(1)}, u32[]{:S(2)}, u32[]{:S(2)}) collective-permute-start(bf16[512,512]{1,0:T(8,128)(2,1)S(1)} %get-tuple-element.14), channel_id=1, source_target_pairs={{0,2},{2,4},{4,6},{6,0},{1,3},{3,5},{5,7},{7,1},{8,10},{10,12},{12... | collective-permute-start | bytes 1572872 | tf_op jit(solution)/shard_map/ppermute | solution.py:285
  108.1 4.2 %collective-permute-start.10 = (bf16[512,512]{1,0:T(8,128)(2,1)S(1)}, bf16[512,512]{1,0:T(8,128)(2,1)S(1)}, u32[]{:S(2)}, u32[]{:S(2)}) collective-permute-start(bf16[512,512]{1,0:T(8,128)(2,1)S(1)} %get-tuple-element.15), channel_id=1, source_target_pairs={{0,6},{2,0},{4,2},{6,4},{1,7},{3,1},{5,3},{7,5},{8,14},{10,8},{12,... | collective-permute-start | bytes 1572872 | tf_op jit(solution)/shard_map/ppermute | solution.py:286
  112.4 0.5 shard_map.77.own_ref
  112.8 5.1 %collective-permute-done.9.left_ref = bf16[512,512]{1,0:T(8,128)(2,1)S(1)} collective-permute-done((bf16[512,512]{1,0:T(8,128)(2,1)S(1)}, bf16[512,512]{1,0:T(8,128)(2,1)S(1)}, u32[]{:S(2)}, u32[]{:S(2)}) %collective-permute-start.9) | collective-permute-done | bytes 524320 | tf_op jit(solution)/shard_map/ppermute | solution.py:285
  117.9 0.5 collective-permute-done.10.right_ref
  118.5 0.2 shard_map.79
  118.6 0.0 copy-start.5
  118.6 41.9 %all_to_all.21 = bf16[64,8,512]{2,1,0:T(8,128)(2,1)S(1)} all-to-all(bf16[64,8,512]{2,1,0:T(8,128)(2,1)S(1)} %bitcast.24), channel_id=1, replica_groups=mesh['expert'=64,'x'=4,'c'=2] {'expert'}, dimensions={0} | all-to-all | bytes 1048576 | tf_op jit(solution)/shard_map/all_to_all | solution.py:296
  160.6 0.9 shard_map.80
  161.5 18.8 %all_to_all.22.parts_ref = bf16[8,48,512]{2,1,0:T(8,128)(2,1)S(1)} all-to-all(bf16[8,48,512]{2,1,0:T(8,128)(2,1)S(1)} %shard_map.80), channel_id=1, replica_groups=mesh['expert'=64,'x'=4,'c'=2] {'x','c'}, dimensions={0} | all-to-all | bytes 786432 | tf_op jit(solution)/shard_map/all_to_all | solution.py:305
  180.3 0.0 copy-done.5
  180.3 0.7 shard_map.81
  (3 shorter events, 0.1 us)
Async XLA Ops:
  0.0 39.2 %copy-start.1 = (bf16[1,2048,256]{2,1,0:T(8,128)(2,1)S(1)}, bf16[1,2048,256]{2,1,0:T(8,128)(2,1)}, u32[]{:S(2)}) copy-start(bf16[1,2048,256]{2,1,0:T(8,128)(2,1)} %param.10) | copy-start | bytes 3145732
  0.0 44.4 %copy-start = (bf16[1,256,2048]{2,1,0:T(8,128)(2,1)S(1)}, bf16[1,256,2048]{2,1,0:T(8,128)(2,1)}, u32[]{:S(2)}) copy-start(bf16[1,256,2048]{2,1,0:T(8,128)(2,1)} %param.12) | copy-start | bytes 3145732
  0.0 1.1 copy-start.2
  1.1 0.9 copy-start.3
  2.0 0.7 copy-start.4
  2.8 0.7 copy-start.6
  24.1 44.0 %all-to-all-start.1 = ((bf16[64,8,512]{2,1,0:T(8,128)(2,1)}), bf16[64,8,512]{2,1,0:T(8,128)(2,1)}, u32[]{:S(2)}, u32[]{:S(2)}) async-start(bf16[64,8,512]{2,1,0:T(8,128)(2,1)} %bitcast.6), calls=%async_computation.1 | async-start | bytes 1048576 | tf_op jit(solution)/shard_map/all_to_all | solution.py:249
  39.2 45.9 %collective-permute-start.2 = (bf16[2048,256]{1,0:T(8,128)(2,1)S(1)}, bf16[2048,256]{1,0:T(8,128)(2,1)}, u32[]{:S(2)}, u32[]{:S(2)}) collective-permute-start(bf16[2048,256]{1,0:T(8,128)(2,1)S(1)} %bitcast.21), channel_id=1, source_target_pairs={{0,1},{1,0},{2,3},{3,2},{4,5},{5,4},{6,7},{7,6},{8,9},{9,8},{10,11... | collective-permute-start | bytes 3145736 | tf_op jit(solution)/shard_map/ppermute | solution.py:225
  42.4 42.7 %collective-permute-start.3 = (bf16[2048,256]{1,0:T(8,128)(2,1)}, bf16[2048,256]{1,0:T(8,128)(2,1)}, u32[]{:S(2)}, u32[]{:S(2)}) collective-permute-start(bf16[2048,256]{1,0:T(8,128)(2,1)} %bitcast.9.u0), channel_id=1, source_target_pairs={{0,1},{1,0},{2,3},{3,2},{4,5},{5,4},{6,7},{7,6},{8,9},{9,8},{10,11... | collective-permute-start | bytes 3145736 | tf_op jit(solution)/shard_map/ppermute | solution.py:225
  44.4 44.6 %collective-permute-start.6 = (bf16[256,2048]{1,0:T(8,128)(2,1)S(1)}, bf16[256,2048]{1,0:T(8,128)(2,1)S(1)}, u32[]{:S(2)}, u32[]{:S(2)}) collective-permute-start(bf16[256,2048]{1,0:T(8,128)(2,1)S(1)} %bitcast.17), channel_id=1, source_target_pairs={{0,1},{1,0},{2,3},{3,2},{4,5},{5,4},{6,7},{7,6},{8,9},{9,8},{10,11... | collective-permute-start | bytes 3145736 | tf_op jit(solution)/shard_map/ppermute | solution.py:225
  68.2 10.9 %collective-permute-start.1 = (bf16[512,512]{1,0:T(8,128)(2,1)}, bf16[512,512]{1,0:T(8,128)(2,1)S(1)}, u32[]{:S(2)}, u32[]{:S(2)}) collective-permute-start(bf16[512,512]{1,0:T(8,128)(2,1)} %bitcast.7.a_ref), channel_id=1, source_target_pairs={{0,6},{2,0},{4,2},{6,4},{1,7},{3,1},{5,3},{7,5},{8,14},{10,8},{12,... | collective-permute-start | bytes 1572872 | tf_op jit(solution)/shard_map/ppermute | solution.py:261
  71.0 12.1 %collective-permute-start = (bf16[512,512]{1,0:T(8,128)(2,1)}, bf16[512,512]{1,0:T(8,128)(2,1)S(1)}, u32[]{:S(2)}, u32[]{:S(2)}) collective-permute-start(bf16[512,512]{1,0:T(8,128)(2,1)} %bitcast.7.a_ref), channel_id=1, source_target_pairs={{0,2},{2,4},{4,6},{6,0},{1,3},{3,5},{5,7},{7,1},{8,10},{10,12},{12... | collective-permute-start | bytes 1572872 | tf_op jit(solution)/shard_map/ppermute | solution.py:260
  79.1 9.9 %collective-permute-start.5 = (bf16[256,512]{1,0:T(8,128)(2,1)S(1)}, bf16[256,512]{1,0:T(8,128)(2,1)S(1)}, u32[]{:S(2)}, u32[]{:S(2)}) collective-permute-start(bf16[256,512]{1,0:T(8,128)(2,1)S(1)} %slice.17), channel_id=1, source_target_pairs={{0,6},{2,0},{4,2},{6,4},{1,7},{3,1},{5,3},{7,5},{8,14},{10,8},{12,... | collective-permute-start | bytes 786440 | tf_op jit(solution)/shard_map/ppermute | solution.py:263
  83.1 8.3 %collective-permute-start.4 = (bf16[256,512]{1,0:T(8,128)(2,1)S(1)}, bf16[256,512]{1,0:T(8,128)(2,1)S(1)}, u32[]{:S(2)}, u32[]{:S(2)}) collective-permute-start(bf16[256,512]{1,0:T(8,128)(2,1)S(1)} %slice.16), channel_id=1, source_target_pairs={{0,2},{2,4},{4,6},{6,0},{1,3},{3,5},{5,7},{7,1},{8,10},{10,12},{12... | collective-permute-start | bytes 786440 | tf_op jit(solution)/shard_map/ppermute | solution.py:262
  94.6 7.1 %collective-permute-start.8 = (bf16[256,512]{1,0:T(8,128)(2,1)S(1)}, bf16[256,512]{1,0:T(8,128)(2,1)S(1)}, u32[]{:S(2)}, u32[]{:S(2)}) collective-permute-start(bf16[256,512]{1,0:T(8,128)(2,1)S(1)} %get-tuple-element.17), channel_id=1, source_target_pairs={{0,6},{2,0},{4,2},{6,4},{1,7},{3,1},{5,3},{7,5},{8,14},{10,8},{12,... | collective-permute-start | bytes 786440 | tf_op jit(solution)/shard_map/ppermute | solution.py:280
  96.8 8.3 %collective-permute-start.7 = (bf16[256,512]{1,0:T(8,128)(2,1)S(1)}, bf16[256,512]{1,0:T(8,128)(2,1)S(1)}, u32[]{:S(2)}, u32[]{:S(2)}) collective-permute-start(bf16[256,512]{1,0:T(8,128)(2,1)S(1)} %get-tuple-element.18), channel_id=1, source_target_pairs={{0,2},{2,4},{4,6},{6,0},{1,3},{3,5},{5,7},{7,1},{8,10},{10,12},{12... | collective-permute-start | bytes 786440 | tf_op jit(solution)/shard_map/ppermute | solution.py:279
  105.9 12.1 %collective-permute-start.9 = (bf16[512,512]{1,0:T(8,128)(2,1)S(1)}, bf16[512,512]{1,0:T(8,128)(2,1)S(1)}, u32[]{:S(2)}, u32[]{:S(2)}) collective-permute-start(bf16[512,512]{1,0:T(8,128)(2,1)S(1)} %get-tuple-element.14), channel_id=1, source_target_pairs={{0,2},{2,4},{4,6},{6,0},{1,3},{3,5},{5,7},{7,1},{8,10},{10,12},{12... | collective-permute-start | bytes 1572872 | tf_op jit(solution)/shard_map/ppermute | solution.py:285
  108.1 10.4 %collective-permute-start.10 = (bf16[512,512]{1,0:T(8,128)(2,1)S(1)}, bf16[512,512]{1,0:T(8,128)(2,1)S(1)}, u32[]{:S(2)}, u32[]{:S(2)}) collective-permute-start(bf16[512,512]{1,0:T(8,128)(2,1)S(1)} %get-tuple-element.15), channel_id=1, source_target_pairs={{0,6},{2,0},{4,2},{6,4},{1,7},{3,1},{5,3},{7,5},{8,14},{10,8},{12,... | collective-permute-start | bytes 1572872 | tf_op jit(solution)/shard_map/ppermute | solution.py:286
  118.6 61.7 %copy-start.5 = (f32[1,3,2048]{2,0,1:T(1,128)S(1)}, f32[1,3,2048]{2,0,1:T(1,128)}, u32[]{:S(2)}) copy-start(f32[1,3,2048]{2,0,1:T(1,128)} %param.8) | copy-start | bytes 73732

commit v3 on v2

--- a/solution.py
+++ b/solution.py
@@ -15,14 +15,21 @@
 PAD = 64
 ROUTE = 16
 VMEM_LIMIT = 12 * 1024 * 1024
-
-
-def call(kernel, out_shape, flops, nbytes):
+FIRST_LIMIT = 60 * 1024 * 1024
+
+
+def call(kernel, out_shape, flops, nbytes, spaces=None, scratch=(), limit=VMEM_LIMIT):
+    kinds = {"v": pltpu.VMEM, "h": pltpu.HBM}
+    specs = {}
+    if spaces is not None:
+        specs = {"in_specs": [pl.BlockSpec(memory_space=kinds[kind]) for kind in spaces]}
     return pl.pallas_call(
         kernel,
         out_shape=out_shape,
-        compiler_params=pltpu.CompilerParams(vmem_limit_bytes=VMEM_LIMIT),
+        scratch_shapes=scratch,
+        compiler_params=pltpu.CompilerParams(vmem_limit_bytes=limit),
         cost_estimate=pl.CostEstimate(flops=flops, bytes_accessed=nbytes, transcendentals=0),
+        **specs,
     )
 
 
@@ -31,7 +38,19 @@
     return high, value - high
 
 
-def modulate_kernel(member_ref, tokens_ref, modulation_ref, router_ref, ids_ref, packet_ref):
+def modulate_kernel(
+    member_ref, ids_ref, tokens_in, modulation_in, router_in, packet_ref,
+    tokens_ref, modulation_ref, router_ref, arrived,
+):
+    copies = [
+        pltpu.make_async_copy(source, target, arrived.at[index])
+        for index, (source, target) in enumerate(
+            ((tokens_in, tokens_ref), (modulation_in, modulation_ref), (router_in, router_ref))
+        )
+    ]
+    for copy in copies:
+        copy.start()
+    copies[0].wait()
     rows, width = tokens_ref.shape
     lanes = packet_ref.shape[2]
     values = tokens_ref[...].astype(F32)
@@ -39,6 +58,8 @@
     centred = values - average
     spread = jnp.mean(centred * centred, axis=-1, keepdims=True)
     normed = centred * lax.rsqrt(spread + EPS)
+    copies[1].wait()
+    copies[2].wait()
     modulated = (normed * (1.0 + modulation_ref[1]) + modulation_ref[0]).astype(BF16)
     logits = lax.dot_general(
         router_ref[...], modulated, (((1,), (1,)), ((), ())), preferred_element_type=F32
@@ -116,67 +137,108 @@
     return pl.ds(pl.multiple_of(lax.rem(quarter_ref[0] + step, blocks) * width, width), width)
 
 
-def near_kernel(quarter_ref, a_ref, l_ref, r_ref, g0, u0, g1, u1, out_ref):
-    width = a_ref.shape[1]
+def near_kernel(quarter_ref, a_ref, l0, l1, r0, r1, g0, u0, g1, u1, out_ref, held, arrived):
+    rows, width = l0.shape
     blocks = g0.shape[0] // width
-    for index, weight_ref in enumerate((g0, u0, g1, u1)):
-        total = None
-        for step, ref in ((0, a_ref), (1, r_ref), (blocks - 1, l_ref)):
-            rows = weight_ref[cut(quarter_ref, step, blocks, width), :]
-            term = jnp.dot(ref[...], rows, preferred_element_type=F32)
-            total = term if total is None else total + term
-        out_ref[index] = total
+    copies = [
+        [
+            pltpu.make_async_copy(
+                weight_ref.at[cut(quarter_ref, step, blocks, width), :],
+                held.at[index, place],
+                arrived.at[index, place],
+            )
+            for place, step in enumerate((0, blocks - 1, 1))
+        ]
+        for index, weight_ref in enumerate((g0, u0, g1, u1))
+    ]
+    for group in copies:
+        for copy in group:
+            copy.start()
+    for index, group in enumerate(copies):
+        for copy in group:
+            copy.wait()
+        for part, (l_ref, r_ref) in enumerate(((l0, r0), (l1, r1))):
+            span = slice(part * rows, (part + 1) * rows)
+            out_ref[index, span, :] = (
+                jnp.dot(a_ref[span, :], held[index, 0], preferred_element_type=F32)
+                + jnp.dot(l_ref[...], held[index, 1], preferred_element_type=F32)
+                + jnp.dot(r_ref[...], held[index, 2], preferred_element_type=F32)
+            )
 
 
 def far_kernel(
-    quarter_ref, near_ref, top_ref, bottom_ref, g0, u0, g1, u1, w0, w1, hidden_ref, out_ref
+    quarter_ref, near_ref, top_ref, bottom_ref, g0, u0, g1, u1, w0, w1,
+    hidden_ref, out_ref, held, held_down, arrived,
 ):
     rows, width = top_ref.shape
     blocks = g0.shape[0] // width
     where = cut(quarter_ref, blocks // 2, blocks, width)
-    for part, ref in enumerate((top_ref, bottom_ref)):
+    copies = [
+        pltpu.make_async_copy(weight_ref.at[where, :], held.at[index], arrived.at[index])
+        for index, weight_ref in enumerate((g0, u0, g1, u1))
+    ] + [
+        pltpu.make_async_copy(down_ref.at[:, where], held_down.at[core], arrived.at[4 + core])
+        for core, down_ref in enumerate((w0, w1))
+    ]
+    for copy in copies:
+        copy.start()
+    for core in range(2):
+        copies[2 * core].wait()
+        copies[2 * core + 1].wait()
+        for part, ref in enumerate((top_ref, bottom_ref)):
+            span = slice(part * rows, (part + 1) * rows)
+            gate, up = [
+                near_ref[index, span, :]
+                + jnp.dot(ref[...], held[index], preferred_element_type=F32)
+                for index in (2 * core, 2 * core + 1)
+            ]
+            hidden_ref[core, span, :] = (gate * jax.nn.sigmoid(gate) * up).astype(BF16)
+    copies[4].wait()
+    copies[5].wait()
+    for part in range(2):
         span = slice(part * rows, (part + 1) * rows)
-        total = [
-            near_ref[index, span, :]
-            + jnp.dot(ref[...], weight_ref[where, :], preferred_element_type=F32)
-            for index, weight_ref in enumerate((g0, u0, g1, u1))
-        ]
-        far = None
-        for core, down_ref in enumerate((w0, w1)):
-            gate, up = total[2 * core], total[2 * core + 1]
-            hidden = (gate * jax.nn.sigmoid(gate) * up).astype(BF16)
-            hidden_ref[core, span, :] = hidden
-            term = jnp.dot(hidden, down_ref[:, where], preferred_element_type=F32)
-            far = term if far is None else far + term
-        out_ref[part] = far.astype(BF16)
-
-
-def down(hidden_ref, w0, w1, where):
-    return jnp.dot(hidden_ref[0], w0[:, where], preferred_element_type=F32) + jnp.dot(
-        hidden_ref[1], w1[:, where], preferred_element_type=F32
-    )
-
-
-def next_kernel(quarter_ref, hidden_ref, w0, w1, top_ref, bottom_ref, right_ref, left_ref):
-    half, width = top_ref.shape
+        out_ref[part] = (
+            jnp.dot(hidden_ref[0, span, :], held_down[0], preferred_element_type=F32)
+            + jnp.dot(hidden_ref[1, span, :], held_down[1], preferred_element_type=F32)
+        ).astype(BF16)
+
+
+def down(hidden_ref, span, w0, w1, where):
+    return jnp.dot(hidden_ref[0, span, :], w0[:, where], preferred_element_type=F32) + jnp.dot(
+        hidden_ref[1, span, :], w1[:, where], preferred_element_type=F32
+    )
+
+
+def direct_kernel(quarter_ref, hidden_ref, w0, w1, right_ref, left_ref):
+    rows, width = right_ref.shape
     blocks = w0.shape[1] // width
-    right = down(hidden_ref, w0, w1, cut(quarter_ref, 1, blocks, width))
-    right_ref[0:half, :] = (right[0:half] + top_ref[...].astype(F32)).astype(BF16)
-    right_ref[half:, :] = right[half:].astype(BF16)
-    left = down(hidden_ref, w0, w1, cut(quarter_ref, blocks - 1, blocks, width))
-    left_ref[0:half, :] = left[0:half].astype(BF16)
-    left_ref[half:, :] = (left[half:] + bottom_ref[...].astype(F32)).astype(BF16)
+    right = down(hidden_ref, slice(rows, None), w0, w1, cut(quarter_ref, 1, blocks, width))
+    left = down(hidden_ref, slice(0, rows), w0, w1, cut(quarter_ref, blocks - 1, blocks, width))
+    right_ref[...] = right.astype(BF16)
+    left_ref[...] = left.astype(BF16)
+
+
+def relay_kernel(quarter_ref, hidden_ref, w0, w1, top_ref, bottom_ref, right_ref, left_ref):
+    rows, width = right_ref.shape
+    blocks = w0.shape[1] // width
+    right = down(hidden_ref, slice(0, rows), w0, w1, cut(quarter_ref, 1, blocks, width))
+    left = down(hidden_ref, slice(rows, None), w0, w1, cut(quarter_ref, blocks - 1, blocks, width))
+    right_ref[...] = (right + top_ref[...].astype(F32)).astype(BF16)
+    left_ref[...] = (left + bottom_ref[...].astype(F32)).astype(BF16)
 
 
 def own_kernel(quarter_ref, hidden_ref, w0, w1, out_ref):
     width = out_ref.shape[1]
-    out_ref[...] = down(hidden_ref, w0, w1, cut(quarter_ref, 0, w0.shape[1] // width, width))
-
-
-def sum_kernel(own_ref, left_ref, right_ref, out_ref):
-    out_ref[...] = (
-        own_ref[...] + left_ref[...].astype(F32) + right_ref[...].astype(F32)
-    ).astype(BF16)
+    where = cut(quarter_ref, 0, w0.shape[1] // width, width)
+    out_ref[...] = down(hidden_ref, slice(None), w0, w1, where)
+
+
+def sum_kernel(own_ref, l0, l1, r0, r1, out_ref):
+    rows = l0.shape[0]
+    for part, (l_ref, r_ref) in enumerate(((l0, r0), (l1, r1))):
+        span = slice(part * rows, (part + 1) * rows)
+        total = own_ref[span, :] + l_ref[...].astype(F32) + r_ref[...].astype(F32)
+        out_ref[span, :] = total.astype(BF16)
 
 
 def combine_kernel(slots_ref, route_ref, out_ref):
@@ -219,22 +281,30 @@
     x = lax.axis_index("x")
     core = lax.axis_index("c")
     tensor = ("x", "c")
-    modulation = jnp.transpose(modulation, (1, 0, 2))
     swap = [(0, 1), (1, 0)]
     weights = [gate_weight[0], up_weight[0], down_weight[0]]
     others = [lax.ppermute(w, "c", swap) for w in weights]
 
+    shift_scale_gate = jnp.transpose(modulation, (1, 0, 2))
     packet = call(
         modulate_kernel,
         jax.ShapeDtypeStruct((members, PAD, lanes), BF16),
         2 * own * width * experts,
         4 * own * width,
+        "vvhhh",
+        [
+            pltpu.VMEM(tokens.shape, BF16),
+            pltpu.VMEM(shift_scale_gate.shape, F32),
+            pltpu.VMEM((experts, width), BF16),
+            pltpu.SemaphoreType.DMA((3,)),
+        ],
+        FIRST_LIMIT,
     )(
         (x * CORES + core).astype(jnp.int32).reshape(1),
+        expert_ids.T,
         tokens,
-        modulation,
+        shift_scale_gate,
         w_router.T,
-        expert_ids.T,
     )
     packet = lax.all_to_all(packet, tensor, 0, 0, tiled=True)
     slots, route = call(
@@ -257,16 +327,21 @@
     g1, u1, w1 = others
     cols = gate_weight.shape[2]
     cut_rows = count // 2
-    left = lax.ppermute(arrived, "x", onward)
-    right = lax.ppermute(arrived, "x", backward)
-    top = lax.ppermute(left[:cut_rows], "x", onward)
-    bottom = lax.ppermute(right[cut_rows:], "x", backward)
+    upper, lower = arrived[:cut_rows], arrived[cut_rows:]
+    l0 = lax.ppermute(upper, "x", onward)
+    r1 = lax.ppermute(lower, "x", backward)
+    l1 = lax.ppermute(lower, "x", onward)
+    r0 = lax.ppermute(upper, "x", backward)
+    top = lax.ppermute(l0, "x", onward)
+    bottom = lax.ppermute(r1, "x", backward)
     near = call(
         near_kernel,
         jax.ShapeDtypeStruct((4, count, cols), F32),
         24 * count * lanes * cols,
         16 * lanes * cols + 16 * count * cols,
-    )(quarter, arrived, left, right, g0, u0, g1, u1)
+        "vvvvvvhhhh",
+        [pltpu.VMEM((4, 3, lanes, cols), BF16), pltpu.SemaphoreType.DMA((4, 3))],
+    )(quarter, arrived, l0, l1, r0, r1, g0, u0, g1, u1)
     hidden, far = call(
         far_kernel,
         (
@@ -275,24 +350,38 @@
         ),
         12 * count * lanes * cols,
         16 * count * cols,
+        "vvvvhhhhhh",
+        [
+            pltpu.VMEM((4, lanes, cols), BF16),
+            pltpu.VMEM((2, cols, lanes), BF16),
+            pltpu.SemaphoreType.DMA((6,)),
+        ],
     )(quarter, near, top, bottom, g0, u0, g1, u1, w0, w1)
     top = lax.ppermute(far[0], "x", onward)
     bottom = lax.ppermute(far[1], "x", backward)
-    piece = jax.ShapeDtypeStruct((count, lanes), BF16)
+    piece = jax.ShapeDtypeStruct((cut_rows, lanes), BF16)
+    direct_right, direct_left = call(
+        direct_kernel, (piece, piece), 4 * count * lanes * cols, 4 * count * lanes
+    )(quarter, hidden, w0, w1)
+    l1 = lax.ppermute(direct_right, "x", onward)
+    r0 = lax.ppermute(direct_left, "x", backward)
     to_right, to_left = call(
-        next_kernel, (piece, piece), 8 * count * lanes * cols, 8 * count * lanes
+        relay_kernel, (piece, piece), 4 * count * lanes * cols, 4 * count * lanes
     )(quarter, hidden, w0, w1, top, bottom)
-    left = lax.ppermute(to_right, "x", onward)
-    right = lax.ppermute(to_left, "x", backward)
+    l0 = lax.ppermute(to_right, "x", onward)
+    r1 = lax.ppermute(to_left, "x", backward)
     own_sum = call(
         own_kernel,
         jax.ShapeDtypeStruct((count, lanes), F32),
         4 * count * lanes * cols,
         4 * count * lanes,
     )(quarter, hidden, w0, w1)
-    summed = call(sum_kernel, piece, 2 * count * lanes, 10 * count * lanes)(
-        own_sum, left, right
-    )
+    summed = call(
+        sum_kernel,
+        jax.ShapeDtypeStruct((count, lanes), BF16),
+        2 * count * lanes,
+        10 * count * lanes,
+    )(own_sum, l0, l1, r0, r1)
     produced = lax.all_to_all(
         summed.reshape(images, half, lanes), "expert", 0, 0, tiled=True
     ).reshape(count, lanes)
@@ -305,7 +394,7 @@
     mixed = lax.all_to_all(mixed, tensor, 0, 0, tiled=True)
     return call(
         gate_kernel, jax.ShapeDtypeStruct((own, width), BF16), own * width, 4 * own * width
-    )(mixed, modulation)
+    )(mixed, shift_scale_gate)
 
 
 def solution(mesh):

time: 182 us -> 174 us (0.956)
  waiting for transfers between devices: 40.3 us -> 27.9 us
  starting transfers between devices: 45.6 us -> 56.9 us
  blocking collectives: 79.4 us -> 74.2 us
  local copies, waits for them, and re-layouts: 3.52 us -> 0.08 us
    ppermute x6 -> x10, starting transfers between devices: 17.7 us -> 30 us  [the longest x1 4.57 us: body(): r0 = lax.ppermute(direct_left, 'x', backward)]
    all_to_all x1, blocking collectives: 41.9 us -> 34.3 us  [body(): lax.all_to_all(summed.reshape(images, half, lanes), 'expert', 0, 0, tiled...]
    ppermute x6 -> x10, waiting for transfers between devices: 13.7 us -> 6.34 us  [the longest x1 3.25 us: body(): l0 = lax.ppermute(to_right, 'x', onward)]
    unnamed x14 -> x4, local copies, waits for them, and re-layouts: 3.45 us -> 0.01 us
    ppermute x1, waiting for transfers between devices: 3.33 us -> 0.01 us  [body(): top = lax.ppermute(far[0], 'x', onward)]
    pallas_call x1, Pallas kernels: 0.62 us -> 3.15 us  [body(): call(modulate_kernel, jax.ShapeDtypeStruct((members, PAD, lanes), BF16),...]
  transfers between devices with their start and end apart: 12 -> 16, of which waited for: 7 -> 4; matrix products, arithmetic and copies ran while one was open for 0% -> 0% of each run, Pallas kernels for 2% -> 3%
where the time goes in v3:
time: 174 us; the launch traced here: 173 us
  blocking collectives  74.2 us (43%)
  starting transfers between devices  56.9 us (33%)
  waiting for transfers between devices  27.9 us (16%)
  Pallas kernels  13.9 us (8%)
    all_to_all x1, blocking collectives, body(): lax.all_to_all(summed.reshape(images, half, lanes), 'expert', 0, 0, tiled...  34.3 us
    all_to_all x1, waiting for transfers between devices, body(): lax.all_to_all(slots.reshape(experts, half, lanes), 'expert', 0, 0, tiled...  21.6 us
    all_to_all x1, blocking collectives, body(): mixed = lax.all_to_all(mixed, tensor, 0, 0, tiled=True)  20.3 us
    all_to_all x1, blocking collectives, body(): packet = lax.all_to_all(packet, tensor, 0, 0, tiled=True)  19.6 us
    all_to_all x1, starting transfers between devices, body(): lax.all_to_all(slots.reshape(experts, half, lanes), 'expert', 0, 0, tiled...  14 us
    ppermute x3, starting transfers between devices, body(): others = [lax.ppermute(w, 'c', swap) for w in weights]  7.57 us
    ppermute x1, starting transfers between devices, body(): r0 = lax.ppermute(direct_left, 'x', backward)  4.57 us
    ppermute x1, starting transfers between devices, body(): r1 = lax.ppermute(to_left, 'x', backward)  4.57 us
  transfers between devices with their start and end apart: 16, of which 4 were waited for; matrix products, arithmetic and copies ran while one was open for 0% of the time, Pallas kernels for 3%

profile of v3, /device:TPU:1, one launch (start us, length us, event | category | flops | bytes accessed | tf_op | source)
XLA Modules:
  0.0 173.3 jit_solution(3445929686186968070)
XLA Ops:
  0.0 0.0 copy-start
  0.0 3.2 %shard_map.73 = bf16[8,64,512]{2,1,0:T(8,128)(2,1)} custom-call(s32[1]{0:T(128)} %bitcast.2.member_ref, s32[2,48]{1,0:T(2,128)} %bitcast.32, bf16[48,2048]{1,0:T(8,128)(2,1)} %tokens_in.1, f32[3,1,2048]{2,1,0:T(1,128)} %bitcast.29, bf16[64,2048]{1,0:T(8,128)(2,1)} %bitcast.31), custom_call_target="tpu_custom_call" | custom-call | flops 12582912 | bytes 393216 | tf_op jit(solution)/shard_map/pallas_call | solution.py:289
  3.2 19.6 %all_to_all.20.packet_ref = bf16[8,64,512]{2,1,0:T(8,128)(2,1)S(1)} all-to-all(bf16[8,64,512]{2,1,0:T(8,128)(2,1)} %shard_map.73), channel_id=1, replica_groups=mesh['expert'=64,'x'=4,'c'=2] {'x','c'}, dimensions={0} | all-to-all | bytes 1048576 | tf_op jit(solution)/shard_map/all_to_all | solution.py:309
  22.8 1.4 shard_map.74
  24.2 14.0 %all-to-all-start.1 = ((bf16[64,8,512]{2,1,0:T(8,128)(2,1)}), bf16[64,8,512]{2,1,0:T(8,128)(2,1)S(1)}, u32[]{:S(2)}, u32[]{:S(2)}) async-start(bf16[64,8,512]{2,1,0:T(8,128)(2,1)} %bitcast.6), calls=%async_computation.1 | async-start | bytes 1048576 | tf_op jit(solution)/shard_map/all_to_all | solution.py:319
  38.2 3.2 %collective-permute-start.4 = (bf16[2048,256]{1,0:T(8,128)(2,1)}, bf16[2048,256]{1,0:T(8,128)(2,1)}, u32[]{:S(2)}, u32[]{:S(2)}) collective-permute-start(bf16[2048,256]{1,0:T(8,128)(2,1)} %bitcast.10.g0), channel_id=1, source_target_pairs={{0,1},{1,0},{2,3},{3,2},{4,5},{5,4},{6,7},{7,6},{8,9},{9,8},{10,11... | collective-permute-start | bytes 3145736 | tf_op jit(solution)/shard_map/ppermute | solution.py:286
  41.5 1.9 %collective-permute-start.5 = (bf16[2048,256]{1,0:T(8,128)(2,1)}, bf16[2048,256]{1,0:T(8,128)(2,1)}, u32[]{:S(2)}, u32[]{:S(2)}) collective-permute-start(bf16[2048,256]{1,0:T(8,128)(2,1)} %bitcast.11.u0), channel_id=1, source_target_pairs={{0,1},{1,0},{2,3},{3,2},{4,5},{5,4},{6,7},{7,6},{8,9},{9,8},{10,11... | collective-permute-start | bytes 3145736 | tf_op jit(solution)/shard_map/ppermute | solution.py:286
  43.4 0.0 copy-done
  43.4 2.4 %collective-permute-start.8 = (bf16[256,2048]{1,0:T(8,128)(2,1)S(1)}, bf16[256,2048]{1,0:T(8,128)(2,1)S(1)}, u32[]{:S(2)}, u32[]{:S(2)}) collective-permute-start(bf16[256,2048]{1,0:T(8,128)(2,1)S(1)} %bitcast.21), channel_id=1, source_target_pairs={{0,1},{1,0},{2,3},{3,2},{4,5},{5,4},{6,7},{7,6},{8,9},{9,8},{10,11... | collective-permute-start | bytes 3145736 | tf_op jit(solution)/shard_map/ppermute | solution.py:286
  45.8 21.6 %all-to-all-done.1 = bf16[64,8,512]{2,1,0:T(8,128)(2,1)S(1)} async-done(((bf16[64,8,512]{2,1,0:T(8,128)(2,1)}), bf16[64,8,512]{2,1,0:T(8,128)(2,1)S(1)}, u32[]{:S(2)}, u32[]{:S(2)}) %all-to-all-start.1) | async-done | bytes 524320 | tf_op jit(solution)/shard_map/all_to_all | solution.py:319
  67.4 2.8 %collective-permute-start.3 = (bf16[256,512]{1,0:T(8,128)(2,1)S(1)}, bf16[256,512]{1,0:T(8,128)(2,1)S(1)}, u32[]{:S(2)}, u32[]{:S(2)}) collective-permute-start(bf16[256,512]{1,0:T(8,128)(2,1)S(1)} %get-tuple-element.23), channel_id=1, source_target_pairs={{0,6},{2,0},{4,2},{6,4},{1,7},{3,1},{5,3},{7,5},{8,14},{10,8},{12,... | collective-permute-start | bytes 786440 | tf_op jit(solution)/shard_map/ppermute | solution.py:332
  70.2 2.5 %collective-permute-start = (bf16[256,512]{1,0:T(8,128)(2,1)S(1)}, bf16[256,512]{1,0:T(8,128)(2,1)S(1)}, u32[]{:S(2)}, u32[]{:S(2)}) collective-permute-start(bf16[256,512]{1,0:T(8,128)(2,1)S(1)} %get-tuple-element.24), channel_id=1, source_target_pairs={{0,2},{2,4},{4,6},{6,0},{1,3},{3,5},{5,7},{7,1},{8,10},{10,12},{12... | collective-permute-start | bytes 786440 | tf_op jit(solution)/shard_map/ppermute | solution.py:331
  72.7 0.0 collective-permute-done.4.g1
  72.7 2.2 %collective-permute-start.1 = (bf16[256,512]{1,0:T(8,128)(2,1)S(1)}, bf16[256,512]{1,0:T(8,128)(2,1)S(1)}, u32[]{:S(2)}, u32[]{:S(2)}) collective-permute-start(bf16[256,512]{1,0:T(8,128)(2,1)S(1)} %get-tuple-element.23), channel_id=1, source_target_pairs={{0,2},{2,4},{4,6},{6,0},{1,3},{3,5},{5,7},{7,1},{8,10},{10,12},{12... | collective-permute-start | bytes 786440 | tf_op jit(solution)/shard_map/ppermute | solution.py:333
  74.9 0.0 collective-permute-done.5.u1
  75.0 4.3 %collective-permute-start.2 = (bf16[256,512]{1,0:T(8,128)(2,1)S(1)}, bf16[256,512]{1,0:T(8,128)(2,1)S(1)}, u32[]{:S(2)}, u32[]{:S(2)}) collective-permute-start(bf16[256,512]{1,0:T(8,128)(2,1)S(1)} %get-tuple-element.24), channel_id=1, source_target_pairs={{0,6},{2,0},{4,2},{6,4},{1,7},{3,1},{5,3},{7,5},{8,14},{10,8},{12,... | collective-permute-start | bytes 786440 | tf_op jit(solution)/shard_map/ppermute | solution.py:334
  79.3 0.0 collective-permute-done.3.r1
  79.3 2.8 %collective-permute-start.7 = (bf16[256,512]{1,0:T(8,128)(2,1)S(1)}, bf16[256,512]{1,0:T(8,128)(2,1)S(1)}, u32[]{:S(2)}, u32[]{:S(2)}) collective-permute-start(bf16[256,512]{1,0:T(8,128)(2,1)S(1)} %collective-permute-done.3.r1), channel_id=1, source_target_pairs={{0,6},{2,0},{4,2},{6,4},{1,7},{3,1},{5,3},{7,5},{8,14},{10,8},{12,... | collective-permute-start | bytes 786440 | tf_op jit(solution)/shard_map/ppermute | solution.py:336
  82.1 0.0 collective-permute-done.l0
  82.1 2.5 %collective-permute-start.6 = (bf16[256,512]{1,0:T(8,128)(2,1)S(1)}, bf16[256,512]{1,0:T(8,128)(2,1)S(1)}, u32[]{:S(2)}, u32[]{:S(2)}) collective-permute-start(bf16[256,512]{1,0:T(8,128)(2,1)S(1)} %collective-permute-done.l0), channel_id=1, source_target_pairs={{0,2},{2,4},{4,6},{6,0},{1,3},{3,5},{5,7},{7,1},{8,10},{10,12},{12... | collective-permute-start | bytes 786440 | tf_op jit(solution)/shard_map/ppermute | solution.py:335
  84.6 0.0 collective-permute-done.1.l1
  84.6 0.0 collective-permute-done.2.r0
  84.6 3.6 %shard_map.75.near_ref = f32[4,512,256]{2,1,0:T(8,128)S(1)} custom-call(s32[1]{0:T(128)} %bitcast.quarter_ref, bf16[512,512]{1,0:T(8,128)(2,1)S(1)} %bitcast.26, bf16[256,512]{1,0:T(8,128)(2,1)S(1)} %collective-permute-done.l0, bf16[256,512]{1,0:T(8,128)(2,1)S(1)} %collective-permute-done.1.l1, bf16[256,512]{1,0:T(8,128)(2,1)S(1)} %collective-permute-done.2.r0, ...), custom_call_target="tpu_custom_call" | custom-call | flops 1610612736 | bytes 4194304 | tf_op jit(solution)/shard_map/pallas_call | solution.py:337
  88.2 0.0 collective-permute-done.8.w1
  88.2 0.0 collective-permute-done.7.bottom_ref
  88.2 2.2 %collective-permute-done.6.top_ref = bf16[256,512]{1,0:T(8,128)(2,1)S(1)} collective-permute-done((bf16[256,512]{1,0:T(8,128)(2,1)S(1)}, bf16[256,512]{1,0:T(8,128)(2,1)S(1)}, u32[]{:S(2)}, u32[]{:S(2)}) %collective-permute-start.6) | collective-permute-done | bytes 262176 | tf_op jit(solution)/shard_map/ppermute | solution.py:335
  90.4 2.5 %shard_map.76 = (bf16[2,512,256]{2,1,0:T(8,128)(2,1)S(1)}, bf16[2,256,512]{2,1,0:T(8,128)(2,1)S(1)}) custom-call(s32[1]{0:T(128)} %bitcast.quarter_ref, f32[4,512,256]{2,1,0:T(8,128)S(1)} %shard_map.75.near_ref, bf16[256,512]{1,0:T(8,128)(2,1)S(1)} %collective-permute-done.6.top_ref, bf16[256,512]{1,0:T(8,128)(2,1)S(1)} %collective-permute-done.7.bottom_ref, ...), custom_call_target="tpu_custom_call" | custom-call | flops 805306368 | bytes 2097152 | tf_op jit(solution)/shard_map/pallas_call | solution.py:345
  92.9 2.2 %collective-permute-start.10 = (bf16[256,512]{1,0:T(8,128)(2,1)S(1)}, bf16[256,512]{1,0:T(8,128)(2,1)S(1)}, u32[]{:S(2)}, u32[]{:S(2)}) collective-permute-start(bf16[256,512]{1,0:T(8,128)(2,1)S(1)} %get-tuple-element.21), channel_id=1, source_target_pairs={{0,6},{2,0},{4,2},{6,4},{1,7},{3,1},{5,3},{7,5},{8,14},{10,8},{12,... | collective-permute-start | bytes 786440 | tf_op jit(solution)/shard_map/ppermute | solution.py:361
  95.1 3.1 %collective-permute-start.9 = (bf16[256,512]{1,0:T(8,128)(2,1)S(1)}, bf16[256,512]{1,0:T(8,128)(2,1)S(1)}, u32[]{:S(2)}, u32[]{:S(2)}) collective-permute-start(bf16[256,512]{1,0:T(8,128)(2,1)S(1)} %get-tuple-element.22), channel_id=1, source_target_pairs={{0,2},{2,4},{4,6},{6,0},{1,3},{3,5},{5,7},{7,1},{8,10},{10,12},{12... | collective-permute-start | bytes 786440 | tf_op jit(solution)/shard_map/ppermute | solution.py:360
  98.2 0.5 shard_map.79
  98.7 1.9 %collective-permute-start.12 = (bf16[256,512]{1,0:T(8,128)(2,1)S(1)}, bf16[256,512]{1,0:T(8,128)(2,1)S(1)}, u32[]{:S(2)}, u32[]{:S(2)}) collective-permute-start(bf16[256,512]{1,0:T(8,128)(2,1)S(1)} %get-tuple-element.17), channel_id=1, source_target_pairs={{0,2},{2,4},{4,6},{6,0},{1,3},{3,5},{5,7},{7,1},{8,10},{10,12},{12... | collective-permute-start | bytes 786440 | tf_op jit(solution)/shard_map/ppermute | solution.py:366
  100.7 4.6 %collective-permute-start.13 = (bf16[256,512]{1,0:T(8,128)(2,1)S(1)}, bf16[256,512]{1,0:T(8,128)(2,1)S(1)}, u32[]{:S(2)}, u32[]{:S(2)}) collective-permute-start(bf16[256,512]{1,0:T(8,128)(2,1)S(1)} %get-tuple-element.18), channel_id=1, source_target_pairs={{0,6},{2,0},{4,2},{6,4},{1,7},{3,1},{5,3},{7,5},{8,14},{10,8},{12,... | collective-permute-start | bytes 786440 | tf_op jit(solution)/shard_map/ppermute | solution.py:367
  105.2 0.0 collective-permute-done.10.bottom_ref
  105.2 0.0 collective-permute-done.9.top_ref
  105.3 0.5 shard_map.78
  105.8 1.9 %collective-permute-start.11 = (bf16[256,512]{1,0:T(8,128)(2,1)S(1)}, bf16[256,512]{1,0:T(8,128)(2,1)S(1)}, u32[]{:S(2)}, u32[]{:S(2)}) collective-permute-start(bf16[256,512]{1,0:T(8,128)(2,1)S(1)} %get-tuple-element.16), channel_id=1, source_target_pairs={{0,2},{2,4},{4,6},{6,0},{1,3},{3,5},{5,7},{7,1},{8,10},{10,12},{12... | collective-permute-start | bytes 786440 | tf_op jit(solution)/shard_map/ppermute | solution.py:371
  107.7 4.6 %collective-permute-start.14 = (bf16[256,512]{1,0:T(8,128)(2,1)S(1)}, bf16[256,512]{1,0:T(8,128)(2,1)S(1)}, u32[]{:S(2)}, u32[]{:S(2)}) collective-permute-start(bf16[256,512]{1,0:T(8,128)(2,1)S(1)} %get-tuple-element.19), channel_id=1, source_target_pairs={{0,6},{2,0},{4,2},{6,4},{1,7},{3,1},{5,3},{7,5},{8,14},{10,8},{12,... | collective-permute-start | bytes 786440 | tf_op jit(solution)/shard_map/ppermute | solution.py:372
  112.3 0.5 shard_map.77.own_ref
  112.7 0.0 collective-permute-done.12.l1
  112.8 0.0 collective-permute-done.13.r0
  112.8 3.2 %collective-permute-done.11.l0 = bf16[256,512]{1,0:T(8,128)(2,1)S(1)} collective-permute-done((bf16[256,512]{1,0:T(8,128)(2,1)S(1)}, bf16[256,512]{1,0:T(8,128)(2,1)S(1)}, u32[]{:S(2)}, u32[]{:S(2)}) %collective-permute-start.11) | collective-permute-done | bytes 262176 | tf_op jit(solution)/shard_map/ppermute | solution.py:371
  116.0 0.9 collective-permute-done.14.r1
  116.9 0.2 shard_map.80
  117.0 0.0 copy-start.1
  117.0 34.3 %all_to_all.21 = bf16[64,8,512]{2,1,0:T(8,128)(2,1)S(1)} all-to-all(bf16[64,8,512]{2,1,0:T(8,128)(2,1)S(1)} %bitcast.27), channel_id=1, replica_groups=mesh['expert'=64,'x'=4,'c'=2] {'expert'}, dimensions={0} | all-to-all | bytes 1048576 | tf_op jit(solution)/shard_map/all_to_all | solution.py:385
  151.3 0.9 shard_map.81
  152.2 20.3 %all_to_all.22.parts_ref = bf16[8,48,512]{2,1,0:T(8,128)(2,1)S(1)} all-to-all(bf16[8,48,512]{2,1,0:T(8,128)(2,1)S(1)} %shard_map.81), channel_id=1, replica_groups=mesh['expert'=64,'x'=4,'c'=2] {'x','c'}, dimensions={0} | all-to-all | bytes 786432 | tf_op jit(solution)/shard_map/all_to_all | solution.py:394
  172.6 0.0 copy-done.1
  172.6 0.7 shard_map.82
  (2 shorter events, 0.1 us)
Async XLA Ops:
  0.0 43.4 %copy-start = (bf16[1,256,2048]{2,1,0:T(8,128)(2,1)S(1)}, bf16[1,256,2048]{2,1,0:T(8,128)(2,1)}, u32[]{:S(2)}) copy-start(bf16[1,256,2048]{2,1,0:T(8,128)(2,1)} %param.12) | copy-start | bytes 3145732
  24.2 43.2 %all-to-all-start.1 = ((bf16[64,8,512]{2,1,0:T(8,128)(2,1)}), bf16[64,8,512]{2,1,0:T(8,128)(2,1)S(1)}, u32[]{:S(2)}, u32[]{:S(2)}) async-start(bf16[64,8,512]{2,1,0:T(8,128)(2,1)} %bitcast.6), calls=%async_computation.1 | async-start | bytes 1048576 | tf_op jit(solution)/shard_map/all_to_all | solution.py:319
  38.2 34.5 %collective-permute-start.4 = (bf16[2048,256]{1,0:T(8,128)(2,1)}, bf16[2048,256]{1,0:T(8,128)(2,1)}, u32[]{:S(2)}, u32[]{:S(2)}) collective-permute-start(bf16[2048,256]{1,0:T(8,128)(2,1)} %bitcast.10.g0), channel_id=1, source_target_pairs={{0,1},{1,0},{2,3},{3,2},{4,5},{5,4},{6,7},{7,6},{8,9},{9,8},{10,11... | collective-permute-start | bytes 3145736 | tf_op jit(solution)/shard_map/ppermute | solution.py:286
  41.5 33.5 %collective-permute-start.5 = (bf16[2048,256]{1,0:T(8,128)(2,1)}, bf16[2048,256]{1,0:T(8,128)(2,1)}, u32[]{:S(2)}, u32[]{:S(2)}) collective-permute-start(bf16[2048,256]{1,0:T(8,128)(2,1)} %bitcast.11.u0), channel_id=1, source_target_pairs={{0,1},{1,0},{2,3},{3,2},{4,5},{5,4},{6,7},{7,6},{8,9},{9,8},{10,11... | collective-permute-start | bytes 3145736 | tf_op jit(solution)/shard_map/ppermute | solution.py:286
  43.4 44.8 %collective-permute-start.8 = (bf16[256,2048]{1,0:T(8,128)(2,1)S(1)}, bf16[256,2048]{1,0:T(8,128)(2,1)S(1)}, u32[]{:S(2)}, u32[]{:S(2)}) collective-permute-start(bf16[256,2048]{1,0:T(8,128)(2,1)S(1)} %bitcast.21), channel_id=1, source_target_pairs={{0,1},{1,0},{2,3},{3,2},{4,5},{5,4},{6,7},{7,6},{8,9},{9,8},{10,11... | collective-permute-start | bytes 3145736 | tf_op jit(solution)/shard_map/ppermute | solution.py:286
  67.4 11.8 %collective-permute-start.3 = (bf16[256,512]{1,0:T(8,128)(2,1)S(1)}, bf16[256,512]{1,0:T(8,128)(2,1)S(1)}, u32[]{:S(2)}, u32[]{:S(2)}) collective-permute-start(bf16[256,512]{1,0:T(8,128)(2,1)S(1)} %get-tuple-element.23), channel_id=1, source_target_pairs={{0,6},{2,0},{4,2},{6,4},{1,7},{3,1},{5,3},{7,5},{8,14},{10,8},{12,... | collective-permute-start | bytes 786440 | tf_op jit(solution)/shard_map/ppermute | solution.py:332
  70.2 11.8 %collective-permute-start = (bf16[256,512]{1,0:T(8,128)(2,1)S(1)}, bf16[256,512]{1,0:T(8,128)(2,1)S(1)}, u32[]{:S(2)}, u32[]{:S(2)}) collective-permute-start(bf16[256,512]{1,0:T(8,128)(2,1)S(1)} %get-tuple-element.24), channel_id=1, source_target_pairs={{0,2},{2,4},{4,6},{6,0},{1,3},{3,5},{5,7},{7,1},{8,10},{10,12},{12... | collective-permute-start | bytes 786440 | tf_op jit(solution)/shard_map/ppermute | solution.py:331
  72.7 11.8 %collective-permute-start.1 = (bf16[256,512]{1,0:T(8,128)(2,1)S(1)}, bf16[256,512]{1,0:T(8,128)(2,1)S(1)}, u32[]{:S(2)}, u32[]{:S(2)}) collective-permute-start(bf16[256,512]{1,0:T(8,128)(2,1)S(1)} %get-tuple-element.23), channel_id=1, source_target_pairs={{0,2},{2,4},{4,6},{6,0},{1,3},{3,5},{5,7},{7,1},{8,10},{10,12},{12... | collective-permute-start | bytes 786440 | tf_op jit(solution)/shard_map/ppermute | solution.py:333
  75.0 9.6 %collective-permute-start.2 = (bf16[256,512]{1,0:T(8,128)(2,1)S(1)}, bf16[256,512]{1,0:T(8,128)(2,1)S(1)}, u32[]{:S(2)}, u32[]{:S(2)}) collective-permute-start(bf16[256,512]{1,0:T(8,128)(2,1)S(1)} %get-tuple-element.24), channel_id=1, source_target_pairs={{0,6},{2,0},{4,2},{6,4},{1,7},{3,1},{5,3},{7,5},{8,14},{10,8},{12,... | collective-permute-start | bytes 786440 | tf_op jit(solution)/shard_map/ppermute | solution.py:334
  79.3 8.9 %collective-permute-start.7 = (bf16[256,512]{1,0:T(8,128)(2,1)S(1)}, bf16[256,512]{1,0:T(8,128)(2,1)S(1)}, u32[]{:S(2)}, u32[]{:S(2)}) collective-permute-start(bf16[256,512]{1,0:T(8,128)(2,1)S(1)} %collective-permute-done.3.r1), channel_id=1, source_target_pairs={{0,6},{2,0},{4,2},{6,4},{1,7},{3,1},{5,3},{7,5},{8,14},{10,8},{12,... | collective-permute-start | bytes 786440 | tf_op jit(solution)/shard_map/ppermute | solution.py:336
  82.1 8.3 %collective-permute-start.6 = (bf16[256,512]{1,0:T(8,128)(2,1)S(1)}, bf16[256,512]{1,0:T(8,128)(2,1)S(1)}, u32[]{:S(2)}, u32[]{:S(2)}) collective-permute-start(bf16[256,512]{1,0:T(8,128)(2,1)S(1)} %collective-permute-done.l0), channel_id=1, source_target_pairs={{0,2},{2,4},{4,6},{6,0},{1,3},{3,5},{5,7},{7,1},{8,10},{10,12},{12... | collective-permute-start | bytes 786440 | tf_op jit(solution)/shard_map/ppermute | solution.py:335
  92.9 12.3 %collective-permute-start.10 = (bf16[256,512]{1,0:T(8,128)(2,1)S(1)}, bf16[256,512]{1,0:T(8,128)(2,1)S(1)}, u32[]{:S(2)}, u32[]{:S(2)}) collective-permute-start(bf16[256,512]{1,0:T(8,128)(2,1)S(1)} %get-tuple-element.21), channel_id=1, source_target_pairs={{0,6},{2,0},{4,2},{6,4},{1,7},{3,1},{5,3},{7,5},{8,14},{10,8},{12,... | collective-permute-start | bytes 786440 | tf_op jit(solution)/shard_map/ppermute | solution.py:361
  95.1 10.1 %collective-permute-start.9 = (bf16[256,512]{1,0:T(8,128)(2,1)S(1)}, bf16[256,512]{1,0:T(8,128)(2,1)S(1)}, u32[]{:S(2)}, u32[]{:S(2)}) collective-permute-start(bf16[256,512]{1,0:T(8,128)(2,1)S(1)} %get-tuple-element.22), channel_id=1, source_target_pairs={{0,2},{2,4},{4,6},{6,0},{1,3},{3,5},{5,7},{7,1},{8,10},{10,12},{12... | collective-permute-start | bytes 786440 | tf_op jit(solution)/shard_map/ppermute | solution.py:360
  98.7 14.0 %collective-permute-start.12 = (bf16[256,512]{1,0:T(8,128)(2,1)S(1)}, bf16[256,512]{1,0:T(8,128)(2,1)S(1)}, u32[]{:S(2)}, u32[]{:S(2)}) collective-permute-start(bf16[256,512]{1,0:T(8,128)(2,1)S(1)} %get-tuple-element.17), channel_id=1, source_target_pairs={{0,2},{2,4},{4,6},{6,0},{1,3},{3,5},{5,7},{7,1},{8,10},{10,12},{12... | collective-permute-start | bytes 786440 | tf_op jit(solution)/shard_map/ppermute | solution.py:366
  100.7 12.1 %collective-permute-start.13 = (bf16[256,512]{1,0:T(8,128)(2,1)S(1)}, bf16[256,512]{1,0:T(8,128)(2,1)S(1)}, u32[]{:S(2)}, u32[]{:S(2)}) collective-permute-start(bf16[256,512]{1,0:T(8,128)(2,1)S(1)} %get-tuple-element.18), channel_id=1, source_target_pairs={{0,6},{2,0},{4,2},{6,4},{1,7},{3,1},{5,3},{7,5},{8,14},{10,8},{12,... | collective-permute-start | bytes 786440 | tf_op jit(solution)/shard_map/ppermute | solution.py:367
  105.8 10.3 %collective-permute-start.11 = (bf16[256,512]{1,0:T(8,128)(2,1)S(1)}, bf16[256,512]{1,0:T(8,128)(2,1)S(1)}, u32[]{:S(2)}, u32[]{:S(2)}) collective-permute-start(bf16[256,512]{1,0:T(8,128)(2,1)S(1)} %get-tuple-element.16), channel_id=1, source_target_pairs={{0,2},{2,4},{4,6},{6,0},{1,3},{3,5},{5,7},{7,1},{8,10},{10,12},{12... | collective-permute-start | bytes 786440 | tf_op jit(solution)/shard_map/ppermute | solution.py:371
  107.7 9.2 %collective-permute-start.14 = (bf16[256,512]{1,0:T(8,128)(2,1)S(1)}, bf16[256,512]{1,0:T(8,128)(2,1)S(1)}, u32[]{:S(2)}, u32[]{:S(2)}) collective-permute-start(bf16[256,512]{1,0:T(8,128)(2,1)S(1)} %get-tuple-element.19), channel_id=1, source_target_pairs={{0,6},{2,0},{4,2},{6,4},{1,7},{3,1},{5,3},{7,5},{8,14},{10,8},{12,... | collective-permute-start | bytes 786440 | tf_op jit(solution)/shard_map/ppermute | solution.py:372
  117.0 55.5 %copy-start.1 = (f32[1,3,2048]{2,0,1:T(1,128)S(1)}, f32[1,3,2048]{2,0,1:T(1,128)}, u32[]{:S(2)}) copy-start(f32[1,3,2048]{2,0,1:T(1,128)} %param.8) | copy-start | bytes 73732

commit v4 on v3

--- a/solution.py
+++ b/solution.py
@@ -133,21 +133,24 @@
     )
 
 
-def cut(quarter_ref, step, blocks, width):
-    return pl.ds(pl.multiple_of(lax.rem(quarter_ref[0] + step, blocks) * width, width), width)
-
-
-def near_kernel(quarter_ref, a_ref, l0, l1, r0, r1, g0, u0, g1, u1, out_ref, held, arrived):
-    rows, width = l0.shape
-    blocks = g0.shape[0] // width
+def cut(place_ref, index, width):
+    return pl.ds(pl.multiple_of(place_ref[index] * width, width), width)
+
+
+def copy_kernel(source_ref, after_ref, out_ref):
+    out_ref[...] = source_ref[...]
+
+
+def near_kernel(place_ref, a_ref, m_ref, g0, u0, g1, u1, out_ref, held, arrived):
+    width = a_ref.shape[1]
     copies = [
         [
             pltpu.make_async_copy(
-                weight_ref.at[cut(quarter_ref, step, blocks, width), :],
+                weight_ref.at[cut(place_ref, place, width), :],
                 held.at[index, place],
                 arrived.at[index, place],
             )
-            for place, step in enumerate((0, blocks - 1, 1))
+            for place in range(2)
         ]
         for index, weight_ref in enumerate((g0, u0, g1, u1))
     ]
@@ -157,88 +160,73 @@
     for index, group in enumerate(copies):
         for copy in group:
             copy.wait()
-        for part, (l_ref, r_ref) in enumerate(((l0, r0), (l1, r1))):
-            span = slice(part * rows, (part + 1) * rows)
-            out_ref[index, span, :] = (
-                jnp.dot(a_ref[span, :], held[index, 0], preferred_element_type=F32)
-                + jnp.dot(l_ref[...], held[index, 1], preferred_element_type=F32)
-                + jnp.dot(r_ref[...], held[index, 2], preferred_element_type=F32)
-            )
+        out_ref[index] = jnp.dot(
+            a_ref[...], held[index, 0], preferred_element_type=F32
+        ) + jnp.dot(m_ref[...], held[index, 1], preferred_element_type=F32)
 
 
 def far_kernel(
-    quarter_ref, near_ref, top_ref, bottom_ref, g0, u0, g1, u1, w0, w1,
+    place_ref, near_ref, n_ref, f_ref, g0, u0, g1, u1, w0, w1,
     hidden_ref, out_ref, held, held_down, arrived,
 ):
-    rows, width = top_ref.shape
-    blocks = g0.shape[0] // width
-    where = cut(quarter_ref, blocks // 2, blocks, width)
+    width = f_ref.shape[1]
+    where = cut(place_ref, 3, width)
     copies = [
-        pltpu.make_async_copy(weight_ref.at[where, :], held.at[index], arrived.at[index])
+        pltpu.make_async_copy(
+            weight_ref.at[cut(place_ref, 2 + part, width), :],
+            held.at[index, part],
+            arrived.at[2 * index + part],
+        )
         for index, weight_ref in enumerate((g0, u0, g1, u1))
+        for part in range(2)
     ] + [
-        pltpu.make_async_copy(down_ref.at[:, where], held_down.at[core], arrived.at[4 + core])
+        pltpu.make_async_copy(down_ref.at[:, where], held_down.at[core], arrived.at[8 + core])
         for core, down_ref in enumerate((w0, w1))
     ]
     for copy in copies:
         copy.start()
     for core in range(2):
-        copies[2 * core].wait()
-        copies[2 * core + 1].wait()
-        for part, ref in enumerate((top_ref, bottom_ref)):
-            span = slice(part * rows, (part + 1) * rows)
-            gate, up = [
-                near_ref[index, span, :]
-                + jnp.dot(ref[...], held[index], preferred_element_type=F32)
-                for index in (2 * core, 2 * core + 1)
-            ]
-            hidden_ref[core, span, :] = (gate * jax.nn.sigmoid(gate) * up).astype(BF16)
-    copies[4].wait()
-    copies[5].wait()
-    for part in range(2):
-        span = slice(part * rows, (part + 1) * rows)
-        out_ref[part] = (
-            jnp.dot(hidden_ref[0, span, :], held_down[0], preferred_element_type=F32)
-            + jnp.dot(hidden_ref[1, span, :], held_down[1], preferred_element_type=F32)
-        ).astype(BF16)
-
-
-def down(hidden_ref, span, w0, w1, where):
-    return jnp.dot(hidden_ref[0, span, :], w0[:, where], preferred_element_type=F32) + jnp.dot(
-        hidden_ref[1, span, :], w1[:, where], preferred_element_type=F32
-    )
-
-
-def direct_kernel(quarter_ref, hidden_ref, w0, w1, right_ref, left_ref):
-    rows, width = right_ref.shape
-    blocks = w0.shape[1] // width
-    right = down(hidden_ref, slice(rows, None), w0, w1, cut(quarter_ref, 1, blocks, width))
-    left = down(hidden_ref, slice(0, rows), w0, w1, cut(quarter_ref, blocks - 1, blocks, width))
-    right_ref[...] = right.astype(BF16)
-    left_ref[...] = left.astype(BF16)
-
-
-def relay_kernel(quarter_ref, hidden_ref, w0, w1, top_ref, bottom_ref, right_ref, left_ref):
-    rows, width = right_ref.shape
-    blocks = w0.shape[1] // width
-    right = down(hidden_ref, slice(0, rows), w0, w1, cut(quarter_ref, 1, blocks, width))
-    left = down(hidden_ref, slice(rows, None), w0, w1, cut(quarter_ref, blocks - 1, blocks, width))
-    right_ref[...] = (right + top_ref[...].astype(F32)).astype(BF16)
-    left_ref[...] = (left + bottom_ref[...].astype(F32)).astype(BF16)
-
-
-def own_kernel(quarter_ref, hidden_ref, w0, w1, out_ref):
-    width = out_ref.shape[1]
-    where = cut(quarter_ref, 0, w0.shape[1] // width, width)
-    out_ref[...] = down(hidden_ref, slice(None), w0, w1, where)
-
-
-def sum_kernel(own_ref, l0, l1, r0, r1, out_ref):
-    rows = l0.shape[0]
-    for part, (l_ref, r_ref) in enumerate(((l0, r0), (l1, r1))):
-        span = slice(part * rows, (part + 1) * rows)
-        total = own_ref[span, :] + l_ref[...].astype(F32) + r_ref[...].astype(F32)
-        out_ref[span, :] = total.astype(BF16)
+        for copy in copies[4 * core : 4 * core + 4]:
+            copy.wait()
+        gate, up = [
+            near_ref[index]
+            + jnp.dot(n_ref[...], held[index, 0], preferred_element_type=F32)
+            + jnp.dot(f_ref[...], held[index, 1], preferred_element_type=F32)
+            for index in (2 * core, 2 * core + 1)
+        ]
+        hidden_ref[core] = (gate * jax.nn.sigmoid(gate) * up).astype(BF16)
+    copies[8].wait()
+    copies[9].wait()
+    out_ref[...] = (
+        jnp.dot(hidden_ref[0], held_down[0], preferred_element_type=F32)
+        + jnp.dot(hidden_ref[1], held_down[1], preferred_element_type=F32)
+    ).astype(BF16)
+
+
+def down(hidden_ref, w0, w1, where):
+    return jnp.dot(hidden_ref[0], w0[:, where], preferred_element_type=F32) + jnp.dot(
+        hidden_ref[1], w1[:, where], preferred_element_type=F32
+    )
+
+
+def direct_kernel(place_ref, hidden_ref, w0, w1, out_ref):
+    where = cut(place_ref, 1, out_ref.shape[1])
+    out_ref[...] = down(hidden_ref, w0, w1, where).astype(BF16)
+
+
+def relay_kernel(place_ref, hidden_ref, w0, w1, came_ref, direct_ref, out_ref, again_ref):
+    where = cut(place_ref, 2, out_ref.shape[1])
+    again_ref[...] = direct_ref[...]
+    out_ref[...] = (down(hidden_ref, w0, w1, where) + came_ref[...].astype(F32)).astype(BF16)
+
+
+def own_kernel(place_ref, hidden_ref, w0, w1, out_ref):
+    out_ref[...] = down(hidden_ref, w0, w1, cut(place_ref, 0, out_ref.shape[1]))
+
+
+def sum_kernel(own_ref, major_ref, minor_ref, out_ref):
+    total = own_ref[...] + major_ref[...].astype(F32) + minor_ref[...].astype(F32)
+    out_ref[...] = total.astype(BF16)
 
 
 def combine_kernel(slots_ref, route_ref, out_ref):
@@ -320,68 +308,57 @@
         slots.reshape(experts, half, lanes), "expert", 0, 0, tiled=True
     ).reshape(count, lanes)
 
-    quarter = x.astype(jnp.int32).reshape(1)
-    onward = [(i, (i + 1) % chips) for i in range(chips)]
-    backward = [(i, (i - 1) % chips) for i in range(chips)]
+    major = [
+        (i * CORES + c, (i + 1 - 2 * c) % chips * CORES + c)
+        for i in range(chips)
+        for c in range(CORES)
+    ]
+    minor = [(target, source) for source, target in major]
+    step = (1 - 2 * core).astype(jnp.int32)
+    at = x.astype(jnp.int32) + chips
+    place = jnp.stack([at, at - step, at + step, at + 2]) % chips
     g0, u0, w0 = weights
     g1, u1, w1 = others
     cols = gate_weight.shape[2]
-    cut_rows = count // 2
-    upper, lower = arrived[:cut_rows], arrived[cut_rows:]
-    l0 = lax.ppermute(upper, "x", onward)
-    r1 = lax.ppermute(lower, "x", backward)
-    l1 = lax.ppermute(lower, "x", onward)
-    r0 = lax.ppermute(upper, "x", backward)
-    top = lax.ppermute(l0, "x", onward)
-    bottom = lax.ppermute(r1, "x", backward)
+    from_major = lax.ppermute(arrived, tensor, major)
+    from_far = lax.ppermute(from_major, tensor, major)
+    again = call(copy_kernel, jax.ShapeDtypeStruct(arrived.shape, BF16), 0, 4 * count * lanes, "vh")(arrived, from_major)
+    from_minor = lax.ppermute(again, tensor, minor)
     near = call(
         near_kernel,
         jax.ShapeDtypeStruct((4, count, cols), F32),
         24 * count * lanes * cols,
         16 * lanes * cols + 16 * count * cols,
-        "vvvvvvhhhh",
-        [pltpu.VMEM((4, 3, lanes, cols), BF16), pltpu.SemaphoreType.DMA((4, 3))],
-    )(quarter, arrived, l0, l1, r0, r1, g0, u0, g1, u1)
+        "vvvhhhh",
+        [pltpu.VMEM((4, 2, lanes, cols), BF16), pltpu.SemaphoreType.DMA((4, 2))],
+    )(place, arrived, from_major, g0, u0, g1, u1)
+    piece = jax.ShapeDtypeStruct((count, lanes), BF16)
     hidden, far = call(
         far_kernel,
-        (
-            jax.ShapeDtypeStruct((2, count, cols), BF16),
-            jax.ShapeDtypeStruct((2, cut_rows, lanes), BF16),
-        ),
+        (jax.ShapeDtypeStruct((2, count, cols), BF16), piece),
         12 * count * lanes * cols,
         16 * count * cols,
         "vvvvhhhhhh",
         [
-            pltpu.VMEM((4, lanes, cols), BF16),
+            pltpu.VMEM((4, 2, lanes, cols), BF16),
             pltpu.VMEM((2, cols, lanes), BF16),
-            pltpu.SemaphoreType.DMA((6,)),
+            pltpu.SemaphoreType.DMA((10,)),
         ],
-    )(quarter, near, top, bottom, g0, u0, g1, u1, w0, w1)
-    top = lax.ppermute(far[0], "x", onward)
-    bottom = lax.ppermute(far[1], "x", backward)
-    piece = jax.ShapeDtypeStruct((cut_rows, lanes), BF16)
-    direct_right, direct_left = call(
-        direct_kernel, (piece, piece), 4 * count * lanes * cols, 4 * count * lanes
-    )(quarter, hidden, w0, w1)
-    l1 = lax.ppermute(direct_right, "x", onward)
-    r0 = lax.ppermute(direct_left, "x", backward)
-    to_right, to_left = call(
-        relay_kernel, (piece, piece), 4 * count * lanes * cols, 4 * count * lanes
-    )(quarter, hidden, w0, w1, top, bottom)
-    l0 = lax.ppermute(to_right, "x", onward)
-    r1 = lax.ppermute(to_left, "x", backward)
-    own_sum = call(
-        own_kernel,
-        jax.ShapeDtypeStruct((count, lanes), F32),
-        4 * count * lanes * cols,
-        4 * count * lanes,
-    )(quarter, hidden, w0, w1)
-    summed = call(
-        sum_kernel,
-        jax.ShapeDtypeStruct((count, lanes), BF16),
-        2 * count * lanes,
-        10 * count * lanes,
-    )(own_sum, l0, l1, r0, r1)
+    )(place, near, from_minor, from_far, g0, u0, g1, u1, w0, w1)
+    work = (4 * count * lanes * cols, 4 * count * lanes)
+    came = lax.ppermute(far, tensor, major)
+    direct = call(direct_kernel, piece, *work)(place, hidden, w0, w1)
+    relayed, direct = call(relay_kernel, (piece, piece), *work)(
+        place, hidden, w0, w1, came, direct
+    )
+    from_major = lax.ppermute(relayed, tensor, major)
+    from_minor = lax.ppermute(direct, tensor, minor)
+    own_sum = call(own_kernel, jax.ShapeDtypeStruct((count, lanes), F32), *work)(
+        place, hidden, w0, w1
+    )
+    summed = call(sum_kernel, piece, 2 * count * lanes, 8 * count * lanes)(
+        own_sum, from_major, from_minor
+    )
     produced = lax.all_to_all(
         summed.reshape(images, half, lanes), "expert", 0, 0, tiled=True
     ).reshape(count, lanes)

time: 174 us -> 187 us (1.075)
  waiting for transfers between devices: 27.9 us -> 47.8 us
  starting transfers between devices: 56.9 us -> 47 us
  Pallas kernels: 13.9 us -> 17.2 us
    ppermute x12 -> x6, waiting for transfers between devices: 6.35 us -> 23.8 us  [the longest x1 8.78 us: body(): from_minor = lax.ppermute(direct, tensor, minor)]
    ppermute x12 -> x6, starting transfers between devices: 35.3 us -> 21.6 us  [the longest x1 5.43 us: body(): came = lax.ppermute(far, tensor, major)]
    all_to_all x1, blocking collectives: 20.3 us -> 11.8 us  [body(): mixed = lax.all_to_all(mixed, tensor, 0, 0, tiled=True)]
    all_to_all x1, blocking collectives: 34.3 us -> 42.5 us  [body(): lax.all_to_all(summed.reshape(images, half, lanes), 'expert', 0, 0, tiled...]
    ppermute x3, starting transfers between devices: 7.57 us -> 11.4 us  [body(): others = [lax.ppermute(w, 'c', swap) for w in weights]]
    pallas_call x5 -> x6, Pallas kernels: 4.09 us -> 7.01 us  [the longest x1 4.46 us: body(): call(far_kernel, (jax.ShapeDtypeStruct((2, count, cols), BF16), piece), 1...]
    all_to_all x1, waiting for transfers between devices: 21.6 us -> 24 us  [body(): lax.all_to_all(slots.reshape(experts, half, lanes), 'expert', 0, 0, tiled...]
  transfers between devices with their start and end apart: 16 -> 10, of which waited for: 4 -> 7; matrix products, arithmetic and copies ran while one was open for 0% -> 0% of each run, Pallas kernels for 3% -> 3%
where the time goes in v4:
time: 187 us; the launch traced here: 186 us
  blocking collectives  73.9 us (40%)
  waiting for transfers between devices  47.8 us (26%)
  starting transfers between devices  47 us (25%)
  Pallas kernels  17.2 us (9%)
    all_to_all x1, blocking collectives, body(): lax.all_to_all(summed.reshape(images, half, lanes), 'expert', 0, 0, tiled...  42.5 us
    all_to_all x1, waiting for transfers between devices, body(): lax.all_to_all(slots.reshape(experts, half, lanes), 'expert', 0, 0, tiled...  24 us
    all_to_all x1, blocking collectives, body(): packet = lax.all_to_all(packet, tensor, 0, 0, tiled=True)  19.6 us
    all_to_all x1, starting transfers between devices, body(): lax.all_to_all(slots.reshape(experts, half, lanes), 'expert', 0, 0, tiled...  14 us
    all_to_all x1, blocking collectives, body(): mixed = lax.all_to_all(mixed, tensor, 0, 0, tiled=True)  11.8 us
    ppermute x3, starting transfers between devices, body(): others = [lax.ppermute(w, 'c', swap) for w in weights]  11.4 us
    ppermute x1, waiting for transfers between devices, body(): from_minor = lax.ppermute(direct, tensor, minor)  8.78 us
    ppermute x1, waiting for transfers between devices, body(): came = lax.ppermute(far, tensor, major)  5.56 us
  transfers between devices with their start and end apart: 10, of which 7 were waited for; matrix products, arithmetic and copies ran while one was open for 0% of the time, Pallas kernels for 3%

profile of v4, /device:TPU:1, one launch (start us, length us, event | category | flops | bytes accessed | tf_op | source)
XLA Modules:
  0.0 186.1 jit_solution(2393656497186214247)
XLA Ops:
  0.0 0.0 copy-start
  0.0 3.1 %shard_map.73 = bf16[8,64,512]{2,1,0:T(8,128)(2,1)} custom-call(s32[1]{0:T(128)} %bitcast.5.member_ref, s32[2,48]{1,0:T(2,128)} %bitcast.29, bf16[48,2048]{1,0:T(8,128)(2,1)} %tokens_in.1, f32[3,1,2048]{2,1,0:T(1,128)} %bitcast.26, bf16[64,2048]{1,0:T(8,128)(2,1)} %bitcast.28), custom_call_target="tpu_custom_call" | custom-call | flops 12582912 | bytes 393216 | tf_op jit(solution)/shard_map/pallas_call | solution.py:277
  3.1 19.6 %all_to_all.20.packet_ref = bf16[8,64,512]{2,1,0:T(8,128)(2,1)S(1)} all-to-all(bf16[8,64,512]{2,1,0:T(8,128)(2,1)} %shard_map.73), channel_id=1, replica_groups=mesh['expert'=64,'x'=4,'c'=2] {'x','c'}, dimensions={0} | all-to-all | bytes 1048576 | tf_op jit(solution)/shard_map/all_to_all | solution.py:297
  22.8 1.4 shard_map.74
  24.2 14.0 %all-to-all-start.1 = ((bf16[64,8,512]{2,1,0:T(8,128)(2,1)}), bf16[64,8,512]{2,1,0:T(8,128)(2,1)S(1)}, u32[]{:S(2)}, u32[]{:S(2)}) async-start(bf16[64,8,512]{2,1,0:T(8,128)(2,1)} %bitcast.9), calls=%async_computation.1 | async-start | bytes 1048576 | tf_op jit(solution)/shard_map/all_to_all | solution.py:307
  38.2 3.2 %collective-permute-start.1 = (bf16[2048,256]{1,0:T(8,128)(2,1)}, bf16[2048,256]{1,0:T(8,128)(2,1)}, u32[]{:S(2)}, u32[]{:S(2)}) collective-permute-start(bf16[2048,256]{1,0:T(8,128)(2,1)} %bitcast.11.g0), channel_id=1, source_target_pairs={{0,1},{1,0},{2,3},{3,2},{4,5},{5,4},{6,7},{7,6},{8,9},{9,8},{10,11... | collective-permute-start | bytes 3145736 | tf_op jit(solution)/shard_map/ppermute | solution.py:274
  41.5 1.9 %collective-permute-start.2 = (bf16[2048,256]{1,0:T(8,128)(2,1)}, bf16[2048,256]{1,0:T(8,128)(2,1)}, u32[]{:S(2)}, u32[]{:S(2)}) collective-permute-start(bf16[2048,256]{1,0:T(8,128)(2,1)} %bitcast.12.u0), channel_id=1, source_target_pairs={{0,1},{1,0},{2,3},{3,2},{4,5},{5,4},{6,7},{7,6},{8,9},{9,8},{10,11... | collective-permute-start | bytes 3145736 | tf_op jit(solution)/shard_map/ppermute | solution.py:274
  43.4 24.0 %all-to-all-done.1 = bf16[64,8,512]{2,1,0:T(8,128)(2,1)S(1)} async-done(((bf16[64,8,512]{2,1,0:T(8,128)(2,1)}), bf16[64,8,512]{2,1,0:T(8,128)(2,1)S(1)}, u32[]{:S(2)}, u32[]{:S(2)}) %all-to-all-start.1) | async-done | bytes 524320 | tf_op jit(solution)/shard_map/all_to_all | solution.py:307
  67.4 2.8 %collective-permute-start = (bf16[512,512]{1,0:T(8,128)(2,1)S(1)}, bf16[512,512]{1,0:T(8,128)(2,1)S(1)}, u32[]{:S(2)}, u32[]{:S(2)}) collective-permute-start(bf16[512,512]{1,0:T(8,128)(2,1)S(1)} %bitcast.21), channel_id=1, source_target_pairs={{0,2},{1,7},{2,4},{3,1},{4,6},{5,3},{6,0},{7,5},{8,10},{9,15},{10,... | collective-permute-start | bytes 1572872 | tf_op jit(solution)/shard_map/ppermute | solution.py:323
  70.2 0.0 copy-done
  70.2 6.2 %collective-permute-start.5 = (bf16[256,2048]{1,0:T(8,128)(2,1)S(1)}, bf16[256,2048]{1,0:T(8,128)(2,1)S(1)}, u32[]{:S(2)}, u32[]{:S(2)}) collective-permute-start(bf16[256,2048]{1,0:T(8,128)(2,1)S(1)} %bitcast.16), channel_id=1, source_target_pairs={{0,1},{1,0},{2,3},{3,2},{4,5},{5,4},{6,7},{7,6},{8,9},{9,8},{10,11... | collective-permute-start | bytes 3145736 | tf_op jit(solution)/shard_map/ppermute | solution.py:274
  76.4 0.9 collective-permute-done.m_ref.after_ref
  77.3 0.8 shard_map.76
  78.1 2.5 %collective-permute-start.3 = (bf16[512,512]{1,0:T(8,128)(2,1)}, bf16[512,512]{1,0:T(8,128)(2,1)}, u32[]{:S(2)}, u32[]{:S(2)}) collective-permute-start(bf16[512,512]{1,0:T(8,128)(2,1)} %shard_map.76), channel_id=1, source_target_pairs={{2,0},{7,1},{4,2},{1,3},{6,4},{3,5},{0,6},{5,7},{10,8},{15,9},{12,... | collective-permute-start | bytes 1572872 | tf_op jit(solution)/shard_map/ppermute | solution.py:326
  80.6 4.0 %collective-permute-start.4 = (bf16[512,512]{1,0:T(8,128)(2,1)S(1)}, bf16[512,512]{1,0:T(8,128)(2,1)}, u32[]{:S(2)}, u32[]{:S(2)}) collective-permute-start(bf16[512,512]{1,0:T(8,128)(2,1)S(1)} %collective-permute-done.m_ref.after_ref), channel_id=1, source_target_pairs={{0,2},{1,7},{2,4},{3,1},{4,6},{5,3},{6,0},{7,5},{8,10},{9,15},{10,... | collective-permute-start | bytes 1572872 | tf_op jit(solution)/shard_map/ppermute | solution.py:324
  84.6 0.1 and_select_fusion.place_ref
  84.7 0.0 collective-permute-done.1.g1
  84.7 0.0 collective-permute-done.2.u1
  84.7 3.9 %shard_map.75.near_ref = f32[4,512,256]{2,1,0:T(8,128)S(1)} custom-call(s32[4]{0:T(128)S(1)} %and_select_fusion.place_ref, bf16[512,512]{1,0:T(8,128)(2,1)S(1)} %bitcast.23, bf16[512,512]{1,0:T(8,128)(2,1)S(1)} %collective-permute-done.m_ref.after_ref, bf16[2048,256]{1,0:T(8,128)(2,1)} %bitcast.11.g0, bf16[2048,256]{1,0:T(8,128)(2,1)} %bitcast.12.u0, ...), custom_call_target="tpu_custom_call" | custom-call | flops 1610612736 | bytes 4194304 | tf_op jit(solution)/shard_map/pallas_call | solution.py:327
  88.7 0.0 collective-permute-done.5.w1
  88.7 0.9 collective-permute-done.3.n_ref
  89.6 3.9 %collective-permute-done.4.f_ref = bf16[512,512]{1,0:T(8,128)(2,1)} collective-permute-done((bf16[512,512]{1,0:T(8,128)(2,1)S(1)}, bf16[512,512]{1,0:T(8,128)(2,1)}, u32[]{:S(2)}, u32[]{:S(2)}) %collective-permute-start.4) | collective-permute-done | bytes 524320 | tf_op jit(solution)/shard_map/ppermute | solution.py:324
  93.5 4.5 %shard_map.77 = (bf16[2,512,256]{2,1,0:T(8,128)(2,1)S(1)}, bf16[512,512]{1,0:T(8,128)(2,1)S(1)}) custom-call(s32[4]{0:T(128)S(1)} %and_select_fusion.place_ref, f32[4,512,256]{2,1,0:T(8,128)S(1)} %shard_map.75.near_ref, bf16[512,512]{1,0:T(8,128)(2,1)} %collective-permute-done.3.n_ref, bf16[512,512]{1,0:T(8,128)(2,1)} %collective-permute-done.4.f_ref, ...), custom_call_target="tpu_custom_call" | custom-call | flops 805306368 | bytes 2097152 | tf_op jit(solution)/shard_map/pallas_call | solution.py:336
  98.0 5.4 %collective-permute-start.6 = (bf16[512,512]{1,0:T(8,128)(2,1)S(1)}, bf16[512,512]{1,0:T(8,128)(2,1)S(1)}, u32[]{:S(2)}, u32[]{:S(2)}) collective-permute-start(bf16[512,512]{1,0:T(8,128)(2,1)S(1)} %get-tuple-element.13), channel_id=1, source_target_pairs={{0,2},{1,7},{2,4},{3,1},{4,6},{5,3},{6,0},{7,5},{8,10},{9,15},{10,... | collective-permute-start | bytes 1572872 | tf_op jit(solution)/shard_map/ppermute | solution.py:349
  103.4 0.5 shard_map.79.direct_ref
  103.9 5.6 %collective-permute-done.6.came_ref = bf16[512,512]{1,0:T(8,128)(2,1)S(1)} collective-permute-done((bf16[512,512]{1,0:T(8,128)(2,1)S(1)}, bf16[512,512]{1,0:T(8,128)(2,1)S(1)}, u32[]{:S(2)}, u32[]{:S(2)}) %collective-permute-start.6) | collective-permute-done | bytes 524320 | tf_op jit(solution)/shard_map/ppermute | solution.py:349
  109.5 0.5 shard_map.80
  110.0 5.0 %collective-permute-start.7 = (bf16[512,512]{1,0:T(8,128)(2,1)S(1)}, bf16[512,512]{1,0:T(8,128)(2,1)S(1)}, u32[]{:S(2)}, u32[]{:S(2)}) collective-permute-start(bf16[512,512]{1,0:T(8,128)(2,1)S(1)} %get-tuple-element.14), channel_id=1, source_target_pairs={{0,2},{1,7},{2,4},{3,1},{4,6},{5,3},{6,0},{7,5},{8,10},{9,15},{10,... | collective-permute-start | bytes 1572872 | tf_op jit(solution)/shard_map/ppermute | solution.py:354
  115.1 1.9 %collective-permute-start.8 = (bf16[512,512]{1,0:T(8,128)(2,1)S(1)}, bf16[512,512]{1,0:T(8,128)(2,1)S(1)}, u32[]{:S(2)}, u32[]{:S(2)}) collective-permute-start(bf16[512,512]{1,0:T(8,128)(2,1)S(1)} %get-tuple-element.15), channel_id=1, source_target_pairs={{2,0},{7,1},{4,2},{1,3},{6,4},{3,5},{0,6},{5,7},{10,8},{15,9},{12,... | collective-permute-start | bytes 1572872 | tf_op jit(solution)/shard_map/ppermute | solution.py:355
  117.0 0.5 shard_map.78.own_ref
  117.5 3.7 %collective-permute-done.7.major_ref = bf16[512,512]{1,0:T(8,128)(2,1)S(1)} collective-permute-done((bf16[512,512]{1,0:T(8,128)(2,1)S(1)}, bf16[512,512]{1,0:T(8,128)(2,1)S(1)}, u32[]{:S(2)}, u32[]{:S(2)}) %collective-permute-start.7) | collective-permute-done | bytes 524320 | tf_op jit(solution)/shard_map/ppermute | solution.py:354
  121.2 8.8 %collective-permute-done.8.minor_ref = bf16[512,512]{1,0:T(8,128)(2,1)S(1)} collective-permute-done((bf16[512,512]{1,0:T(8,128)(2,1)S(1)}, bf16[512,512]{1,0:T(8,128)(2,1)S(1)}, u32[]{:S(2)}, u32[]{:S(2)}) %collective-permute-start.8) | collective-permute-done | bytes 524320 | tf_op jit(solution)/shard_map/ppermute | solution.py:355
  130.0 0.2 shard_map.81
  130.1 0.0 copy-start.1
  130.1 42.5 %all_to_all.21 = bf16[64,8,512]{2,1,0:T(8,128)(2,1)S(1)} all-to-all(bf16[64,8,512]{2,1,0:T(8,128)(2,1)S(1)} %bitcast.24), channel_id=1, replica_groups=mesh['expert'=64,'x'=4,'c'=2] {'expert'}, dimensions={0} | all-to-all | bytes 1048576 | tf_op jit(solution)/shard_map/all_to_all | solution.py:362
  172.6 0.9 shard_map.82
  173.5 11.8 %all_to_all.22.parts_ref = bf16[8,48,512]{2,1,0:T(8,128)(2,1)S(1)} all-to-all(bf16[8,48,512]{2,1,0:T(8,128)(2,1)S(1)} %shard_map.82), channel_id=1, replica_groups=mesh['expert'=64,'x'=4,'c'=2] {'x','c'}, dimensions={0} | all-to-all | bytes 786432 | tf_op jit(solution)/shard_map/all_to_all | solution.py:371
  185.3 0.0 copy-done.1
  185.4 0.7 shard_map.83
Async XLA Ops:
  0.0 70.2 %copy-start = (bf16[1,256,2048]{2,1,0:T(8,128)(2,1)S(1)}, bf16[1,256,2048]{2,1,0:T(8,128)(2,1)}, u32[]{:S(2)}) copy-start(bf16[1,256,2048]{2,1,0:T(8,128)(2,1)} %param.12) | copy-start | bytes 3145732
  24.2 43.2 %all-to-all-start.1 = ((bf16[64,8,512]{2,1,0:T(8,128)(2,1)}), bf16[64,8,512]{2,1,0:T(8,128)(2,1)S(1)}, u32[]{:S(2)}, u32[]{:S(2)}) async-start(bf16[64,8,512]{2,1,0:T(8,128)(2,1)} %bitcast.9), calls=%async_computation.1 | async-start | bytes 1048576 | tf_op jit(solution)/shard_map/all_to_all | solution.py:307
  38.2 46.5 %collective-permute-start.1 = (bf16[2048,256]{1,0:T(8,128)(2,1)}, bf16[2048,256]{1,0:T(8,128)(2,1)}, u32[]{:S(2)}, u32[]{:S(2)}) collective-permute-start(bf16[2048,256]{1,0:T(8,128)(2,1)} %bitcast.11.g0), channel_id=1, source_target_pairs={{0,1},{1,0},{2,3},{3,2},{4,5},{5,4},{6,7},{7,6},{8,9},{9,8},{10,11... | collective-permute-start | bytes 3145736 | tf_op jit(solution)/shard_map/ppermute | solution.py:274
  41.5 43.3 %collective-permute-start.2 = (bf16[2048,256]{1,0:T(8,128)(2,1)}, bf16[2048,256]{1,0:T(8,128)(2,1)}, u32[]{:S(2)}, u32[]{:S(2)}) collective-permute-start(bf16[2048,256]{1,0:T(8,128)(2,1)} %bitcast.12.u0), channel_id=1, source_target_pairs={{0,1},{1,0},{2,3},{3,2},{4,5},{5,4},{6,7},{7,6},{8,9},{9,8},{10,11... | collective-permute-start | bytes 3145736 | tf_op jit(solution)/shard_map/ppermute | solution.py:274
  67.4 9.9 %collective-permute-start = (bf16[512,512]{1,0:T(8,128)(2,1)S(1)}, bf16[512,512]{1,0:T(8,128)(2,1)S(1)}, u32[]{:S(2)}, u32[]{:S(2)}) collective-permute-start(bf16[512,512]{1,0:T(8,128)(2,1)S(1)} %bitcast.21), channel_id=1, source_target_pairs={{0,2},{1,7},{2,4},{3,1},{4,6},{5,3},{6,0},{7,5},{8,10},{9,15},{10,... | collective-permute-start | bytes 1572872 | tf_op jit(solution)/shard_map/ppermute | solution.py:323
  70.2 18.5 %collective-permute-start.5 = (bf16[256,2048]{1,0:T(8,128)(2,1)S(1)}, bf16[256,2048]{1,0:T(8,128)(2,1)S(1)}, u32[]{:S(2)}, u32[]{:S(2)}) collective-permute-start(bf16[256,2048]{1,0:T(8,128)(2,1)S(1)} %bitcast.16), channel_id=1, source_target_pairs={{0,1},{1,0},{2,3},{3,2},{4,5},{5,4},{6,7},{7,6},{8,9},{9,8},{10,11... | collective-permute-start | bytes 3145736 | tf_op jit(solution)/shard_map/ppermute | solution.py:274
  78.1 11.4 %collective-permute-start.3 = (bf16[512,512]{1,0:T(8,128)(2,1)}, bf16[512,512]{1,0:T(8,128)(2,1)}, u32[]{:S(2)}, u32[]{:S(2)}) collective-permute-start(bf16[512,512]{1,0:T(8,128)(2,1)} %shard_map.76), channel_id=1, source_target_pairs={{2,0},{7,1},{4,2},{1,3},{6,4},{3,5},{0,6},{5,7},{10,8},{15,9},{12,... | collective-permute-start | bytes 1572872 | tf_op jit(solution)/shard_map/ppermute | solution.py:326
  80.6 12.9 %collective-permute-start.4 = (bf16[512,512]{1,0:T(8,128)(2,1)S(1)}, bf16[512,512]{1,0:T(8,128)(2,1)}, u32[]{:S(2)}, u32[]{:S(2)}) collective-permute-start(bf16[512,512]{1,0:T(8,128)(2,1)S(1)} %collective-permute-done.m_ref.after_ref), channel_id=1, source_target_pairs={{0,2},{1,7},{2,4},{3,1},{4,6},{5,3},{6,0},{7,5},{8,10},{9,15},{10,... | collective-permute-start | bytes 1572872 | tf_op jit(solution)/shard_map/ppermute | solution.py:324
  98.0 11.5 %collective-permute-start.6 = (bf16[512,512]{1,0:T(8,128)(2,1)S(1)}, bf16[512,512]{1,0:T(8,128)(2,1)S(1)}, u32[]{:S(2)}, u32[]{:S(2)}) collective-permute-start(bf16[512,512]{1,0:T(8,128)(2,1)S(1)} %get-tuple-element.13), channel_id=1, source_target_pairs={{0,2},{1,7},{2,4},{3,1},{4,6},{5,3},{6,0},{7,5},{8,10},{9,15},{10,... | collective-permute-start | bytes 1572872 | tf_op jit(solution)/shard_map/ppermute | solution.py:349
  110.0 11.1 %collective-permute-start.7 = (bf16[512,512]{1,0:T(8,128)(2,1)S(1)}, bf16[512,512]{1,0:T(8,128)(2,1)S(1)}, u32[]{:S(2)}, u32[]{:S(2)}) collective-permute-start(bf16[512,512]{1,0:T(8,128)(2,1)S(1)} %get-tuple-element.14), channel_id=1, source_target_pairs={{0,2},{1,7},{2,4},{3,1},{4,6},{5,3},{6,0},{7,5},{8,10},{9,15},{10,... | collective-permute-start | bytes 1572872 | tf_op jit(solution)/shard_map/ppermute | solution.py:354
  115.1 14.9 %collective-permute-start.8 = (bf16[512,512]{1,0:T(8,128)(2,1)S(1)}, bf16[512,512]{1,0:T(8,128)(2,1)S(1)}, u32[]{:S(2)}, u32[]{:S(2)}) collective-permute-start(bf16[512,512]{1,0:T(8,128)(2,1)S(1)} %get-tuple-element.15), channel_id=1, source_target_pairs={{2,0},{7,1},{4,2},{1,3},{6,4},{3,5},{0,6},{5,7},{10,8},{15,9},{12,... | collective-permute-start | bytes 1572872 | tf_op jit(solution)/shard_map/ppermute | solution.py:355
  130.1 55.2 %copy-start.1 = (f32[1,3,2048]{2,0,1:T(1,128)S(1)}, f32[1,3,2048]{2,0,1:T(1,128)}, u32[]{:S(2)}) copy-start(f32[1,3,2048]{2,0,1:T(1,128)} %param.8) | copy-start | bytes 73732

commit v5 on v3

--- a/solution.py
+++ b/solution.py
@@ -19,7 +19,7 @@
 
 
 def call(kernel, out_shape, flops, nbytes, spaces=None, scratch=(), limit=VMEM_LIMIT):
-    kinds = {"v": pltpu.VMEM, "h": pltpu.HBM}
+    kinds = {"v": pltpu.VMEM, "h": pltpu.HBM, "s": pltpu.SMEM}
     specs = {}
     if spaces is not None:
         specs = {"in_specs": [pl.BlockSpec(memory_space=kinds[kind]) for kind in spaces]}
@@ -39,13 +39,18 @@
 
 
 def modulate_kernel(
-    member_ref, ids_ref, tokens_in, modulation_in, router_in, packet_ref,
-    tokens_ref, modulation_ref, router_ref, arrived,
+    member_ref, ids_in, tokens_in, modulation_in, router_in, packet_ref,
+    tokens_ref, modulation_ref, router_ref, ids_ref, arrived,
 ):
     copies = [
         pltpu.make_async_copy(source, target, arrived.at[index])
         for index, (source, target) in enumerate(
-            ((tokens_in, tokens_ref), (modulation_in, modulation_ref), (router_in, router_ref))
+            (
+                (tokens_in, tokens_ref),
+                (modulation_in, modulation_ref),
+                (router_in, router_ref),
+                (ids_in, ids_ref),
+            )
         )
     ]
     for copy in copies:
@@ -60,6 +65,7 @@
     normed = centred * lax.rsqrt(spread + EPS)
     copies[1].wait()
     copies[2].wait()
+    copies[3].wait()
     modulated = (normed * (1.0 + modulation_ref[1]) + modulation_ref[0]).astype(BF16)
     logits = lax.dot_general(
         router_ref[...], modulated, (((1,), (1,)), ((), ())), preferred_element_type=F32
@@ -291,12 +297,13 @@
         jax.ShapeDtypeStruct((members, PAD, lanes), BF16),
         2 * own * width * experts,
         4 * own * width,
-        "vvhhh",
+        "shhhh",
         [
             pltpu.VMEM(tokens.shape, BF16),
             pltpu.VMEM(shift_scale_gate.shape, F32),
             pltpu.VMEM((experts, width), BF16),
-            pltpu.SemaphoreType.DMA((3,)),
+            pltpu.VMEM((2, own), jnp.int32),
+            pltpu.SemaphoreType.DMA((4,)),
         ],
         FIRST_LIMIT,
     )(

time: 174 us -> 173 us (level)
  no operation moved by 1% of the time
where the time goes in v5:
time: 173 us
  blocking collectives  74.3 us (43%)
  starting transfers between devices  56.9 us (33%)
  waiting for transfers between devices  27.9 us (16%)
  Pallas kernels  13.2 us (8%)
    all_to_all x1, blocking collectives, body(): lax.all_to_all(summed.reshape(images, half, lanes), 'expert', 0, 0, tiled...  34.3 us
    all_to_all x1, waiting for transfers between devices, body(): lax.all_to_all(slots.reshape(experts, half, lanes), 'expert', 0, 0, tiled...  21.6 us
    all_to_all x1, blocking collectives, body(): mixed = lax.all_to_all(mixed, tensor, 0, 0, tiled=True)  20.4 us
    all_to_all x1, blocking collectives, body(): packet = lax.all_to_all(packet, tensor, 0, 0, tiled=True)  19.6 us
    all_to_all x1, starting transfers between devices, body(): lax.all_to_all(slots.reshape(experts, half, lanes), 'expert', 0, 0, tiled...  14 us
    ppermute x3, starting transfers between devices, body(): others = [lax.ppermute(w, 'c', swap) for w in weights]  7.56 us
    ppermute x1, starting transfers between devices, body(): r1 = lax.ppermute(to_left, 'x', backward)  4.57 us
    ppermute x1, starting transfers between devices, body(): r0 = lax.ppermute(direct_left, 'x', backward)  4.57 us
  transfers between devices with their start and end apart: 16, of which 4 were waited for; matrix products, arithmetic and copies ran while one was open for 0% of the time, Pallas kernels for 3%

profile of v5, /device:TPU:1, one launch (start us, length us, event | category | flops | bytes accessed | tf_op | source)
XLA Modules:
  0.0 172.7 jit_solution(14261355170362378888)
XLA Ops:
  0.0 0.0 copy-start
  0.0 2.5 %shard_map.73 = bf16[8,64,512]{2,1,0:T(8,128)(2,1)} custom-call(s32[1]{0:T(128)} %bitcast.2.member_ref, s32[2,48]{1,0:T(2,128)} %bitcast.32, bf16[48,2048]{1,0:T(8,128)(2,1)} %tokens_in.1, f32[3,1,2048]{2,1,0:T(1,128)} %bitcast.29, bf16[64,2048]{1,0:T(8,128)(2,1)} %bitcast.31), custom_call_target="tpu_custom_call" | custom-call | flops 12582912 | bytes 393216 | tf_op jit(solution)/shard_map/pallas_call | solution.py:295
  2.5 19.6 %all_to_all.20.packet_ref = bf16[8,64,512]{2,1,0:T(8,128)(2,1)S(1)} all-to-all(bf16[8,64,512]{2,1,0:T(8,128)(2,1)} %shard_map.73), channel_id=1, replica_groups=mesh['expert'=64,'x'=4,'c'=2] {'x','c'}, dimensions={0} | all-to-all | bytes 1048576 | tf_op jit(solution)/shard_map/all_to_all | solution.py:316
  22.1 1.4 shard_map.74
  23.6 14.0 %all-to-all-start.1 = ((bf16[64,8,512]{2,1,0:T(8,128)(2,1)}), bf16[64,8,512]{2,1,0:T(8,128)(2,1)S(1)}, u32[]{:S(2)}, u32[]{:S(2)}) async-start(bf16[64,8,512]{2,1,0:T(8,128)(2,1)} %bitcast.6), calls=%async_computation.1 | async-start | bytes 1048576 | tf_op jit(solution)/shard_map/all_to_all | solution.py:326
  37.6 3.2 %collective-permute-start.4 = (bf16[2048,256]{1,0:T(8,128)(2,1)}, bf16[2048,256]{1,0:T(8,128)(2,1)}, u32[]{:S(2)}, u32[]{:S(2)}) collective-permute-start(bf16[2048,256]{1,0:T(8,128)(2,1)} %bitcast.10.g0), channel_id=1, source_target_pairs={{0,1},{1,0},{2,3},{3,2},{4,5},{5,4},{6,7},{7,6},{8,9},{9,8},{10,11... | collective-permute-start | bytes 3145736 | tf_op jit(solution)/shard_map/ppermute | solution.py:292
  40.8 1.9 %collective-permute-start.5 = (bf16[2048,256]{1,0:T(8,128)(2,1)}, bf16[2048,256]{1,0:T(8,128)(2,1)}, u32[]{:S(2)}, u32[]{:S(2)}) collective-permute-start(bf16[2048,256]{1,0:T(8,128)(2,1)} %bitcast.11.u0), channel_id=1, source_target_pairs={{0,1},{1,0},{2,3},{3,2},{4,5},{5,4},{6,7},{7,6},{8,9},{9,8},{10,11... | collective-permute-start | bytes 3145736 | tf_op jit(solution)/shard_map/ppermute | solution.py:292
  42.7 0.0 copy-done
  42.7 2.4 %collective-permute-start.8 = (bf16[256,2048]{1,0:T(8,128)(2,1)S(1)}, bf16[256,2048]{1,0:T(8,128)(2,1)S(1)}, u32[]{:S(2)}, u32[]{:S(2)}) collective-permute-start(bf16[256,2048]{1,0:T(8,128)(2,1)S(1)} %bitcast.21), channel_id=1, source_target_pairs={{0,1},{1,0},{2,3},{3,2},{4,5},{5,4},{6,7},{7,6},{8,9},{9,8},{10,11... | collective-permute-start | bytes 3145736 | tf_op jit(solution)/shard_map/ppermute | solution.py:292
  45.2 21.6 %all-to-all-done.1 = bf16[64,8,512]{2,1,0:T(8,128)(2,1)S(1)} async-done(((bf16[64,8,512]{2,1,0:T(8,128)(2,1)}), bf16[64,8,512]{2,1,0:T(8,128)(2,1)S(1)}, u32[]{:S(2)}, u32[]{:S(2)}) %all-to-all-start.1) | async-done | bytes 524320 | tf_op jit(solution)/shard_map/all_to_all | solution.py:326
  66.8 2.8 %collective-permute-start.3 = (bf16[256,512]{1,0:T(8,128)(2,1)S(1)}, bf16[256,512]{1,0:T(8,128)(2,1)S(1)}, u32[]{:S(2)}, u32[]{:S(2)}) collective-permute-start(bf16[256,512]{1,0:T(8,128)(2,1)S(1)} %get-tuple-element.23), channel_id=1, source_target_pairs={{0,6},{2,0},{4,2},{6,4},{1,7},{3,1},{5,3},{7,5},{8,14},{10,8},{12,... | collective-permute-start | bytes 786440 | tf_op jit(solution)/shard_map/ppermute | solution.py:339
  69.6 2.5 %collective-permute-start = (bf16[256,512]{1,0:T(8,128)(2,1)S(1)}, bf16[256,512]{1,0:T(8,128)(2,1)S(1)}, u32[]{:S(2)}, u32[]{:S(2)}) collective-permute-start(bf16[256,512]{1,0:T(8,128)(2,1)S(1)} %get-tuple-element.24), channel_id=1, source_target_pairs={{0,2},{2,4},{4,6},{6,0},{1,3},{3,5},{5,7},{7,1},{8,10},{10,12},{12... | collective-permute-start | bytes 786440 | tf_op jit(solution)/shard_map/ppermute | solution.py:338
  72.1 0.0 collective-permute-done.4.g1
  72.1 2.2 %collective-permute-start.1 = (bf16[256,512]{1,0:T(8,128)(2,1)S(1)}, bf16[256,512]{1,0:T(8,128)(2,1)S(1)}, u32[]{:S(2)}, u32[]{:S(2)}) collective-permute-start(bf16[256,512]{1,0:T(8,128)(2,1)S(1)} %get-tuple-element.23), channel_id=1, source_target_pairs={{0,2},{2,4},{4,6},{6,0},{1,3},{3,5},{5,7},{7,1},{8,10},{10,12},{12... | collective-permute-start | bytes 786440 | tf_op jit(solution)/shard_map/ppermute | solution.py:340
  74.3 0.0 collective-permute-done.5.u1
  74.3 4.3 %collective-permute-start.2 = (bf16[256,512]{1,0:T(8,128)(2,1)S(1)}, bf16[256,512]{1,0:T(8,128)(2,1)S(1)}, u32[]{:S(2)}, u32[]{:S(2)}) collective-permute-start(bf16[256,512]{1,0:T(8,128)(2,1)S(1)} %get-tuple-element.24), channel_id=1, source_target_pairs={{0,6},{2,0},{4,2},{6,4},{1,7},{3,1},{5,3},{7,5},{8,14},{10,8},{12,... | collective-permute-start | bytes 786440 | tf_op jit(solution)/shard_map/ppermute | solution.py:341
  78.6 0.0 collective-permute-done.3.r1
  78.6 2.8 %collective-permute-start.7 = (bf16[256,512]{1,0:T(8,128)(2,1)S(1)}, bf16[256,512]{1,0:T(8,128)(2,1)S(1)}, u32[]{:S(2)}, u32[]{:S(2)}) collective-permute-start(bf16[256,512]{1,0:T(8,128)(2,1)S(1)} %collective-permute-done.3.r1), channel_id=1, source_target_pairs={{0,6},{2,0},{4,2},{6,4},{1,7},{3,1},{5,3},{7,5},{8,14},{10,8},{12,... | collective-permute-start | bytes 786440 | tf_op jit(solution)/shard_map/ppermute | solution.py:343
  81.4 0.0 collective-permute-done.l0
  81.4 2.5 %collective-permute-start.6 = (bf16[256,512]{1,0:T(8,128)(2,1)S(1)}, bf16[256,512]{1,0:T(8,128)(2,1)S(1)}, u32[]{:S(2)}, u32[]{:S(2)}) collective-permute-start(bf16[256,512]{1,0:T(8,128)(2,1)S(1)} %collective-permute-done.l0), channel_id=1, source_target_pairs={{0,2},{2,4},{4,6},{6,0},{1,3},{3,5},{5,7},{7,1},{8,10},{10,12},{12... | collective-permute-start | bytes 786440 | tf_op jit(solution)/shard_map/ppermute | solution.py:342
  83.9 0.0 collective-permute-done.1.l1
  83.9 0.0 collective-permute-done.2.r0
  83.9 3.6 %shard_map.75.near_ref = f32[4,512,256]{2,1,0:T(8,128)S(1)} custom-call(s32[1]{0:T(128)} %bitcast.quarter_ref, bf16[512,512]{1,0:T(8,128)(2,1)S(1)} %bitcast.26, bf16[256,512]{1,0:T(8,128)(2,1)S(1)} %collective-permute-done.l0, bf16[256,512]{1,0:T(8,128)(2,1)S(1)} %collective-permute-done.1.l1, bf16[256,512]{1,0:T(8,128)(2,1)S(1)} %collective-permute-done.2.r0, ...), custom_call_target="tpu_custom_call" | custom-call | flops 1610612736 | bytes 4194304 | tf_op jit(solution)/shard_map/pallas_call | solution.py:344
  87.5 0.0 collective-permute-done.8.w1
  87.5 0.0 collective-permute-done.7.bottom_ref
  87.5 2.2 %collective-permute-done.6.top_ref = bf16[256,512]{1,0:T(8,128)(2,1)S(1)} collective-permute-done((bf16[256,512]{1,0:T(8,128)(2,1)S(1)}, bf16[256,512]{1,0:T(8,128)(2,1)S(1)}, u32[]{:S(2)}, u32[]{:S(2)}) %collective-permute-start.6) | collective-permute-done | bytes 262176 | tf_op jit(solution)/shard_map/ppermute | solution.py:342
  89.7 2.5 %shard_map.76 = (bf16[2,512,256]{2,1,0:T(8,128)(2,1)S(1)}, bf16[2,256,512]{2,1,0:T(8,128)(2,1)S(1)}) custom-call(s32[1]{0:T(128)} %bitcast.quarter_ref, f32[4,512,256]{2,1,0:T(8,128)S(1)} %shard_map.75.near_ref, bf16[256,512]{1,0:T(8,128)(2,1)S(1)} %collective-permute-done.6.top_ref, bf16[256,512]{1,0:T(8,128)(2,1)S(1)} %collective-permute-done.7.bottom_ref, ...), custom_call_target="tpu_custom_call" | custom-call | flops 805306368 | bytes 2097152 | tf_op jit(solution)/shard_map/pallas_call | solution.py:352
  92.3 2.2 %collective-permute-start.10 = (bf16[256,512]{1,0:T(8,128)(2,1)S(1)}, bf16[256,512]{1,0:T(8,128)(2,1)S(1)}, u32[]{:S(2)}, u32[]{:S(2)}) collective-permute-start(bf16[256,512]{1,0:T(8,128)(2,1)S(1)} %get-tuple-element.21), channel_id=1, source_target_pairs={{0,6},{2,0},{4,2},{6,4},{1,7},{3,1},{5,3},{7,5},{8,14},{10,8},{12,... | collective-permute-start | bytes 786440 | tf_op jit(solution)/shard_map/ppermute | solution.py:368
  94.5 3.1 %collective-permute-start.9 = (bf16[256,512]{1,0:T(8,128)(2,1)S(1)}, bf16[256,512]{1,0:T(8,128)(2,1)S(1)}, u32[]{:S(2)}, u32[]{:S(2)}) collective-permute-start(bf16[256,512]{1,0:T(8,128)(2,1)S(1)} %get-tuple-element.22), channel_id=1, source_target_pairs={{0,2},{2,4},{4,6},{6,0},{1,3},{3,5},{5,7},{7,1},{8,10},{10,12},{12... | collective-permute-start | bytes 786440 | tf_op jit(solution)/shard_map/ppermute | solution.py:367
  97.6 0.5 shard_map.79
  98.0 1.9 %collective-permute-start.12 = (bf16[256,512]{1,0:T(8,128)(2,1)S(1)}, bf16[256,512]{1,0:T(8,128)(2,1)S(1)}, u32[]{:S(2)}, u32[]{:S(2)}) collective-permute-start(bf16[256,512]{1,0:T(8,128)(2,1)S(1)} %get-tuple-element.17), channel_id=1, source_target_pairs={{0,2},{2,4},{4,6},{6,0},{1,3},{3,5},{5,7},{7,1},{8,10},{10,12},{12... | collective-permute-start | bytes 786440 | tf_op jit(solution)/shard_map/ppermute | solution.py:373
  100.0 4.6 %collective-permute-start.13 = (bf16[256,512]{1,0:T(8,128)(2,1)S(1)}, bf16[256,512]{1,0:T(8,128)(2,1)S(1)}, u32[]{:S(2)}, u32[]{:S(2)}) collective-permute-start(bf16[256,512]{1,0:T(8,128)(2,1)S(1)} %get-tuple-element.18), channel_id=1, source_target_pairs={{0,6},{2,0},{4,2},{6,4},{1,7},{3,1},{5,3},{7,5},{8,14},{10,8},{12,... | collective-permute-start | bytes 786440 | tf_op jit(solution)/shard_map/ppermute | solution.py:374
  104.6 0.0 collective-permute-done.10.bottom_ref
  104.6 0.0 collective-permute-done.9.top_ref
  104.6 0.5 shard_map.78
  105.1 1.9 %collective-permute-start.11 = (bf16[256,512]{1,0:T(8,128)(2,1)S(1)}, bf16[256,512]{1,0:T(8,128)(2,1)S(1)}, u32[]{:S(2)}, u32[]{:S(2)}) collective-permute-start(bf16[256,512]{1,0:T(8,128)(2,1)S(1)} %get-tuple-element.16), channel_id=1, source_target_pairs={{0,2},{2,4},{4,6},{6,0},{1,3},{3,5},{5,7},{7,1},{8,10},{10,12},{12... | collective-permute-start | bytes 786440 | tf_op jit(solution)/shard_map/ppermute | solution.py:378
  107.0 4.6 %collective-permute-start.14 = (bf16[256,512]{1,0:T(8,128)(2,1)S(1)}, bf16[256,512]{1,0:T(8,128)(2,1)S(1)}, u32[]{:S(2)}, u32[]{:S(2)}) collective-permute-start(bf16[256,512]{1,0:T(8,128)(2,1)S(1)} %get-tuple-element.19), channel_id=1, source_target_pairs={{0,6},{2,0},{4,2},{6,4},{1,7},{3,1},{5,3},{7,5},{8,14},{10,8},{12,... | collective-permute-start | bytes 786440 | tf_op jit(solution)/shard_map/ppermute | solution.py:379
  111.6 0.5 shard_map.77.own_ref
  112.1 0.0 collective-permute-done.12.l1
  112.1 0.0 collective-permute-done.13.r0
  112.1 3.2 %collective-permute-done.11.l0 = bf16[256,512]{1,0:T(8,128)(2,1)S(1)} collective-permute-done((bf16[256,512]{1,0:T(8,128)(2,1)S(1)}, bf16[256,512]{1,0:T(8,128)(2,1)S(1)}, u32[]{:S(2)}, u32[]{:S(2)}) %collective-permute-start.11) | collective-permute-done | bytes 262176 | tf_op jit(solution)/shard_map/ppermute | solution.py:378
  115.3 0.9 collective-permute-done.14.r1
  116.2 0.2 shard_map.80
  116.3 0.0 copy-start.1
  116.4 34.3 %all_to_all.21 = bf16[64,8,512]{2,1,0:T(8,128)(2,1)S(1)} all-to-all(bf16[64,8,512]{2,1,0:T(8,128)(2,1)S(1)} %bitcast.27), channel_id=1, replica_groups=mesh['expert'=64,'x'=4,'c'=2] {'expert'}, dimensions={0} | all-to-all | bytes 1048576 | tf_op jit(solution)/shard_map/all_to_all | solution.py:392
  150.6 0.9 shard_map.81
  151.6 20.4 %all_to_all.22.parts_ref = bf16[8,48,512]{2,1,0:T(8,128)(2,1)S(1)} all-to-all(bf16[8,48,512]{2,1,0:T(8,128)(2,1)S(1)} %shard_map.81), channel_id=1, replica_groups=mesh['expert'=64,'x'=4,'c'=2] {'x','c'}, dimensions={0} | all-to-all | bytes 786432 | tf_op jit(solution)/shard_map/all_to_all | solution.py:401
  171.9 0.0 copy-done.1
  171.9 0.7 shard_map.82
  (2 shorter events, 0.1 us)
Async XLA Ops:
  0.0 42.7 %copy-start = (bf16[1,256,2048]{2,1,0:T(8,128)(2,1)S(1)}, bf16[1,256,2048]{2,1,0:T(8,128)(2,1)}, u32[]{:S(2)}) copy-start(bf16[1,256,2048]{2,1,0:T(8,128)(2,1)} %param.12) | copy-start | bytes 3145732
  23.6 43.2 %all-to-all-start.1 = ((bf16[64,8,512]{2,1,0:T(8,128)(2,1)}), bf16[64,8,512]{2,1,0:T(8,128)(2,1)S(1)}, u32[]{:S(2)}, u32[]{:S(2)}) async-start(bf16[64,8,512]{2,1,0:T(8,128)(2,1)} %bitcast.6), calls=%async_computation.1 | async-start | bytes 1048576 | tf_op jit(solution)/shard_map/all_to_all | solution.py:326
  37.6 34.5 %collective-permute-start.4 = (bf16[2048,256]{1,0:T(8,128)(2,1)}, bf16[2048,256]{1,0:T(8,128)(2,1)}, u32[]{:S(2)}, u32[]{:S(2)}) collective-permute-start(bf16[2048,256]{1,0:T(8,128)(2,1)} %bitcast.10.g0), channel_id=1, source_target_pairs={{0,1},{1,0},{2,3},{3,2},{4,5},{5,4},{6,7},{7,6},{8,9},{9,8},{10,11... | collective-permute-start | bytes 3145736 | tf_op jit(solution)/shard_map/ppermute | solution.py:292
  40.8 33.5 %collective-permute-start.5 = (bf16[2048,256]{1,0:T(8,128)(2,1)}, bf16[2048,256]{1,0:T(8,128)(2,1)}, u32[]{:S(2)}, u32[]{:S(2)}) collective-permute-start(bf16[2048,256]{1,0:T(8,128)(2,1)} %bitcast.11.u0), channel_id=1, source_target_pairs={{0,1},{1,0},{2,3},{3,2},{4,5},{5,4},{6,7},{7,6},{8,9},{9,8},{10,11... | collective-permute-start | bytes 3145736 | tf_op jit(solution)/shard_map/ppermute | solution.py:292
  42.7 44.8 %collective-permute-start.8 = (bf16[256,2048]{1,0:T(8,128)(2,1)S(1)}, bf16[256,2048]{1,0:T(8,128)(2,1)S(1)}, u32[]{:S(2)}, u32[]{:S(2)}) collective-permute-start(bf16[256,2048]{1,0:T(8,128)(2,1)S(1)} %bitcast.21), channel_id=1, source_target_pairs={{0,1},{1,0},{2,3},{3,2},{4,5},{5,4},{6,7},{7,6},{8,9},{9,8},{10,11... | collective-permute-start | bytes 3145736 | tf_op jit(solution)/shard_map/ppermute | solution.py:292
  66.8 11.8 %collective-permute-start.3 = (bf16[256,512]{1,0:T(8,128)(2,1)S(1)}, bf16[256,512]{1,0:T(8,128)(2,1)S(1)}, u32[]{:S(2)}, u32[]{:S(2)}) collective-permute-start(bf16[256,512]{1,0:T(8,128)(2,1)S(1)} %get-tuple-element.23), channel_id=1, source_target_pairs={{0,6},{2,0},{4,2},{6,4},{1,7},{3,1},{5,3},{7,5},{8,14},{10,8},{12,... | collective-permute-start | bytes 786440 | tf_op jit(solution)/shard_map/ppermute | solution.py:339
  69.6 11.8 %collective-permute-start = (bf16[256,512]{1,0:T(8,128)(2,1)S(1)}, bf16[256,512]{1,0:T(8,128)(2,1)S(1)}, u32[]{:S(2)}, u32[]{:S(2)}) collective-permute-start(bf16[256,512]{1,0:T(8,128)(2,1)S(1)} %get-tuple-element.24), channel_id=1, source_target_pairs={{0,2},{2,4},{4,6},{6,0},{1,3},{3,5},{5,7},{7,1},{8,10},{10,12},{12... | collective-permute-start | bytes 786440 | tf_op jit(solution)/shard_map/ppermute | solution.py:338
  72.1 11.8 %collective-permute-start.1 = (bf16[256,512]{1,0:T(8,128)(2,1)S(1)}, bf16[256,512]{1,0:T(8,128)(2,1)S(1)}, u32[]{:S(2)}, u32[]{:S(2)}) collective-permute-start(bf16[256,512]{1,0:T(8,128)(2,1)S(1)} %get-tuple-element.23), channel_id=1, source_target_pairs={{0,2},{2,4},{4,6},{6,0},{1,3},{3,5},{5,7},{7,1},{8,10},{10,12},{12... | collective-permute-start | bytes 786440 | tf_op jit(solution)/shard_map/ppermute | solution.py:340
  74.3 9.6 %collective-permute-start.2 = (bf16[256,512]{1,0:T(8,128)(2,1)S(1)}, bf16[256,512]{1,0:T(8,128)(2,1)S(1)}, u32[]{:S(2)}, u32[]{:S(2)}) collective-permute-start(bf16[256,512]{1,0:T(8,128)(2,1)S(1)} %get-tuple-element.24), channel_id=1, source_target_pairs={{0,6},{2,0},{4,2},{6,4},{1,7},{3,1},{5,3},{7,5},{8,14},{10,8},{12,... | collective-permute-start | bytes 786440 | tf_op jit(solution)/shard_map/ppermute | solution.py:341
  78.6 8.9 %collective-permute-start.7 = (bf16[256,512]{1,0:T(8,128)(2,1)S(1)}, bf16[256,512]{1,0:T(8,128)(2,1)S(1)}, u32[]{:S(2)}, u32[]{:S(2)}) collective-permute-start(bf16[256,512]{1,0:T(8,128)(2,1)S(1)} %collective-permute-done.3.r1), channel_id=1, source_target_pairs={{0,6},{2,0},{4,2},{6,4},{1,7},{3,1},{5,3},{7,5},{8,14},{10,8},{12,... | collective-permute-start | bytes 786440 | tf_op jit(solution)/shard_map/ppermute | solution.py:343
  81.4 8.3 %collective-permute-start.6 = (bf16[256,512]{1,0:T(8,128)(2,1)S(1)}, bf16[256,512]{1,0:T(8,128)(2,1)S(1)}, u32[]{:S(2)}, u32[]{:S(2)}) collective-permute-start(bf16[256,512]{1,0:T(8,128)(2,1)S(1)} %collective-permute-done.l0), channel_id=1, source_target_pairs={{0,2},{2,4},{4,6},{6,0},{1,3},{3,5},{5,7},{7,1},{8,10},{10,12},{12... | collective-permute-start | bytes 786440 | tf_op jit(solution)/shard_map/ppermute | solution.py:342
  92.3 12.3 %collective-permute-start.10 = (bf16[256,512]{1,0:T(8,128)(2,1)S(1)}, bf16[256,512]{1,0:T(8,128)(2,1)S(1)}, u32[]{:S(2)}, u32[]{:S(2)}) collective-permute-start(bf16[256,512]{1,0:T(8,128)(2,1)S(1)} %get-tuple-element.21), channel_id=1, source_target_pairs={{0,6},{2,0},{4,2},{6,4},{1,7},{3,1},{5,3},{7,5},{8,14},{10,8},{12,... | collective-permute-start | bytes 786440 | tf_op jit(solution)/shard_map/ppermute | solution.py:368
  94.5 10.1 %collective-permute-start.9 = (bf16[256,512]{1,0:T(8,128)(2,1)S(1)}, bf16[256,512]{1,0:T(8,128)(2,1)S(1)}, u32[]{:S(2)}, u32[]{:S(2)}) collective-permute-start(bf16[256,512]{1,0:T(8,128)(2,1)S(1)} %get-tuple-element.22), channel_id=1, source_target_pairs={{0,2},{2,4},{4,6},{6,0},{1,3},{3,5},{5,7},{7,1},{8,10},{10,12},{12... | collective-permute-start | bytes 786440 | tf_op jit(solution)/shard_map/ppermute | solution.py:367
  98.0 14.0 %collective-permute-start.12 = (bf16[256,512]{1,0:T(8,128)(2,1)S(1)}, bf16[256,512]{1,0:T(8,128)(2,1)S(1)}, u32[]{:S(2)}, u32[]{:S(2)}) collective-permute-start(bf16[256,512]{1,0:T(8,128)(2,1)S(1)} %get-tuple-element.17), channel_id=1, source_target_pairs={{0,2},{2,4},{4,6},{6,0},{1,3},{3,5},{5,7},{7,1},{8,10},{10,12},{12... | collective-permute-start | bytes 786440 | tf_op jit(solution)/shard_map/ppermute | solution.py:373
  100.0 12.1 %collective-permute-start.13 = (bf16[256,512]{1,0:T(8,128)(2,1)S(1)}, bf16[256,512]{1,0:T(8,128)(2,1)S(1)}, u32[]{:S(2)}, u32[]{:S(2)}) collective-permute-start(bf16[256,512]{1,0:T(8,128)(2,1)S(1)} %get-tuple-element.18), channel_id=1, source_target_pairs={{0,6},{2,0},{4,2},{6,4},{1,7},{3,1},{5,3},{7,5},{8,14},{10,8},{12,... | collective-permute-start | bytes 786440 | tf_op jit(solution)/shard_map/ppermute | solution.py:374
  105.1 10.2 %collective-permute-start.11 = (bf16[256,512]{1,0:T(8,128)(2,1)S(1)}, bf16[256,512]{1,0:T(8,128)(2,1)S(1)}, u32[]{:S(2)}, u32[]{:S(2)}) collective-permute-start(bf16[256,512]{1,0:T(8,128)(2,1)S(1)} %get-tuple-element.16), channel_id=1, source_target_pairs={{0,2},{2,4},{4,6},{6,0},{1,3},{3,5},{5,7},{7,1},{8,10},{10,12},{12... | collective-permute-start | bytes 786440 | tf_op jit(solution)/shard_map/ppermute | solution.py:378
  107.0 9.2 %collective-permute-start.14 = (bf16[256,512]{1,0:T(8,128)(2,1)S(1)}, bf16[256,512]{1,0:T(8,128)(2,1)S(1)}, u32[]{:S(2)}, u32[]{:S(2)}) collective-permute-start(bf16[256,512]{1,0:T(8,128)(2,1)S(1)} %get-tuple-element.19), channel_id=1, source_target_pairs={{0,6},{2,0},{4,2},{6,4},{1,7},{3,1},{5,3},{7,5},{8,14},{10,8},{12,... | collective-permute-start | bytes 786440 | tf_op jit(solution)/shard_map/ppermute | solution.py:379
  116.3 55.6 %copy-start.1 = (f32[1,3,2048]{2,0,1:T(1,128)S(1)}, f32[1,3,2048]{2,0,1:T(1,128)}, u32[]{:S(2)}) copy-start(f32[1,3,2048]{2,0,1:T(1,128)} %param.8) | copy-start | bytes 73732

commit v6 on v5

--- a/solution.py
+++ b/solution.py
@@ -173,10 +173,11 @@
 
 
 def far_kernel(
-    quarter_ref, near_ref, top_ref, bottom_ref, g0, u0, g1, u1, w0, w1,
+    part, quarter_ref, near_ref, far_ref, g0, u0, g1, u1, w0, w1,
     hidden_ref, out_ref, held, held_down, arrived,
 ):
-    rows, width = top_ref.shape
+    rows, width = far_ref.shape
+    span = slice(part * rows, (part + 1) * rows)
     blocks = g0.shape[0] // width
     where = cut(quarter_ref, blocks // 2, blocks, width)
     copies = [
@@ -191,52 +192,52 @@
     for core in range(2):
         copies[2 * core].wait()
         copies[2 * core + 1].wait()
-        for part, ref in enumerate((top_ref, bottom_ref)):
-            span = slice(part * rows, (part + 1) * rows)
-            gate, up = [
-                near_ref[index, span, :]
-                + jnp.dot(ref[...], held[index], preferred_element_type=F32)
-                for index in (2 * core, 2 * core + 1)
-            ]
-            hidden_ref[core, span, :] = (gate * jax.nn.sigmoid(gate) * up).astype(BF16)
+        gate, up = [
+            near_ref[index, span, :]
+            + jnp.dot(far_ref[...], held[index], preferred_element_type=F32)
+            for index in (2 * core, 2 * core + 1)
+        ]
+        hidden_ref[core] = (gate * jax.nn.sigmoid(gate) * up).astype(BF16)
     copies[4].wait()
     copies[5].wait()
-    for part in range(2):
-        span = slice(part * rows, (part + 1) * rows)
-        out_ref[part] = (
-            jnp.dot(hidden_ref[0, span, :], held_down[0], preferred_element_type=F32)
-            + jnp.dot(hidden_ref[1, span, :], held_down[1], preferred_element_type=F32)
-        ).astype(BF16)
-
-
-def down(hidden_ref, span, w0, w1, where):
-    return jnp.dot(hidden_ref[0, span, :], w0[:, where], preferred_element_type=F32) + jnp.dot(
-        hidden_ref[1, span, :], w1[:, where], preferred_element_type=F32
-    )
-
-
-def direct_kernel(quarter_ref, hidden_ref, w0, w1, right_ref, left_ref):
+    out_ref[...] = (
+        jnp.dot(hidden_ref[0], held_down[0], preferred_element_type=F32)
+        + jnp.dot(hidden_ref[1], held_down[1], preferred_element_type=F32)
+    ).astype(BF16)
+
+
+def down(hidden_ref, w0, w1, where):
+    return jnp.dot(hidden_ref[0], w0[:, where], preferred_element_type=F32) + jnp.dot(
+        hidden_ref[1], w1[:, where], preferred_element_type=F32
+    )
+
+
+def direct_kernel(quarter_ref, upper_ref, lower_ref, w0, w1, right_ref, left_ref):
     rows, width = right_ref.shape
     blocks = w0.shape[1] // width
-    right = down(hidden_ref, slice(rows, None), w0, w1, cut(quarter_ref, 1, blocks, width))
-    left = down(hidden_ref, slice(0, rows), w0, w1, cut(quarter_ref, blocks - 1, blocks, width))
+    right = down(lower_ref, w0, w1, cut(quarter_ref, 1, blocks, width))
+    left = down(upper_ref, w0, w1, cut(quarter_ref, blocks - 1, blocks, width))
     right_ref[...] = right.astype(BF16)
     left_ref[...] = left.astype(BF16)
 
 
-def relay_kernel(quarter_ref, hidden_ref, w0, w1, top_ref, bottom_ref, right_ref, left_ref):
+def relay_kernel(
+    quarter_ref, upper_ref, lower_ref, w0, w1, top_ref, bottom_ref, right_ref, left_ref
+):
     rows, width = right_ref.shape
     blocks = w0.shape[1] // width
-    right = down(hidden_ref, slice(0, rows), w0, w1, cut(quarter_ref, 1, blocks, width))
-    left = down(hidden_ref, slice(rows, None), w0, w1, cut(quarter_ref, blocks - 1, blocks, width))
+    right = down(upper_ref, w0, w1, cut(quarter_ref, 1, blocks, width))
+    left = down(lower_ref, w0, w1, cut(quarter_ref, blocks - 1, blocks, width))
     right_ref[...] = (right + top_ref[...].astype(F32)).astype(BF16)
     left_ref[...] = (left + bottom_ref[...].astype(F32)).astype(BF16)
 
 
-def own_kernel(quarter_ref, hidden_ref, w0, w1, out_ref):
+def own_kernel(quarter_ref, upper_ref, lower_ref, w0, w1, out_ref):
     width = out_ref.shape[1]
     where = cut(quarter_ref, 0, w0.shape[1] // width, width)
-    out_ref[...] = down(hidden_ref, slice(None), w0, w1, where)
+    rows = upper_ref.shape[1]
+    out_ref[0:rows, :] = down(upper_ref, w0, w1, where)
+    out_ref[rows:, :] = down(lower_ref, w0, w1, where)
 
 
 def sum_kernel(own_ref, l0, l1, r0, r1, out_ref):
@@ -349,32 +350,37 @@
         "vvvvvvhhhh",
         [pltpu.VMEM((4, 3, lanes, cols), BF16), pltpu.SemaphoreType.DMA((4, 3))],
     )(quarter, arrived, l0, l1, r0, r1, g0, u0, g1, u1)
-    hidden, far = call(
-        far_kernel,
-        (
-            jax.ShapeDtypeStruct((2, count, cols), BF16),
-            jax.ShapeDtypeStruct((2, cut_rows, lanes), BF16),
-        ),
-        12 * count * lanes * cols,
-        16 * count * cols,
-        "vvvvhhhhhh",
-        [
-            pltpu.VMEM((4, lanes, cols), BF16),
-            pltpu.VMEM((2, cols, lanes), BF16),
-            pltpu.SemaphoreType.DMA((6,)),
-        ],
-    )(quarter, near, top, bottom, g0, u0, g1, u1, w0, w1)
-    top = lax.ppermute(far[0], "x", onward)
-    bottom = lax.ppermute(far[1], "x", backward)
+    halves = []
+    for part, came in ((1, bottom), (0, top)):
+        halves.append(
+            call(
+                functools.partial(far_kernel, part),
+                (
+                    jax.ShapeDtypeStruct((2, cut_rows, cols), BF16),
+                    jax.ShapeDtypeStruct((cut_rows, lanes), BF16),
+                ),
+                6 * count * lanes * cols,
+                8 * count * cols,
+                "vvvhhhhhh",
+                [
+                    pltpu.VMEM((4, lanes, cols), BF16),
+                    pltpu.VMEM((2, cols, lanes), BF16),
+                    pltpu.SemaphoreType.DMA((6,)),
+                ],
+            )(quarter, near, came, g0, u0, g1, u1, w0, w1)
+        )
+    (lower_hidden, lower_far), (upper_hidden, upper_far) = halves
+    bottom = lax.ppermute(lower_far, "x", backward)
+    top = lax.ppermute(upper_far, "x", onward)
     piece = jax.ShapeDtypeStruct((cut_rows, lanes), BF16)
     direct_right, direct_left = call(
         direct_kernel, (piece, piece), 4 * count * lanes * cols, 4 * count * lanes
-    )(quarter, hidden, w0, w1)
+    )(quarter, upper_hidden, lower_hidden, w0, w1)
     l1 = lax.ppermute(direct_right, "x", onward)
     r0 = lax.ppermute(direct_left, "x", backward)
     to_right, to_left = call(
         relay_kernel, (piece, piece), 4 * count * lanes * cols, 4 * count * lanes
-    )(quarter, hidden, w0, w1, top, bottom)
+    )(quarter, upper_hidden, lower_hidden, w0, w1, top, bottom)
     l0 = lax.ppermute(to_right, "x", onward)
     r1 = lax.ppermute(to_left, "x", backward)
     own_sum = call(
@@ -382,7 +388,7 @@
         jax.ShapeDtypeStruct((count, lanes), F32),
         4 * count * lanes * cols,
         4 * count * lanes,
-    )(quarter, hidden, w0, w1)
+    )(quarter, upper_hidden, lower_hidden, w0, w1)
     summed = call(
         sum_kernel,
         jax.ShapeDtypeStruct((count, lanes), BF16),

time: 173 us -> 176 us (1.017)
  Pallas kernels: 13.2 us -> 15.3 us
    ppermute x1, waiting for transfers between devices: 2.21 us -> 0.01 us  [body(): top = lax.ppermute(l0, 'x', onward)]
    pallas_call x1 -> x2, Pallas kernels: 2.47 us -> 4.01 us  [body(): call(functools.partial(far_kernel, part), (jax.ShapeDtypeStruct((2, cut_r...]
  transfers between devices with their start and end apart: 16 -> 16, of which waited for: 4 -> 3; matrix products, arithmetic and copies ran while one was open for 0% -> 1% of each run, Pallas kernels for 3% -> 5%
where the time goes in v6:
time: 176 us; the launch traced here: 175 us
  blocking collectives  73.8 us (42%)
  starting transfers between devices  57.8 us (33%)
  waiting for transfers between devices  26.7 us (15%)
  Pallas kernels  15.3 us (9%)
    all_to_all x1, blocking collectives, body(): lax.all_to_all(summed.reshape(images, half, lanes), 'expert', 0, 0, tiled...  33.5 us
    all_to_all x1, waiting for transfers between devices, body(): lax.all_to_all(slots.reshape(experts, half, lanes), 'expert', 0, 0, tiled...  21.4 us
    all_to_all x1, blocking collectives, body(): mixed = lax.all_to_all(mixed, tensor, 0, 0, tiled=True)  20.7 us
    all_to_all x1, blocking collectives, body(): packet = lax.all_to_all(packet, tensor, 0, 0, tiled=True)  19.6 us
    all_to_all x1, starting transfers between devices, body(): lax.all_to_all(slots.reshape(experts, half, lanes), 'expert', 0, 0, tiled...  14.2 us
    ppermute x3, starting transfers between devices, body(): others = [lax.ppermute(w, 'c', swap) for w in weights]  7.56 us
    ppermute x1, starting transfers between devices, body(): r1 = lax.ppermute(to_left, 'x', backward)  4.57 us
    ppermute x1, starting transfers between devices, body(): r0 = lax.ppermute(direct_left, 'x', backward)  4.57 us
  transfers between devices with their start and end apart: 16, of which 3 were waited for; matrix products, arithmetic and copies ran while one was open for 1% of the time, Pallas kernels for 5%

profile of v6, /device:TPU:1, one launch (start us, length us, event | category | flops | bytes accessed | tf_op | source)
XLA Modules:
  0.0 175.1 jit_solution(4939816266258898114)
XLA Ops:
  0.0 0.0 copy-start.1
  0.0 0.0 copy-start
  0.0 2.5 %shard_map.73 = bf16[8,64,512]{2,1,0:T(8,128)(2,1)} custom-call(s32[1]{0:T(128)} %bitcast.2.member_ref, s32[2,48]{1,0:T(2,128)} %bitcast.32, bf16[48,2048]{1,0:T(8,128)(2,1)} %tokens_in.1, f32[3,1,2048]{2,1,0:T(1,128)} %bitcast.29, bf16[64,2048]{1,0:T(8,128)(2,1)} %bitcast.31), custom_call_target="tpu_custom_call" | custom-call | flops 12582912 | bytes 393216 | tf_op jit(solution)/shard_map/pallas_call | solution.py:296
  2.6 19.6 %all_to_all.20.packet_ref = bf16[8,64,512]{2,1,0:T(8,128)(2,1)S(1)} all-to-all(bf16[8,64,512]{2,1,0:T(8,128)(2,1)} %shard_map.73), channel_id=1, replica_groups=mesh['expert'=64,'x'=4,'c'=2] {'x','c'}, dimensions={0} | all-to-all | bytes 1048576 | tf_op jit(solution)/shard_map/all_to_all | solution.py:317
  22.2 1.4 shard_map.74
  23.6 14.2 %all-to-all-start.1 = ((bf16[64,8,512]{2,1,0:T(8,128)(2,1)}), bf16[64,8,512]{2,1,0:T(8,128)(2,1)}, u32[]{:S(2)}, u32[]{:S(2)}) async-start(bf16[64,8,512]{2,1,0:T(8,128)(2,1)} %bitcast.6), calls=%async_computation.1 | async-start | bytes 1048576 | tf_op jit(solution)/shard_map/all_to_all | solution.py:327
  37.9 0.0 copy-done.1
  37.9 3.2 %collective-permute-start.4 = (bf16[2048,256]{1,0:T(8,128)(2,1)S(1)}, bf16[2048,256]{1,0:T(8,128)(2,1)}, u32[]{:S(2)}, u32[]{:S(2)}) collective-permute-start(bf16[2048,256]{1,0:T(8,128)(2,1)S(1)} %bitcast.23), channel_id=1, source_target_pairs={{0,1},{1,0},{2,3},{3,2},{4,5},{5,4},{6,7},{7,6},{8,9},{9,8},{10,11... | collective-permute-start | bytes 3145736 | tf_op jit(solution)/shard_map/ppermute | solution.py:293
  41.1 1.9 %collective-permute-start.5 = (bf16[2048,256]{1,0:T(8,128)(2,1)}, bf16[2048,256]{1,0:T(8,128)(2,1)}, u32[]{:S(2)}, u32[]{:S(2)}) collective-permute-start(bf16[2048,256]{1,0:T(8,128)(2,1)} %bitcast.11.u0), channel_id=1, source_target_pairs={{0,1},{1,0},{2,3},{3,2},{4,5},{5,4},{6,7},{7,6},{8,9},{9,8},{10,11... | collective-permute-start | bytes 3145736 | tf_op jit(solution)/shard_map/ppermute | solution.py:293
  43.0 0.0 copy-done
  43.1 2.4 %collective-permute-start.7 = (bf16[256,2048]{1,0:T(8,128)(2,1)S(1)}, bf16[256,2048]{1,0:T(8,128)(2,1)S(1)}, u32[]{:S(2)}, u32[]{:S(2)}) collective-permute-start(bf16[256,2048]{1,0:T(8,128)(2,1)S(1)} %bitcast.17), channel_id=1, source_target_pairs={{0,1},{1,0},{2,3},{3,2},{4,5},{5,4},{6,7},{7,6},{8,9},{9,8},{10,11... | collective-permute-start | bytes 3145736 | tf_op jit(solution)/shard_map/ppermute | solution.py:293
  45.5 21.4 %all-to-all-done.1 = bf16[64,8,512]{2,1,0:T(8,128)(2,1)} async-done(((bf16[64,8,512]{2,1,0:T(8,128)(2,1)}), bf16[64,8,512]{2,1,0:T(8,128)(2,1)}, u32[]{:S(2)}, u32[]{:S(2)}) %all-to-all-start.1) | async-done | bytes 524320 | tf_op jit(solution)/shard_map/all_to_all | solution.py:327
  66.9 1.1 slice_bitcast_fusion
  67.9 2.8 %collective-permute-start.3 = (bf16[256,512]{1,0:T(8,128)(2,1)S(1)}, bf16[256,512]{1,0:T(8,128)(2,1)S(1)}, u32[]{:S(2)}, u32[]{:S(2)}) collective-permute-start(bf16[256,512]{1,0:T(8,128)(2,1)S(1)} %get-tuple-element.25), channel_id=1, source_target_pairs={{0,6},{2,0},{4,2},{6,4},{1,7},{3,1},{5,3},{7,5},{8,14},{10,8},{12,... | collective-permute-start | bytes 786440 | tf_op jit(solution)/shard_map/ppermute | solution.py:340
  70.7 2.5 %collective-permute-start = (bf16[256,512]{1,0:T(8,128)(2,1)S(1)}, bf16[256,512]{1,0:T(8,128)(2,1)S(1)}, u32[]{:S(2)}, u32[]{:S(2)}) collective-permute-start(bf16[256,512]{1,0:T(8,128)(2,1)S(1)} %get-tuple-element.26), channel_id=1, source_target_pairs={{0,2},{2,4},{4,6},{6,0},{1,3},{3,5},{5,7},{7,1},{8,10},{10,12},{12... | collective-permute-start | bytes 786440 | tf_op jit(solution)/shard_map/ppermute | solution.py:339
  73.2 0.0 collective-permute-done.4.g1
  73.2 2.2 %collective-permute-start.1 = (bf16[256,512]{1,0:T(8,128)(2,1)S(1)}, bf16[256,512]{1,0:T(8,128)(2,1)S(1)}, u32[]{:S(2)}, u32[]{:S(2)}) collective-permute-start(bf16[256,512]{1,0:T(8,128)(2,1)S(1)} %get-tuple-element.25), channel_id=1, source_target_pairs={{0,2},{2,4},{4,6},{6,0},{1,3},{3,5},{5,7},{7,1},{8,10},{10,12},{12... | collective-permute-start | bytes 786440 | tf_op jit(solution)/shard_map/ppermute | solution.py:341
  75.5 0.0 collective-permute-done.5.u1
  75.5 4.3 %collective-permute-start.2 = (bf16[256,512]{1,0:T(8,128)(2,1)S(1)}, bf16[256,512]{1,0:T(8,128)(2,1)S(1)}, u32[]{:S(2)}, u32[]{:S(2)}) collective-permute-start(bf16[256,512]{1,0:T(8,128)(2,1)S(1)} %get-tuple-element.26), channel_id=1, source_target_pairs={{0,6},{2,0},{4,2},{6,4},{1,7},{3,1},{5,3},{7,5},{8,14},{10,8},{12,... | collective-permute-start | bytes 786440 | tf_op jit(solution)/shard_map/ppermute | solution.py:342
  79.8 0.0 collective-permute-done.3.r1
  79.8 2.8 %collective-permute-start.8 = (bf16[256,512]{1,0:T(8,128)(2,1)S(1)}, bf16[256,512]{1,0:T(8,128)(2,1)S(1)}, u32[]{:S(2)}, u32[]{:S(2)}) collective-permute-start(bf16[256,512]{1,0:T(8,128)(2,1)S(1)} %collective-permute-done.3.r1), channel_id=1, source_target_pairs={{0,6},{2,0},{4,2},{6,4},{1,7},{3,1},{5,3},{7,5},{8,14},{10,8},{12,... | collective-permute-start | bytes 786440 | tf_op jit(solution)/shard_map/ppermute | solution.py:344
  82.6 0.0 collective-permute-done.l0
  82.6 2.5 %collective-permute-start.6 = (bf16[256,512]{1,0:T(8,128)(2,1)S(1)}, bf16[256,512]{1,0:T(8,128)(2,1)S(1)}, u32[]{:S(2)}, u32[]{:S(2)}) collective-permute-start(bf16[256,512]{1,0:T(8,128)(2,1)S(1)} %collective-permute-done.l0), channel_id=1, source_target_pairs={{0,2},{2,4},{4,6},{6,0},{1,3},{3,5},{5,7},{7,1},{8,10},{10,12},{12... | collective-permute-start | bytes 786440 | tf_op jit(solution)/shard_map/ppermute | solution.py:343
  85.1 0.0 collective-permute-done.1.l1
  85.1 0.0 collective-permute-done.2.r0
  85.1 4.1 %shard_map.75.near_ref = f32[4,512,256]{2,1,0:T(8,128)S(1)} custom-call(s32[1]{0:T(128)} %bitcast.quarter_ref, bf16[512,512]{1,0:T(8,128)(2,1)} %bitcast.7.a_ref, bf16[256,512]{1,0:T(8,128)(2,1)S(1)} %collective-permute-done.l0, bf16[256,512]{1,0:T(8,128)(2,1)S(1)} %collective-permute-done.1.l1, bf16[256,512]{1,0:T(8,128)(2,1)S(1)} %collective-permute-done.2.r0, ...), custom_call_target="tpu_custom_call" | custom-call | flops 1610612736 | bytes 4194304 | tf_op jit(solution)/shard_map/pallas_call | solution.py:345
  89.2 0.0 collective-permute-done.7.w1
  89.2 0.0 collective-permute-done.8.far_ref
  89.2 2.0 %shard_map.77 = (bf16[2,256,256]{2,1,0:T(8,128)(2,1)S(1)}, bf16[256,512]{1,0:T(8,128)(2,1)S(1)}) custom-call(s32[1]{0:T(128)} %bitcast.quarter_ref, f32[4,512,256]{2,1,0:T(8,128)S(1)} %shard_map.75.near_ref, bf16[256,512]{1,0:T(8,128)(2,1)S(1)} %collective-permute-done.8.far_ref, bf16[2048,256]{1,0:T(8,128)(2,1)S(1)} %bitcast.25, ...), custom_call_target="tpu_custom_call" | custom-call | flops 402653184 | bytes 1048576 | tf_op jit(solution)/shard_map/pallas_call | solution.py:356
  91.2 4.0 %collective-permute-start.10 = (bf16[256,512]{1,0:T(8,128)(2,1)S(1)}, bf16[256,512]{1,0:T(8,128)(2,1)S(1)}, u32[]{:S(2)}, u32[]{:S(2)}) collective-permute-start(bf16[256,512]{1,0:T(8,128)(2,1)S(1)} %get-tuple-element.19), channel_id=1, source_target_pairs={{0,6},{2,0},{4,2},{6,4},{1,7},{3,1},{5,3},{7,5},{8,14},{10,8},{12,... | collective-permute-start | bytes 786440 | tf_op jit(solution)/shard_map/ppermute | solution.py:373
  95.2 0.0 collective-permute-done.6.far_ref
  95.3 2.0 %shard_map.76 = (bf16[2,256,256]{2,1,0:T(8,128)(2,1)S(1)}, bf16[256,512]{1,0:T(8,128)(2,1)S(1)}) custom-call(s32[1]{0:T(128)} %bitcast.quarter_ref, f32[4,512,256]{2,1,0:T(8,128)S(1)} %shard_map.75.near_ref, bf16[256,512]{1,0:T(8,128)(2,1)S(1)} %collective-permute-done.6.far_ref, bf16[2048,256]{1,0:T(8,128)(2,1)S(1)} %bitcast.26, ...), custom_call_target="tpu_custom_call" | custom-call | flops 402653184 | bytes 1048576 | tf_op jit(solution)/shard_map/pallas_call | solution.py:356
  97.3 1.9 %collective-permute-start.9 = (bf16[256,512]{1,0:T(8,128)(2,1)S(1)}, bf16[256,512]{1,0:T(8,128)(2,1)S(1)}, u32[]{:S(2)}, u32[]{:S(2)}) collective-permute-start(bf16[256,512]{1,0:T(8,128)(2,1)S(1)} %get-tuple-element.18), channel_id=1, source_target_pairs={{0,2},{2,4},{4,6},{6,0},{1,3},{3,5},{5,7},{7,1},{8,10},{10,12},{12... | collective-permute-start | bytes 786440 | tf_op jit(solution)/shard_map/ppermute | solution.py:374
  99.2 0.5 shard_map.80
  99.7 1.9 %collective-permute-start.12 = (bf16[256,512]{1,0:T(8,128)(2,1)S(1)}, bf16[256,512]{1,0:T(8,128)(2,1)S(1)}, u32[]{:S(2)}, u32[]{:S(2)}) collective-permute-start(bf16[256,512]{1,0:T(8,128)(2,1)S(1)} %get-tuple-element.21), channel_id=1, source_target_pairs={{0,2},{2,4},{4,6},{6,0},{1,3},{3,5},{5,7},{7,1},{8,10},{10,12},{12... | collective-permute-start | bytes 786440 | tf_op jit(solution)/shard_map/ppermute | solution.py:379
  101.6 4.6 %collective-permute-start.13 = (bf16[256,512]{1,0:T(8,128)(2,1)S(1)}, bf16[256,512]{1,0:T(8,128)(2,1)S(1)}, u32[]{:S(2)}, u32[]{:S(2)}) collective-permute-start(bf16[256,512]{1,0:T(8,128)(2,1)S(1)} %get-tuple-element.22), channel_id=1, source_target_pairs={{0,6},{2,0},{4,2},{6,4},{1,7},{3,1},{5,3},{7,5},{8,14},{10,8},{12,... | collective-permute-start | bytes 786440 | tf_op jit(solution)/shard_map/ppermute | solution.py:380
  106.2 0.0 collective-permute-done.10.bottom_ref
  106.2 0.0 collective-permute-done.9.top_ref
  106.2 0.5 shard_map.79
  106.7 1.9 %collective-permute-start.11 = (bf16[256,512]{1,0:T(8,128)(2,1)S(1)}, bf16[256,512]{1,0:T(8,128)(2,1)S(1)}, u32[]{:S(2)}, u32[]{:S(2)}) collective-permute-start(bf16[256,512]{1,0:T(8,128)(2,1)S(1)} %get-tuple-element.20), channel_id=1, source_target_pairs={{0,2},{2,4},{4,6},{6,0},{1,3},{3,5},{5,7},{7,1},{8,10},{10,12},{12... | collective-permute-start | bytes 786440 | tf_op jit(solution)/shard_map/ppermute | solution.py:384
  108.6 4.6 %collective-permute-start.14 = (bf16[256,512]{1,0:T(8,128)(2,1)S(1)}, bf16[256,512]{1,0:T(8,128)(2,1)S(1)}, u32[]{:S(2)}, u32[]{:S(2)}) collective-permute-start(bf16[256,512]{1,0:T(8,128)(2,1)S(1)} %get-tuple-element.23), channel_id=1, source_target_pairs={{0,6},{2,0},{4,2},{6,4},{1,7},{3,1},{5,3},{7,5},{8,14},{10,8},{12,... | collective-permute-start | bytes 786440 | tf_op jit(solution)/shard_map/ppermute | solution.py:385
  113.2 0.5 shard_map.78.own_ref
  113.7 0.0 collective-permute-done.12.l1
  113.7 0.0 collective-permute-done.13.r0
  113.7 4.5 %collective-permute-done.11.l0 = bf16[256,512]{1,0:T(8,128)(2,1)S(1)} collective-permute-done((bf16[256,512]{1,0:T(8,128)(2,1)S(1)}, bf16[256,512]{1,0:T(8,128)(2,1)S(1)}, u32[]{:S(2)}, u32[]{:S(2)}) %collective-permute-start.11) | collective-permute-done | bytes 262176 | tf_op jit(solution)/shard_map/ppermute | solution.py:384
  118.2 0.8 collective-permute-done.14.r1
  119.0 0.2 shard_map.81
  119.2 0.0 copy-start.2
  119.2 33.5 %all_to_all.21 = bf16[64,8,512]{2,1,0:T(8,128)(2,1)S(1)} all-to-all(bf16[64,8,512]{2,1,0:T(8,128)(2,1)S(1)} %bitcast.27), channel_id=1, replica_groups=mesh['expert'=64,'x'=4,'c'=2] {'expert'}, dimensions={0} | all-to-all | bytes 1048576 | tf_op jit(solution)/shard_map/all_to_all | solution.py:398
  152.7 0.9 shard_map.82
  153.7 20.7 %all_to_all.22.parts_ref = bf16[8,48,512]{2,1,0:T(8,128)(2,1)S(1)} all-to-all(bf16[8,48,512]{2,1,0:T(8,128)(2,1)S(1)} %shard_map.82), channel_id=1, replica_groups=mesh['expert'=64,'x'=4,'c'=2] {'x','c'}, dimensions={0} | all-to-all | bytes 786432 | tf_op jit(solution)/shard_map/all_to_all | solution.py:407
  174.3 0.0 copy-done.2
  174.3 0.7 shard_map.83
Async XLA Ops:
  0.0 37.9 %copy-start.1 = (bf16[1,2048,256]{2,1,0:T(8,128)(2,1)S(1)}, bf16[1,2048,256]{2,1,0:T(8,128)(2,1)}, u32[]{:S(2)}) copy-start(bf16[1,2048,256]{2,1,0:T(8,128)(2,1)} %param.10) | copy-start | bytes 3145732
  0.0 43.0 %copy-start = (bf16[1,256,2048]{2,1,0:T(8,128)(2,1)S(1)}, bf16[1,256,2048]{2,1,0:T(8,128)(2,1)}, u32[]{:S(2)}) copy-start(bf16[1,256,2048]{2,1,0:T(8,128)(2,1)} %param.12) | copy-start | bytes 3145732
  23.6 43.3 %all-to-all-start.1 = ((bf16[64,8,512]{2,1,0:T(8,128)(2,1)}), bf16[64,8,512]{2,1,0:T(8,128)(2,1)}, u32[]{:S(2)}, u32[]{:S(2)}) async-start(bf16[64,8,512]{2,1,0:T(8,128)(2,1)} %bitcast.6), calls=%async_computation.1 | async-start | bytes 1048576 | tf_op jit(solution)/shard_map/all_to_all | solution.py:327
  37.9 35.4 %collective-permute-start.4 = (bf16[2048,256]{1,0:T(8,128)(2,1)S(1)}, bf16[2048,256]{1,0:T(8,128)(2,1)}, u32[]{:S(2)}, u32[]{:S(2)}) collective-permute-start(bf16[2048,256]{1,0:T(8,128)(2,1)S(1)} %bitcast.23), channel_id=1, source_target_pairs={{0,1},{1,0},{2,3},{3,2},{4,5},{5,4},{6,7},{7,6},{8,9},{9,8},{10,11... | collective-permute-start | bytes 3145736 | tf_op jit(solution)/shard_map/ppermute | solution.py:293
  41.1 34.3 %collective-permute-start.5 = (bf16[2048,256]{1,0:T(8,128)(2,1)}, bf16[2048,256]{1,0:T(8,128)(2,1)}, u32[]{:S(2)}, u32[]{:S(2)}) collective-permute-start(bf16[2048,256]{1,0:T(8,128)(2,1)} %bitcast.11.u0), channel_id=1, source_target_pairs={{0,1},{1,0},{2,3},{3,2},{4,5},{5,4},{6,7},{7,6},{8,9},{9,8},{10,11... | collective-permute-start | bytes 3145736 | tf_op jit(solution)/shard_map/ppermute | solution.py:293
  43.1 46.1 %collective-permute-start.7 = (bf16[256,2048]{1,0:T(8,128)(2,1)S(1)}, bf16[256,2048]{1,0:T(8,128)(2,1)S(1)}, u32[]{:S(2)}, u32[]{:S(2)}) collective-permute-start(bf16[256,2048]{1,0:T(8,128)(2,1)S(1)} %bitcast.17), channel_id=1, source_target_pairs={{0,1},{1,0},{2,3},{3,2},{4,5},{5,4},{6,7},{7,6},{8,9},{9,8},{10,11... | collective-permute-start | bytes 3145736 | tf_op jit(solution)/shard_map/ppermute | solution.py:293
  67.9 11.8 %collective-permute-start.3 = (bf16[256,512]{1,0:T(8,128)(2,1)S(1)}, bf16[256,512]{1,0:T(8,128)(2,1)S(1)}, u32[]{:S(2)}, u32[]{:S(2)}) collective-permute-start(bf16[256,512]{1,0:T(8,128)(2,1)S(1)} %get-tuple-element.25), channel_id=1, source_target_pairs={{0,6},{2,0},{4,2},{6,4},{1,7},{3,1},{5,3},{7,5},{8,14},{10,8},{12,... | collective-permute-start | bytes 786440 | tf_op jit(solution)/shard_map/ppermute | solution.py:340
  70.7 11.8 %collective-permute-start = (bf16[256,512]{1,0:T(8,128)(2,1)S(1)}, bf16[256,512]{1,0:T(8,128)(2,1)S(1)}, u32[]{:S(2)}, u32[]{:S(2)}) collective-permute-start(bf16[256,512]{1,0:T(8,128)(2,1)S(1)} %get-tuple-element.26), channel_id=1, source_target_pairs={{0,2},{2,4},{4,6},{6,0},{1,3},{3,5},{5,7},{7,1},{8,10},{10,12},{12... | collective-permute-start | bytes 786440 | tf_op jit(solution)/shard_map/ppermute | solution.py:339
  73.2 11.8 %collective-permute-start.1 = (bf16[256,512]{1,0:T(8,128)(2,1)S(1)}, bf16[256,512]{1,0:T(8,128)(2,1)S(1)}, u32[]{:S(2)}, u32[]{:S(2)}) collective-permute-start(bf16[256,512]{1,0:T(8,128)(2,1)S(1)} %get-tuple-element.25), channel_id=1, source_target_pairs={{0,2},{2,4},{4,6},{6,0},{1,3},{3,5},{5,7},{7,1},{8,10},{10,12},{12... | collective-permute-start | bytes 786440 | tf_op jit(solution)/shard_map/ppermute | solution.py:341
  75.5 9.6 %collective-permute-start.2 = (bf16[256,512]{1,0:T(8,128)(2,1)S(1)}, bf16[256,512]{1,0:T(8,128)(2,1)S(1)}, u32[]{:S(2)}, u32[]{:S(2)}) collective-permute-start(bf16[256,512]{1,0:T(8,128)(2,1)S(1)} %get-tuple-element.26), channel_id=1, source_target_pairs={{0,6},{2,0},{4,2},{6,4},{1,7},{3,1},{5,3},{7,5},{8,14},{10,8},{12,... | collective-permute-start | bytes 786440 | tf_op jit(solution)/shard_map/ppermute | solution.py:342
  79.8 9.4 %collective-permute-start.8 = (bf16[256,512]{1,0:T(8,128)(2,1)S(1)}, bf16[256,512]{1,0:T(8,128)(2,1)S(1)}, u32[]{:S(2)}, u32[]{:S(2)}) collective-permute-start(bf16[256,512]{1,0:T(8,128)(2,1)S(1)} %collective-permute-done.3.r1), channel_id=1, source_target_pairs={{0,6},{2,0},{4,2},{6,4},{1,7},{3,1},{5,3},{7,5},{8,14},{10,8},{12,... | collective-permute-start | bytes 786440 | tf_op jit(solution)/shard_map/ppermute | solution.py:344
  82.6 12.7 %collective-permute-start.6 = (bf16[256,512]{1,0:T(8,128)(2,1)S(1)}, bf16[256,512]{1,0:T(8,128)(2,1)S(1)}, u32[]{:S(2)}, u32[]{:S(2)}) collective-permute-start(bf16[256,512]{1,0:T(8,128)(2,1)S(1)} %collective-permute-done.l0), channel_id=1, source_target_pairs={{0,2},{2,4},{4,6},{6,0},{1,3},{3,5},{5,7},{7,1},{8,10},{10,12},{12... | collective-permute-start | bytes 786440 | tf_op jit(solution)/shard_map/ppermute | solution.py:343
  91.2 15.0 %collective-permute-start.10 = (bf16[256,512]{1,0:T(8,128)(2,1)S(1)}, bf16[256,512]{1,0:T(8,128)(2,1)S(1)}, u32[]{:S(2)}, u32[]{:S(2)}) collective-permute-start(bf16[256,512]{1,0:T(8,128)(2,1)S(1)} %get-tuple-element.19), channel_id=1, source_target_pairs={{0,6},{2,0},{4,2},{6,4},{1,7},{3,1},{5,3},{7,5},{8,14},{10,8},{12,... | collective-permute-start | bytes 786440 | tf_op jit(solution)/shard_map/ppermute | solution.py:373
  97.3 8.9 %collective-permute-start.9 = (bf16[256,512]{1,0:T(8,128)(2,1)S(1)}, bf16[256,512]{1,0:T(8,128)(2,1)S(1)}, u32[]{:S(2)}, u32[]{:S(2)}) collective-permute-start(bf16[256,512]{1,0:T(8,128)(2,1)S(1)} %get-tuple-element.18), channel_id=1, source_target_pairs={{0,2},{2,4},{4,6},{6,0},{1,3},{3,5},{5,7},{7,1},{8,10},{10,12},{12... | collective-permute-start | bytes 786440 | tf_op jit(solution)/shard_map/ppermute | solution.py:374
  99.7 14.0 %collective-permute-start.12 = (bf16[256,512]{1,0:T(8,128)(2,1)S(1)}, bf16[256,512]{1,0:T(8,128)(2,1)S(1)}, u32[]{:S(2)}, u32[]{:S(2)}) collective-permute-start(bf16[256,512]{1,0:T(8,128)(2,1)S(1)} %get-tuple-element.21), channel_id=1, source_target_pairs={{0,2},{2,4},{4,6},{6,0},{1,3},{3,5},{5,7},{7,1},{8,10},{10,12},{12... | collective-permute-start | bytes 786440 | tf_op jit(solution)/shard_map/ppermute | solution.py:379
  101.6 12.1 %collective-permute-start.13 = (bf16[256,512]{1,0:T(8,128)(2,1)S(1)}, bf16[256,512]{1,0:T(8,128)(2,1)S(1)}, u32[]{:S(2)}, u32[]{:S(2)}) collective-permute-start(bf16[256,512]{1,0:T(8,128)(2,1)S(1)} %get-tuple-element.22), channel_id=1, source_target_pairs={{0,6},{2,0},{4,2},{6,4},{1,7},{3,1},{5,3},{7,5},{8,14},{10,8},{12,... | collective-permute-start | bytes 786440 | tf_op jit(solution)/shard_map/ppermute | solution.py:380
  106.7 11.5 %collective-permute-start.11 = (bf16[256,512]{1,0:T(8,128)(2,1)S(1)}, bf16[256,512]{1,0:T(8,128)(2,1)S(1)}, u32[]{:S(2)}, u32[]{:S(2)}) collective-permute-start(bf16[256,512]{1,0:T(8,128)(2,1)S(1)} %get-tuple-element.20), channel_id=1, source_target_pairs={{0,2},{2,4},{4,6},{6,0},{1,3},{3,5},{5,7},{7,1},{8,10},{10,12},{12... | collective-permute-start | bytes 786440 | tf_op jit(solution)/shard_map/ppermute | solution.py:384
  108.6 10.4 %collective-permute-start.14 = (bf16[256,512]{1,0:T(8,128)(2,1)S(1)}, bf16[256,512]{1,0:T(8,128)(2,1)S(1)}, u32[]{:S(2)}, u32[]{:S(2)}) collective-permute-start(bf16[256,512]{1,0:T(8,128)(2,1)S(1)} %get-tuple-element.23), channel_id=1, source_target_pairs={{0,6},{2,0},{4,2},{6,4},{1,7},{3,1},{5,3},{7,5},{8,14},{10,8},{12,... | collective-permute-start | bytes 786440 | tf_op jit(solution)/shard_map/ppermute | solution.py:385
  119.2 55.1 %copy-start.2 = (f32[1,3,2048]{2,0,1:T(1,128)S(1)}, f32[1,3,2048]{2,0,1:T(1,128)}, u32[]{:S(2)}) copy-start(f32[1,3,2048]{2,0,1:T(1,128)} %param.8) | copy-start | bytes 73732
